TPU v7x, 32 devices: a whole 2x2x4 slice. The times are simulated.
32 devices in a mesh: group: 2 (over x), expert: 16 (over z, y, core).
Axes of the slice: x: 2, y: 2, z: 4, core: 2. Of those that a mesh axis runs over, the one named last changes fastest.
Arguments:
- hidden_slots: bfloat16 [32, 512, 2048], P(('group', 'expert')), parts along dimension 0, may hold values from -6 to 6
- adapter_in: bfloat16 [16, 16, 2048], P('expert'), may hold values from -8 to 8
- adapter_out: bfloat16 [16, 16, 7168], P('expert'), may hold values from -8 to 8
- expert_ids: int32 [4096, 2], P(('group', 'expert')), parts along dimension 0, may hold values from 0 to 15, all different within a row; in each aligned block of 128 rows (0 to 127, 128 to 255, ...) at most 32 rows name the same one
- gate_weights: float32 [4096, 2], P(('group', 'expert')), parts along dimension 0, may hold values from 0.05 to 0.5
- cotangent: bfloat16 [4096, 7168], P(('group', 'expert')), parts along dimension 0, may hold values from -6 to 6
Outputs:
- adapter_delta: bfloat16 [4096, 7168], P(('group', 'expert')), parts along dimension 0
- scaled_in_grad: float32 [32, 16, 2048], P(('group', 'expert')), parts along dimension 0
- scaled_out_grad: float32 [32, 16, 7168], P(('group', 'expert')), parts along dimension 0
There are 2 independent parts, one for each index of `group`. A program takes and returns all parts, laid end to end along the dimension named above; an argument that names none is the same for every part. Nothing has to cross between parts.
Inputs may be any that keep to these rules, and one draw needn't show every extreme that they name: `expert_ids`: each row names 2 different experts. In each aligned block of 128 rows (the rows of one device) no expert is named by more than 32 rows, a bound that some block reaches.
All inputs are finite; a program needn't handle non-finite values.
Results may differ from a plain program's by a relative error of at most 0.0063.
Values may be sent and summed in bfloat16 or wider, within the bound.
No kernel may reach another device: no remote copies, remote signals or barrier semaphores. Data moves between devices by JAX's collectives and lax.ppermute only.
A program may use at most 128 MiB of HBM per device.

v0:
```python
import jax
import jax.numpy as jnp
from jax import lax
from jax.sharding import PartitionSpec as P

HIGHEST = lax.Precision.HIGHEST


def route_layout(expert_ids, gate_weights, experts, capacity):
    rows_here = expert_ids.shape[0]
    chosen = expert_ids[:, :, None] == jnp.arange(experts, dtype=jnp.int32)[None, None, :]
    per_token = jnp.sum(chosen, axis=1).astype(jnp.float32)
    earlier = (jnp.arange(rows_here)[:, None] > jnp.arange(rows_here)[None, :]).astype(jnp.float32)
    before = jnp.dot(earlier, per_token, precision=HIGHEST)
    position = jnp.sum(jnp.where(chosen, before[:, None, :], 0.0), axis=2).astype(jnp.int32)
    slot_index = expert_ids * capacity + position
    rounded_gate = gate_weights.astype(jnp.bfloat16)
    matches = (
        slot_index[None, :, :] == jnp.arange(experts * capacity, dtype=jnp.int32)[:, None, None]
    )
    picked = jnp.where(matches, rounded_gate[None, :, :], jnp.zeros((), jnp.bfloat16))
    return jnp.sum(picked.astype(jnp.float32), axis=2).astype(jnp.bfloat16)


def owner_stats(adapter_in, adapter_out):
    gram_in = jnp.dot(adapter_in[0], adapter_in[0].T, preferred_element_type=jnp.float32)
    gram_out = jnp.dot(adapter_out[0], adapter_out[0].T, preferred_element_type=jnp.float32)
    traces = lax.psum((jnp.trace(gram_in), jnp.trace(gram_out)), "expert")
    return (gram_in, gram_out, traces)


def send_cotangents(route_table, cotangent):
    grad_slots = jnp.dot(route_table, cotangent, preferred_element_type=jnp.float32).astype(
        jnp.bfloat16
    )
    return lax.all_to_all(grad_slots, "expert", split_axis=0, concat_axis=0, tiled=True)


def forward(hidden_rows, adapter_in, adapter_out, route_table, capacity):
    low_rank = lax.dot_general(
        hidden_rows, adapter_in[0], (((1,), (1,)), ((), ())), preferred_element_type=jnp.float32
    ).astype(jnp.bfloat16)
    width = adapter_out.shape[2]
    returned = lax.all_to_all(low_rank, "expert", split_axis=0, concat_axis=0, tiled=True)
    rank_dim = low_rank.shape[1]
    shards = lax.all_gather(adapter_out, "expert", axis=0, tiled=True)
    number = shards.shape[0]
    lows = returned.reshape(number, capacity, rank_dim)
    expert_out = jnp.einsum(
        "ecr,erd->ecd", lows, shards, preferred_element_type=jnp.float32
    ).astype(jnp.bfloat16)
    summed = lax.dot_general(
        route_table,
        expert_out.reshape(number * capacity, width),
        (((0,), (0,)), ((), ())),
        preferred_element_type=jnp.float32,
    )
    return (low_rank, summed.astype(jnp.bfloat16))


def on_device(hidden_slots, adapter_in, adapter_out, expert_ids, gate_weights, cotangent):
    experts = lax.axis_size("expert")
    capacity = hidden_slots.shape[1] // experts
    route_table = route_layout(expert_ids, gate_weights, experts, capacity)
    hidden_rows = hidden_slots[0]
    low_rank, adapter_delta = forward(hidden_rows, adapter_in, adapter_out, route_table, capacity)
    grad_rows = send_cotangents(route_table, cotangent)
    gram_in, gram_out, traces = owner_stats(adapter_in, adapter_out)
    grad_low = lax.dot_general(
        grad_rows, adapter_out[0], (((1,), (1,)), ((), ())), preferred_element_type=jnp.float32
    ).astype(jnp.bfloat16)
    out_grad = lax.dot_general(
        low_rank, grad_rows, (((0,), (0,)), ((), ())), preferred_element_type=jnp.float32
    )
    in_grad = lax.dot_general(
        grad_low, hidden_rows, (((0,), (0,)), ((), ())), preferred_element_type=jnp.float32
    )
    rank_dim = gram_in.shape[0]
    identity = jnp.eye(rank_dim, dtype=jnp.float32)
    damp_in = traces[0] / (rank_dim * experts)
    damp_out = traces[1] / (rank_dim * experts)
    factor_out = jnp.linalg.cholesky(gram_out + damp_out * identity)
    factor_in = jnp.linalg.cholesky(gram_in + damp_in * identity)
    scaled_in = jax.scipy.linalg.cho_solve((factor_out, True), in_grad)
    scaled_out = jax.scipy.linalg.cho_solve((factor_in, True), out_grad)
    return (adapter_delta, scaled_in[None], scaled_out[None])


def solution(mesh):
    return jax.shard_map(
        on_device,
        mesh=mesh,
        in_specs=(
            P(("group", "expert"), None, None),
            P("expert", None, None),
            P("expert", None, None),
            P(("group", "expert"), None),
            P(("group", "expert"), None),
            P(("group", "expert"), None),
        ),
        out_specs=(
            P(("group", "expert"), None),
            P(("group", "expert"), None, None),
            P(("group", "expert"), None, None),
        ),
        check_vma=False,
    )
```

profile of v0, /device:TPU:16, one launch (start us, length us, event | category | flops | bytes accessed | tf_op | source)
XLA Modules:
  0.0 269.8 jit_solution(3399556631646143656)
XLA Ops:
  7.2 1.6 copy-done
  8.8 1.5 fusion.4
  10.4 0.7 reshape.39
  11.1 6.2 %all-to-all-start = ((bf16[16,2,256]{2,1,0:T(2,128)(2,1)}), bf16[16,2,256]{2,1,0:T(2,128)(2,1)S(1)}, u32[]{:S(2)}, u32[]{:S(2)}) async-start(bf16[16,2,256]{2,1,0:T(2,128)(2,1)} %reshape.39), calls=%async_computation | async-start | bytes 32768 | tf_op jit(solution)/shard_map/all_to_all | solution.py:44
  17.3 0.7 convert_reduce_fusion
  18.1 0.8 select_reduce_fusion
  18.9 0.7 convert_add_fusion
  19.6 0.7 convert_element_type.34
  20.3 6.6 %convolution_convert_fusion = bf16[512,7168]{1,0:T(8,128)(2,1)} fusion(bf16[512,128]{1,0:T(8,128)(2,1)S(1)} %fusion.8, bf16[128,7168]{1,0:T(8,128)(2,1)} %param.12), kind=kOutput, calls=%fused_computation | convolution fusion | flops 943194112 | bytes 9306112 | tf_op jit(solution)/shard_map/dot_general | solution.py:33
  26.9 6.2 %all-to-all-start.1 = ((bf16[16,32,7168]{2,1,0:T(8,128)(2,1)}), bf16[16,32,7168]{2,1,0:T(8,128)(2,1)}, u32[]{:S(2)}, u32[]{:S(2)}) async-start(bf16[16,32,7168]{2,1,0:T(8,128)(2,1)} %bitcast.72), calls=%async_computation.1 | async-start | bytes 14680064 | tf_op jit(solution)/shard_map/all_to_all | solution.py:36
  33.1 0.7 all-gather.2.cloned.1.call-update
  33.8 0.8 fusion.33
  34.6 0.8 fusion.31
  35.4 198.5 %all-reduce = (f32[]{:T(128)}, f32[]{:T(128)}) all-reduce(f32[]{:T(128)} %get-tuple-element.6, f32[]{:T(128)} %get-tuple-element.8), channel_id=1, replica_groups=mesh['group'=2,'expert'=16] {'expert'}, use_global_device_ids=true, to_apply=%region_4.5 | all-reduce | flops 2 | bytes 16 | tf_op jit(solution)/shard_map/psum | solution.py:28
  234.7 1.5 cholesky.55
  237.5 1.2 custom-call.17
  239.6 1.5 cholesky.44
  242.4 1.2 custom-call.16
  243.7 4.1 %convolution_convert_fusion.1 = bf16[16,32,7168]{2,1,0:T(8,128)(2,1)S(1)} fusion(bf16[16,16,7168]{2,1,0:T(8,128)(2,1)} %all-gather.2.cloned.1.call-done, bf16[16,16,32]{2,1,0:T(8,128)(2,1)S(1)} %reshape.40), kind=kOutput, calls=%fused_computation.1 | convolution fusion | flops 121110528 | bytes 11026432 | tf_op jit(solution)/shard_map/ecr,erd->ecd/dot_general | solution.py:49
  247.9 2.4 convolution_convert_fusion.2
  250.3 4.1 %fusion.37 = f32[16,7168]{1,0:T(8,128)S(1)} fusion(bf16[512,16]{0,1:T(8,128)(2,1)S(1)} %fusion.4, bf16[512,7168]{1,0:T(8,128)(2,1)} %bitcast.8), kind=kOutput, calls=%fused_computation.57 | convolution fusion | flops 117440512 | bytes 7815168 | tf_op jit(solution)/shard_map/dot_general | solution.py:72
  254.5 5.4 %fusion = f32[16,2048]{1,0:T(8,128)S(1)} fusion(bf16[1,512,2048]{2,1,0:T(8,128)(2,1)S(1)} %copy-done, bf16[512,7168]{1,0:T(8,128)(2,1)} %bitcast.8, bf16[1,16,7168]{2,1,0:T(8,128)(2,1)S(1)} %copy-done.1), kind=kOutput, calls=%fused_computation.5 | convolution fusion | flops 151003136 | bytes 9797632 | tf_op jit(solution)/shard_map/dot_general | solution.py:75
  260.5 1.3 convolution_bitcast_fusion
  262.1 0.9 convolution_bitcast_fusion.1
  (30 shorter events, 4.4 us)
Async XLA Ops:
  7.2 1.6 copy-start
  11.1 15.8 %all-to-all-start = ((bf16[16,2,256]{2,1,0:T(2,128)(2,1)}), bf16[16,2,256]{2,1,0:T(2,128)(2,1)S(1)}, u32[]{:S(2)}, u32[]{:S(2)}) async-start(bf16[16,2,256]{2,1,0:T(2,128)(2,1)} %reshape.39), calls=%async_computation | async-start | bytes 32768 | tf_op jit(solution)/shard_map/all_to_all | solution.py:44
  26.9 6.9 %copy-start.2 = (bf16[1,16,2048]{2,1,0:T(8,128)(2,1)S(1)}, bf16[1,16,2048]{2,1,0:T(8,128)(2,1)}, u32[]{:S(2)}) copy-start(bf16[1,16,2048]{2,1,0:T(8,128)(2,1)} %param.8) | copy-start | bytes 196612
  26.9 7.7 %copy-start.1 = (bf16[1,16,7168]{2,1,0:T(8,128)(2,1)S(1)}, bf16[1,16,7168]{2,1,0:T(8,128)(2,1)}, u32[]{:S(2)}) copy-start(bf16[1,16,7168]{2,1,0:T(8,128)(2,1)} %param.9) | copy-start | bytes 688132
  26.9 223.4 %all-to-all-start.1 = ((bf16[16,32,7168]{2,1,0:T(8,128)(2,1)}), bf16[16,32,7168]{2,1,0:T(8,128)(2,1)}, u32[]{:S(2)}, u32[]{:S(2)}) async-start(bf16[16,32,7168]{2,1,0:T(8,128)(2,1)} %bitcast.72), calls=%async_computation.1 | async-start | bytes 14680064 | tf_op jit(solution)/shard_map/all_to_all | solution.py:36
  33.1 210.7 %all-gather.2.cloned.1.call-start = ((), (), s32[]{:S(2)}) async-start(), calls=%async_computation.2 | async-start | bytes 3899392 | tf_op jit(solution)/shard_map/all_gather | solution.py:46
Sparse Core Ops, SparseCore 0:
  36.2 130.3 all-gather.1
where the time goes:
time: 270 us
  blocking collectives  199 us (74%)
  matrix products  29 us (11%)
  between operations  15.5 us (6%)
  starting transfers between devices  12.4 us (5%)
  other arithmetic  10.9 us (4%)
  local copies, waits for them, and re-layouts  2.85 us (1%)
    psum x1, blocking collectives, owner_stats(): traces = lax.psum((jnp.trace(gram_in), jnp.trace(gram_out)), 'expert')  199 us
    dot_general x1, matrix products, send_cotangents(): jnp.dot(route_table, cotangent, preferred_element_type=jnp.float32)  6.59 us
    all_to_all x1, starting transfers between devices, forward(): lax.all_to_all(low_rank, 'expert', split_axis=0, concat_axis=0, tiled=True)  6.18 us
    all_to_all x1, starting transfers between devices, send_cotangents(): lax.all_to_all(grad_slots, 'expert', split_axis=0, concat_axis=0, tiled=T...  6.16 us
    dot_general x1, matrix products, on_device(): lax.dot_general(grad_low, hidden_rows, (((0,), (0,)), ((), ())), preferre...  5.44 us
  transfers between devices with their start and end apart: 3, of which 0 were waited for; matrix products, arithmetic and copies ran while one was open for 10% of the time, Pallas kernels for 0%

commit v1 on v0

v1 whole, which is shorter than its diff:
```python
import functools

import jax
import jax.numpy as jnp
from jax import lax
from jax.experimental import pallas as pl
from jax.experimental.pallas import tpu as pltpu
from jax.sharding import Mesh, PartitionSpec as P

PLANE = 4
BF = jnp.bfloat16
F32 = jnp.float32
HIGHEST = lax.Precision.HIGHEST
PARAMS = pltpu.CompilerParams(vmem_limit_bytes=48 * 1024 * 1024)


def mm(a, b, ca=1, cb=0, precision=None):
    return lax.dot_general(
        a, b, (((ca,), (cb,)), ((), ())), preferred_element_type=F32, precision=precision
    )


def call(kernel, outs, args, flops=0):
    size = sum(x.size * x.dtype.itemsize for x in args)
    size += sum(o.size * o.dtype.itemsize for o in outs)
    return pl.pallas_call(
        kernel,
        out_shape=outs,
        compiler_params=PARAMS,
        cost_estimate=pl.CostEstimate(flops=flops, bytes_accessed=size, transcendentals=0),
    )(*args)


def split(x):
    high = x.astype(BF)
    return high, (x - high.astype(F32)).astype(BF)


def split_factor_kernel(a_out, out):
    width = out.shape[2]
    for q in range(PLANE):
        out[q] = a_out[:, q * width : (q + 1) * width]


def pack_tokens_kernel(cot, ids, gates, out):
    tokens, width = cot.shape[0], out.shape[2]
    for q in range(PLANE):
        out[q, 0:tokens, :] = cot[:, q * width : (q + 1) * width]
    diagonal = (
        lax.broadcasted_iota(jnp.int32, (tokens, tokens), 0)
        == lax.broadcasted_iota(jnp.int32, (tokens, tokens), 1)
    ).astype(BF)
    id_rows = mm(ids[...].astype(F32).astype(BF), diagonal, 0, 0)
    gate_rows = mm(gates[...].astype(BF), diagonal, 0, 0)
    row = lax.broadcasted_iota(jnp.int32, (16, tokens), 0)
    meta = jnp.where(row == 0, id_rows[0:1], 0.0)
    meta = jnp.where(row == 1, id_rows[1:2], meta)
    meta = jnp.where(row == 2, gate_rows[0:1], meta)
    meta = jnp.where(row == 3, gate_rows[1:2], meta).astype(BF)
    for q in range(PLANE):
        out[q, tokens : tokens + 16, 0:tokens] = meta
        out[q, tokens : tokens + 16, tokens:] = jnp.zeros((16, width - tokens), BF)


def low_rank_kernel(hidden, a_in, a_out, out):
    slots = out.shape[2]
    low = mm(a_in[...], hidden[...], 1, 1).astype(BF)
    wide_in, wide_out = a_in[...].astype(F32), a_out[...].astype(F32)
    total_in = jnp.sum(jnp.sum(wide_in * wide_in, axis=1, keepdims=True), axis=0, keepdims=True)
    total_out = jnp.sum(jnp.sum(wide_out * wide_out, axis=1, keepdims=True), axis=0, keepdims=True)
    row = lax.broadcasted_iota(jnp.int32, (16, slots), 0)
    stats = jnp.zeros((16, slots), F32)
    for base, total in ((0, total_in), (3, total_out)):
        rest = jnp.broadcast_to(total, (16, slots))
        for piece in range(3):
            part = rest.astype(BF).astype(F32)
            stats = jnp.where(row == base + piece, part, stats)
            rest = rest - part
    stats = stats.astype(BF)
    for device in range(out.shape[0]):
        plane = device // PLANE
        out[device, 0:16, :] = low[:, plane * slots : (plane + 1) * slots]
        out[device, 16:32, :] = stats


def fold_of(slots, experts, capacity, source):
    column = lax.broadcasted_iota(jnp.int32, (slots, experts * capacity), 1)
    row = lax.broadcasted_iota(jnp.int32, (slots, experts * capacity), 0)
    return (row == source * capacity + lax.rem(column, capacity)).astype(BF)


def own_expert(experts, capacity, rank):
    shape = (experts * rank, experts * capacity)
    row = lax.div(lax.broadcasted_iota(jnp.int32, shape, 0), rank)
    column = lax.div(lax.broadcasted_iota(jnp.int32, shape, 1), capacity)
    return row == column


def weighted_rows_kernel(packed, lows, z_out, w_out, part_out):
    experts, slots = lows.shape[0], lows.shape[2]
    rank, capacity = 16, slots // PLANE
    tokens = packed.shape[1] - 16
    low = lows[:, 0:rank, :].reshape(experts * rank, slots)
    own = own_expert(experts, capacity, rank)
    expert = lax.broadcasted_iota(jnp.int32, (experts, tokens), 0).astype(F32)
    earlier = (
        lax.broadcasted_iota(jnp.int32, (tokens, tokens), 0)
        < lax.broadcasted_iota(jnp.int32, (tokens, tokens), 1)
    ).astype(BF)
    place = lax.broadcasted_iota(jnp.int32, (experts, capacity, tokens), 1).astype(F32)
    part = jnp.zeros(part_out.shape, F32)
    for s in range(PLANE):
        meta = packed[s, tokens : tokens + 16, 0:tokens].astype(F32)
        first = (meta[0:1] == expert).astype(F32)
        second = (meta[1:2] == expert).astype(F32)
        before = mm((first + second).astype(BF), earlier)
        gate = first * meta[2:3] + second * meta[3:4]
        spread = jnp.where(before[:, None, :] == place, gate[:, None, :], 0.0)
        weights = spread.reshape(experts * capacity, tokens).astype(BF)
        wide = mm(low, fold_of(slots, experts, capacity, s))
        wide = jnp.where(own, wide, 0.0).astype(BF)
        z = mm(wide, weights).astype(BF)
        z_out[:, s * tokens : (s + 1) * tokens] = z
        w_out[s] = weights
        part = part + mm(z, packed[s, 0:tokens, :])
    part_out[...] = part.astype(BF)


def grad_low_kernel(packed, factor, w, out):
    experts = factor.shape[0] // 16
    slots, tokens = out.shape[1], w.shape[2]
    capacity = slots // PLANE
    own = own_expert(experts, capacity, 16)
    total = jnp.zeros(out.shape, F32)
    for s in range(PLANE):
        coords = mm(factor[...], packed[s, 0:tokens, :], 1, 1)
        high, low = split(coords)
        picked = mm(high, w[s], 1, 1) + mm(low, w[s], 1, 1)
        picked = jnp.where(own, picked, 0.0)
        high, low = split(picked)
        fold = fold_of(slots, experts, capacity, s)
        total = total + mm(high, fold, 1, 1) + mm(low, fold, 1, 1)
    out[...] = total


def delta_kernel(z, factor, out):
    tokens = out.shape[1]
    for s in range(PLANE):
        rows = mm(z[:, s * tokens : (s + 1) * tokens], factor[...], 0, 0)
        out[s] = rows.astype(BF)


def inverse_kernel(a_in, a_out, lows, inv_in, inv_out):
    experts = lows.shape[0]
    stats = jnp.sum(lows[:, 16:32, :].astype(F32), axis=0)
    row = lax.broadcasted_iota(jnp.int32, (16, 16), 0)
    column = lax.broadcasted_iota(jnp.int32, (16, 16), 1)
    eye = (row == column).astype(F32)
    works = []
    for base, factor in ((0, a_in), (3, a_out)):
        pieces = stats[base : base + 1, 0:1] + stats[base + 1 : base + 2, 0:1]
        damp = (pieces + stats[base + 2 : base + 3, 0:1]) / (16.0 * experts)
        gram = mm(factor[...], factor[...], 1, 1) + damp * eye
        works.append([gram, eye])
    for j in range(16):
        for work in works:
            gram, inverse = work
            pivot = 1.0 / gram[j : j + 1, j : j + 1]
            gram_row, inverse_row = gram[j : j + 1] * pivot, inverse[j : j + 1] * pivot
            scale = gram[:, j : j + 1]
            work[0] = jnp.where(row == j, gram_row, gram - scale * gram_row)
            work[1] = jnp.where(row == j, inverse_row, inverse - scale * inverse_row)
    inv_in[...] = works[0][1]
    inv_out[...] = works[1][1]


def scaled_in_kernel(coords, hidden, inverse, out):
    planes = coords.shape[0] // PLANE
    pieces = []
    for z in range(planes):
        total = coords[PLANE * z]
        for q in range(1, PLANE):
            total = total + coords[PLANE * z + q]
        pieces.append(total)
    grad_low = jnp.concatenate(pieces, axis=1).astype(BF)
    out[...] = mm(inverse[...], mm(grad_low, hidden[...]), precision=HIGHEST)


def scaled_out_kernel(rows, inverse, out):
    width = rows.shape[2]
    for q in range(PLANE):
        out[:, q * width : (q + 1) * width] = mm(inverse[...], rows[q], precision=HIGHEST)


def on_device(hidden_slots, adapter_in, adapter_out, expert_ids, gate_weights, cotangent):
    planes = lax.axis_size("z")
    experts = planes * PLANE
    hidden, a_in, a_out = hidden_slots[0], adapter_in[0], adapter_out[0]
    rank, width = a_out.shape
    quarter = width // PLANE
    tokens = cotangent.shape[0]
    slots = hidden.shape[0] // planes
    capacity = slots // PLANE
    struct = jax.ShapeDtypeStruct
    plane, every = ("y", "core"), ("z", "y", "core")
    exchange = functools.partial(lax.all_to_all, split_axis=0, concat_axis=0, tiled=True)

    (own_factor,) = call(split_factor_kernel, [struct((PLANE, rank, quarter), BF)], [a_out])
    plane_factor = exchange(own_factor, plane).reshape(PLANE * rank, quarter)
    factor = lax.all_gather(plane_factor, "z", axis=0, tiled=True)

    (packed,) = call(
        pack_tokens_kernel,
        [struct((PLANE, tokens + 16, quarter), BF)],
        [cotangent, expert_ids, gate_weights],
    )
    packed = exchange(packed, plane)

    (lows,) = call(
        low_rank_kernel, [struct((experts, 2 * rank, slots), BF)], [hidden, a_in, a_out]
    )
    lows = exchange(lows, every)

    inv_in, inv_out = call(
        inverse_kernel, [struct((rank, rank), F32)] * 2, [a_in, a_out, lows]
    )
    z, weights, part = call(
        weighted_rows_kernel,
        [
            struct((experts * rank, PLANE * tokens), BF),
            struct((PLANE, experts * capacity, tokens), BF),
            struct((experts * rank, quarter), BF),
        ],
        [packed, lows],
    )
    part = exchange(part.reshape(planes, PLANE * rank, quarter), "z")
    rows = jnp.sum(part.astype(F32), axis=0).reshape(PLANE, rank, quarter)
    rows = exchange(rows, plane)
    (scaled_out,) = call(scaled_out_kernel, [struct((rank, width), F32)], [rows, inv_in])

    (coords,) = call(
        grad_low_kernel, [struct((experts * rank, slots), F32)], [packed, factor, weights]
    )
    coords = exchange(coords.reshape(experts, rank, slots), every)
    (scaled_in,) = call(
        scaled_in_kernel, [struct((rank, hidden.shape[1]), F32)], [coords, hidden, inv_out]
    )

    (delta,) = call(delta_kernel, [struct((PLANE, tokens, quarter), BF)], [z, factor])
    delta = exchange(delta, plane)
    delta = jnp.swapaxes(delta, 0, 1).reshape(tokens, width)
    return delta, scaled_in[None], scaled_out[None]


def solution(mesh):
    groups, experts = mesh.shape["group"], mesh.shape["expert"]
    fine = Mesh(
        mesh.devices.reshape(groups, experts // PLANE, PLANE // 2, 2),
        ("group", "z", "y", "core"),
    )
    every = ("z", "y", "core")
    return jax.shard_map(
        on_device,
        mesh=fine,
        in_specs=(
            P(("group", *every), None, None),
            P(every, None, None),
            P(every, None, None),
            P(("group", *every), None),
            P(("group", *every), None),
            P(("group", *every), None),
        ),
        out_specs=(
            P(("group", *every), None),
            P(("group", *every), None, None),
            P(("group", *every), None, None),
        ),
        check_vma=False,
    )
```

time: 270 us -> 141 us (0.52)
  the two profiles are of different devices: /device:TPU:16 before, /device:TPU:0 now
where the time goes in v1:
time: 141 us; the launch traced here: 140 us
  waiting for transfers between devices  54 us (38%)
  blocking collectives  30.4 us (22%)
  starting transfers between devices  25.2 us (18%)
  local copies, waits for them, and re-layouts  14.2 us (10%)
  Pallas kernels  13.5 us (10%)
  other arithmetic  2.26 us (2%)
    all_to_all x1, waiting for transfers between devices, on_device(): part = exchange(part.reshape(planes, PLANE * rank, quarter), 'z')  20.8 us
    all_to_all x1, waiting for transfers between devices, on_device(): delta = exchange(delta, plane)  20.7 us
    all_gather x1, blocking collectives, on_device(): factor = lax.all_gather(plane_factor, 'z', axis=0, tiled=True)  19.9 us
    pallas_call x9, Pallas kernels, call(): pl.pallas_call(kernel, out_shape=outs, compiler_params=PARAMS, cost_estim...  13.5 us
    unnamed x33, local copies, waits for them, and re-layouts  11.3 us
    all_to_all x1, blocking collectives, on_device(): coords = exchange(coords.reshape(experts, rank, slots), every)  10.5 us
    all_to_all x1, waiting for transfers between devices, on_device(): lows = exchange(lows, every)  6.18 us
    all_to_all x1, starting transfers between devices, on_device(): lows = exchange(lows, every)  6.02 us
  transfers between devices with their start and end apart: 6, of which 5 were waited for; matrix products, arithmetic and copies ran while one was open for 6% of the time, Pallas kernels for 4%

profile of v1, /device:TPU:0, one launch (start us, length us, event | category | flops | bytes accessed | tf_op | source)
XLA Modules:
  0.0 140.5 jit_solution(12380030485747696323)
XLA Ops:
  2.3 4.2 %all-to-all-start.2 = ((bf16[4,16,1792]{2,1,0:T(8,128)(2,1)}), bf16[4,16,1792]{2,1,0:T(8,128)(2,1)S(1)}, u32[]{:S(2)}, u32[]{:S(2)}) async-start(bf16[4,16,1792]{2,1,0:T(8,128)(2,1)} %shard_map.88), calls=%async_computation.2 | async-start | bytes 458752 | tf_op jit(solution)/shard_map/all_to_all | solution.py:209
  6.5 1.6 %copy-done = bf16[1,512,2048]{2,1,0:T(8,128)(2,1)S(1)} copy-done((bf16[1,512,2048]{2,1,0:T(8,128)(2,1)S(1)}, bf16[1,512,2048]{2,1,0:T(8,128)(2,1)}, u32[]{:S(2)}) %copy-start) | copy-done | bytes 2097176
  9.9 1.3 shard_map.86
  12.9 6.0 %all-to-all-start.1 = ((bf16[16,32,128]{2,1,0:T(8,128)(2,1)}), bf16[16,32,128]{2,1,0:T(8,128)(2,1)S(1)}, u32[]{:S(2)}, u32[]{:S(2)}) async-start(bf16[16,32,128]{2,1,0:T(8,128)(2,1)} %shard_map.86), calls=%async_computation.1 | async-start | bytes 262144 | tf_op jit(solution)/shard_map/all_to_all | solution.py:222
  19.3 1.3 copy-done.2
  20.7 6.2 %all-to-all-done.1.lows = bf16[16,32,128]{2,1,0:T(8,128)(2,1)S(1)} async-done(((bf16[16,32,128]{2,1,0:T(8,128)(2,1)}), bf16[16,32,128]{2,1,0:T(8,128)(2,1)S(1)}, u32[]{:S(2)}, u32[]{:S(2)}) %all-to-all-start.1) | async-done | bytes 131104 | tf_op jit(solution)/shard_map/all_to_all | solution.py:222
  26.9 3.6 %all-to-all-start = ((bf16[4,144,1792]{2,1,0:T(8,128)(2,1)}), bf16[4,144,1792]{2,1,0:T(8,128)(2,1)S(1)}, u32[]{:S(2)}, u32[]{:S(2)}) async-start(bf16[4,144,1792]{2,1,0:T(8,128)(2,1)} %copy-done.2), calls=%async_computation | async-start | bytes 4128768 | tf_op jit(solution)/shard_map/all_to_all | solution.py:217
  30.5 19.9 %all_gather.3.factor = bf16[256,1792]{1,0:T(8,128)(2,1)S(1)} all-gather(bf16[64,1792]{1,0:T(8,128)(2,1)S(1)} %bitcast.22), channel_id=1, replica_groups=mesh['group'=2,'z'=4,'y'=2,'core'=2] {'z'}, dimensions={0}, use_global_device_ids=true | all-gather | bytes 1146880 | tf_op jit(solution)/shard_map/all_gather | solution.py:210
  50.4 5.4 %all-to-all-done.packed = bf16[4,144,1792]{2,1,0:T(8,128)(2,1)S(1)} async-done(((bf16[4,144,1792]{2,1,0:T(8,128)(2,1)}), bf16[4,144,1792]{2,1,0:T(8,128)(2,1)S(1)}, u32[]{:S(2)}, u32[]{:S(2)}) %all-to-all-start) | async-done | bytes 2064416 | tf_op jit(solution)/shard_map/all_to_all | solution.py:217
  55.8 2.2 %shard_map.87 = (bf16[256,512]{1,0:T(8,128)(2,1)S(1)}, bf16[4,512,128]{2,1,0:T(8,128)(2,1)S(1)}, bf16[256,1792]{1,0:T(8,128)(2,1)S(1)}) custom-call(bf16[4,144,1792]{2,1,0:T(8,128)(2,1)S(1)} %all-to-all-done.packed, bf16[16,32,128]{2,1,0:T(8,128)(2,1)S(1)} %all-to-all-done.1.lows), custom_call_target="tpu_custom_call" | custom-call | bytes 3899392 | tf_op jit(solution)/shard_map/pallas_call | solution.py:26
  58.9 3.0 %shard_map.90 = f32[256,128]{1,0:T(8,128)S(1)} custom-call(bf16[4,144,1792]{2,1,0:T(8,128)(2,1)S(1)} %all-to-all-done.packed, bf16[256,1792]{1,0:T(8,128)(2,1)S(1)} %all_gather.3.factor, bf16[4,512,128]{2,1,0:T(8,128)(2,1)S(1)} %get-tuple-element.9.w), custom_call_target="tpu_custom_call" | custom-call | bytes 3637248 | tf_op jit(solution)/shard_map/pallas_call | solution.py:26
  61.9 10.5 %all_to_all.35.coords = f32[16,16,128]{2,1,0:T(8,128)S(1)} all-to-all(f32[16,16,128]{2,1,0:T(8,128)S(1)} %bitcast.17), channel_id=1, replica_groups=mesh['group'=2,'z'=4,'y'=2,'core'=2] {'z','y','core'}, dimensions={0} | all-to-all | bytes 262144 | tf_op jit(solution)/shard_map/all_to_all | solution.py:244
  72.5 3.5 %all-to-all-start.5 = ((bf16[4,64,1792]{2,1,0:T(8,128)(2,1)}), bf16[4,64,1792]{2,1,0:T(8,128)(2,1)S(1)}, u32[]{:S(2)}, u32[]{:S(2)}) async-start(bf16[4,64,1792]{2,1,0:T(8,128)(2,1)} %bitcast.16), calls=%async_computation.5 | async-start | bytes 1835008 | tf_op jit(solution)/shard_map/all_to_all | solution.py:236
  76.0 1.9 %shard_map.89 = bf16[4,128,1792]{2,1,0:T(8,128)(2,1)} custom-call(bf16[256,512]{1,0:T(8,128)(2,1)S(1)} %get-tuple-element.8.z, bf16[256,1792]{1,0:T(8,128)(2,1)S(1)} %all_gather.3.factor), custom_call_target="tpu_custom_call" | custom-call | bytes 3014656 | tf_op jit(solution)/shard_map/pallas_call | solution.py:26
  77.9 20.8 %all-to-all-done.5 = bf16[4,64,1792]{2,1,0:T(8,128)(2,1)S(1)} async-done(((bf16[4,64,1792]{2,1,0:T(8,128)(2,1)}), bf16[4,64,1792]{2,1,0:T(8,128)(2,1)S(1)}, u32[]{:S(2)}, u32[]{:S(2)}) %all-to-all-start.5) | async-done | bytes 917536 | tf_op jit(solution)/shard_map/all_to_all | solution.py:236
  99.6 4.4 %all-to-all-start.3 = ((bf16[4,128,1792]{2,1,0:T(8,128)(2,1)}), bf16[4,128,1792]{2,1,0:T(8,128)(2,1)}, u32[]{:S(2)}, u32[]{:S(2)}) async-start(bf16[4,128,1792]{2,1,0:T(8,128)(2,1)} %shard_map.89), calls=%async_computation.3 | async-start | bytes 3670016 | tf_op jit(solution)/shard_map/all_to_all | solution.py:250
  104.0 2.3 %convert_reduce_fusion = f32[64,1792]{1,0:T(8,128)} fusion(bf16[4,64,1792]{2,1,0:T(8,128)(2,1)} %copy-done.10), kind=kLoop, calls=%fused_computation | loop fusion | flops 802816 | bytes 1376256 | tf_op jit(solution)/shard_map/reduce_sum | solution.py:237
  106.3 20.7 %all-to-all-done.3 = bf16[4,128,1792]{2,1,0:T(8,128)(2,1)} async-done(((bf16[4,128,1792]{2,1,0:T(8,128)(2,1)}), bf16[4,128,1792]{2,1,0:T(8,128)(2,1)}, u32[]{:S(2)}, u32[]{:S(2)}) %all-to-all-start.3) | async-done | bytes 1835040 | tf_op jit(solution)/shard_map/all_to_all | solution.py:250
  127.0 3.5 %all-to-all-start.6 = ((f32[4,16,1792]{2,1,0:T(8,128)}), f32[4,16,1792]{2,1,0:T(8,128)S(1)}, u32[]{:S(2)}, u32[]{:S(2)}) async-start(f32[4,16,1792]{2,1,0:T(8,128)} %bitcast.21), calls=%async_computation.6 | async-start | bytes 917504 | tf_op jit(solution)/shard_map/all_to_all | solution.py:238
  130.5 1.6 %shard_map.91 = (f32[16,16]{1,0:T(8,128)S(1)}, f32[16,16]{1,0:T(8,128)S(1)}) custom-call(bf16[16,2048]{1,0:T(8,128)(2,1)S(1)} %bitcast.19, bf16[16,7168]{1,0:T(8,128)(2,1)S(1)} %bitcast.15, bf16[16,32,128]{2,1,0:T(8,128)(2,1)S(1)} %all-to-all-done.1.lows), custom_call_target="tpu_custom_call" | custom-call | bytes 428032 | tf_op jit(solution)/shard_map/pallas_call | solution.py:26
  132.0 1.3 shard_map.92
  133.3 2.9 %copy.13 = bf16[128,4,1792]{0,2,1:T(8,128)(2,1)S(1)} copy(bf16[128,4,1792]{2,0,1:T(8,128)(2,1)} %bitcast.4) | data formatting | bytes 3670016 | tf_op jit(solution)/shard_map/transpose | solution.py:251
  136.2 2.9 %copy.14 = bf16[128,7168]{1,0:T(8,128)(2,1)} copy(bf16[128,7168]{0,1:T(8,128)(2,1)S(1)} %bitcast.20) | data formatting | bytes 3670016
  139.1 1.4 shard_map.93
  (34 shorter events, 7.4 us)
Async XLA Ops:
  0.6 0.9 copy-start.3
  1.6 17.3 %copy-start.13 = (s32[128,2]{0,1:T(2,128)S(1)}, s32[128,2]{0,1:T(2,128)}, u32[]{:S(2)}) copy-start(s32[128,2]{0,1:T(2,128)} %param.9) | copy-start | bytes 3076
  1.6 17.5 %copy-start.14 = (f32[128,2]{0,1:T(2,128)S(1)}, f32[128,2]{0,1:T(2,128)}, u32[]{:S(2)}) copy-start(f32[128,2]{0,1:T(2,128)} %param.10) | copy-start | bytes 3076
  2.3 9.9 %all-to-all-start.2 = ((bf16[4,16,1792]{2,1,0:T(8,128)(2,1)}), bf16[4,16,1792]{2,1,0:T(8,128)(2,1)S(1)}, u32[]{:S(2)}, u32[]{:S(2)}) async-start(bf16[4,16,1792]{2,1,0:T(8,128)(2,1)} %shard_map.88), calls=%async_computation.2 | async-start | bytes 458752 | tf_op jit(solution)/shard_map/all_to_all | solution.py:209
  6.5 1.6 %copy-start = (bf16[1,512,2048]{2,1,0:T(8,128)(2,1)S(1)}, bf16[1,512,2048]{2,1,0:T(8,128)(2,1)}, u32[]{:S(2)}) copy-start(bf16[1,512,2048]{2,1,0:T(8,128)(2,1)} %param.6) | copy-start | bytes 6291460
  8.1 0.9 copy-start.4
  9.0 0.8 copy-start.8
  9.9 9.3 %copy-start.6 = (bf16[128,7168]{1,0:T(8,128)(2,1)S(1)}, bf16[128,7168]{1,0:T(8,128)(2,1)}, u32[]{:S(2)}) copy-start(bf16[128,7168]{1,0:T(8,128)(2,1)} %cot.1) | copy-start | bytes 5505028
  12.2 0.7 copy-start.11
  12.9 14.0 %all-to-all-start.1 = ((bf16[16,32,128]{2,1,0:T(8,128)(2,1)}), bf16[16,32,128]{2,1,0:T(8,128)(2,1)S(1)}, u32[]{:S(2)}, u32[]{:S(2)}) async-start(bf16[16,32,128]{2,1,0:T(8,128)(2,1)} %shard_map.86), calls=%async_computation.1 | async-start | bytes 262144 | tf_op jit(solution)/shard_map/all_to_all | solution.py:222
  19.3 1.3 copy-start.2
  20.7 9.8 %copy-start.12 = (bf16[4,16,1792]{2,1,0:T(8,128)(2,1)S(1)}, bf16[4,16,1792]{2,1,0:T(8,128)(2,1)}, u32[]{:S(2)}) copy-start(bf16[4,16,1792]{2,1,0:T(8,128)(2,1)} %copy-done.11) | copy-start | bytes 688132
  26.9 28.9 %all-to-all-start = ((bf16[4,144,1792]{2,1,0:T(8,128)(2,1)}), bf16[4,144,1792]{2,1,0:T(8,128)(2,1)S(1)}, u32[]{:S(2)}, u32[]{:S(2)}) async-start(bf16[4,144,1792]{2,1,0:T(8,128)(2,1)} %copy-done.2), calls=%async_computation | async-start | bytes 4128768 | tf_op jit(solution)/shard_map/all_to_all | solution.py:217
  58.0 0.9 copy-start.7
  72.5 26.2 %all-to-all-start.5 = ((bf16[4,64,1792]{2,1,0:T(8,128)(2,1)}), bf16[4,64,1792]{2,1,0:T(8,128)(2,1)S(1)}, u32[]{:S(2)}, u32[]{:S(2)}) async-start(bf16[4,64,1792]{2,1,0:T(8,128)(2,1)} %bitcast.16), calls=%async_computation.5 | async-start | bytes 1835008 | tf_op jit(solution)/shard_map/all_to_all | solution.py:236
  98.6 1.0 copy-start.10
  98.6 31.8 %copy-start.5 = (bf16[1,16,7168]{2,1,0:T(8,128)(2,1)S(1)}, bf16[1,16,7168]{2,1,0:T(8,128)(2,1)}, u32[]{:S(2)}) copy-start(bf16[1,16,7168]{2,1,0:T(8,128)(2,1)} %param.8) | copy-start | bytes 688132
  99.6 27.4 %all-to-all-start.3 = ((bf16[4,128,1792]{2,1,0:T(8,128)(2,1)}), bf16[4,128,1792]{2,1,0:T(8,128)(2,1)}, u32[]{:S(2)}, u32[]{:S(2)}) async-start(bf16[4,128,1792]{2,1,0:T(8,128)(2,1)} %shard_map.89), calls=%async_computation.3 | async-start | bytes 3670016 | tf_op jit(solution)/shard_map/all_to_all | solution.py:250
  104.0 26.4 %copy-start.9 = (bf16[1,16,2048]{2,1,0:T(8,128)(2,1)S(1)}, bf16[1,16,2048]{2,1,0:T(8,128)(2,1)}, u32[]{:S(2)}) copy-start(bf16[1,16,2048]{2,1,0:T(8,128)(2,1)} %param.7) | copy-start | bytes 196612
  104.0 28.0 %copy-start.1 = (bf16[1,512,2048]{2,1,0:T(8,128)(2,1)S(1)}, bf16[1,512,2048]{2,1,0:T(8,128)(2,1)}, u32[]{:S(2)}) copy-start(bf16[1,512,2048]{2,1,0:T(8,128)(2,1)} %param.6) | copy-start | bytes 6291460
  127.0 12.1 %all-to-all-start.6 = ((f32[4,16,1792]{2,1,0:T(8,128)}), f32[4,16,1792]{2,1,0:T(8,128)S(1)}, u32[]{:S(2)}, u32[]{:S(2)}) async-start(f32[4,16,1792]{2,1,0:T(8,128)} %bitcast.21), calls=%async_computation.6 | async-start | bytes 917504 | tf_op jit(solution)/shard_map/all_to_all | solution.py:238

commit v2 on v1

v2 whole, which is shorter than its diff:
```python
import jax
import jax.numpy as jnp
from jax import lax
from jax.experimental import pallas as pl
from jax.experimental.pallas import tpu as pltpu
from jax.sharding import PartitionSpec as P

BF = jnp.bfloat16
F32 = jnp.float32
HIGHEST = lax.Precision.HIGHEST
RANK = 16
CHUNKS = 2


def mm(a, b, ca=1, cb=0, precision=None):
    return lax.dot_general(
        a, b, (((ca,), (cb,)), ((), ())), preferred_element_type=F32, precision=precision
    )


def call(kernel, outs, args, scalars=None, flops=0):
    size = sum(x.size * x.dtype.itemsize for x in args)
    size += sum(o.size * o.dtype.itemsize for o in outs)
    specs = [pl.BlockSpec(memory_space=pltpu.VMEM)] * len(args)
    if scalars is not None:
        args = [scalars, *args]
        specs = [pl.BlockSpec(memory_space=pltpu.SMEM), *specs]
    return pl.pallas_call(
        kernel,
        out_shape=[jax.ShapeDtypeStruct(o.shape, o.dtype) for o in outs],
        in_specs=specs,
        out_specs=[pl.BlockSpec(memory_space=pltpu.VMEM)] * len(outs),
        compiler_params=pltpu.CompilerParams(vmem_limit_bytes=48 * 1024 * 1024),
        cost_estimate=pl.CostEstimate(flops=flops, bytes_accessed=size, transcendentals=0),
    )(*args)


def split(x):
    high = x.astype(BF)
    return high, (x - high.astype(F32)).astype(BF)


def lanes(start, size):
    return pl.ds(pl.multiple_of(start, 128), size)


def half_factor_kernel(where, a_out, out):
    half = out.shape[1]
    out[...] = a_out[:, lanes(where[2] * half, half)]


def pack_tokens_kernel(where, cot, ids, gates, out, own):
    tokens, half = cot.shape[0], out.shape[1]
    out[0:tokens, :] = cot[:, lanes((1 - where[1]) * half, half)]
    diagonal = (
        lax.broadcasted_iota(jnp.int32, (tokens, tokens), 0)
        == lax.broadcasted_iota(jnp.int32, (tokens, tokens), 1)
    ).astype(BF)
    id_rows = mm(ids[...].astype(F32).astype(BF), diagonal, 0, 0)
    gate_rows = mm(gates[...].astype(BF), diagonal, 0, 0)
    row = lax.broadcasted_iota(jnp.int32, (16, tokens), 0)
    meta = jnp.where(row == 0, id_rows[0:1], 0.0)
    meta = jnp.where(row == 1, id_rows[1:2], meta)
    meta = jnp.where(row == 2, gate_rows[0:1], meta)
    meta = jnp.where(row == 3, gate_rows[1:2], meta).astype(BF)
    own[...] = meta
    out[tokens : tokens + 16, 0:tokens] = meta
    out[tokens : tokens + 16, tokens:] = jnp.zeros((16, half - tokens), BF)


def low_rank_kernel(hidden, a_in, a_out, out):
    slots = out.shape[2] // 2
    low = mm(a_in[...], hidden[...], 1, 1).astype(BF)
    wide_in, wide_out = a_in[...].astype(F32), a_out[...].astype(F32)
    total_in = jnp.sum(jnp.sum(wide_in * wide_in, axis=1, keepdims=True), axis=0, keepdims=True)
    total_out = jnp.sum(jnp.sum(wide_out * wide_out, axis=1, keepdims=True), axis=0, keepdims=True)
    row = lax.broadcasted_iota(jnp.int32, (RANK, slots), 0)
    stats = jnp.zeros((RANK, slots), F32)
    for base, total in ((0, total_in), (3, total_out)):
        rest = jnp.broadcast_to(total, (RANK, slots))
        for piece in range(3):
            part = rest.astype(BF).astype(F32)
            stats = jnp.where(row == base + piece, part, stats)
            rest = rest - part
    stats = stats.astype(BF)
    for device in range(out.shape[0]):
        chip = device // 2
        out[device, :, 0:slots] = low[:, chip * slots : (chip + 1) * slots]
        out[device, :, slots:] = stats


def fold_of(slots, experts, capacity, source):
    column = lax.broadcasted_iota(jnp.int32, (slots, experts * capacity), 1)
    row = lax.broadcasted_iota(jnp.int32, (slots, experts * capacity), 0)
    return (row == source * capacity + lax.rem(column, capacity)).astype(BF)


def own_expert(experts, capacity):
    shape = (experts * RANK, experts * capacity)
    row = lax.div(lax.broadcasted_iota(jnp.int32, shape, 0), RANK)
    column = lax.div(lax.broadcasted_iota(jnp.int32, shape, 1), capacity)
    return row == column


def relative_experts(order_size, tokens, me):
    row = lax.broadcasted_iota(jnp.int32, (order_size, tokens), 0)
    return jnp.bitwise_xor(row, me).astype(F32)


def partial_kernel(order, where, cot, packed, own_meta, lows, z_out, w_out, *outs):
    keeps, sends = outs[:CHUNKS], outs[CHUNKS:]
    me, core = where[0], where[1]
    experts, tokens = lows.shape[0], cot.shape[0]
    slots = lows.shape[2] // 2
    capacity = slots // 2
    half = packed.shape[1]
    low = jnp.concatenate(
        [lows[jnp.bitwise_xor(me, e)][:, 0:slots] for e in range(experts)], axis=0
    )
    own = own_expert(experts, capacity)
    expert = relative_experts(experts, tokens, me)
    earlier = (
        lax.broadcasted_iota(jnp.int32, (tokens, tokens), 0)
        < lax.broadcasted_iota(jnp.int32, (tokens, tokens), 1)
    ).astype(BF)
    place = lax.broadcasted_iota(jnp.int32, (experts, capacity, tokens), 1).astype(F32)
    rows = []
    for s in range(2):
        meta = (own_meta[...] if s == 0 else packed[tokens:, 0:tokens]).astype(F32)
        first = (meta[0:1] == expert).astype(F32)
        second = (meta[1:2] == expert).astype(F32)
        before = mm((first + second).astype(BF), earlier)
        gate = first * meta[2:3] + second * meta[3:4]
        spread = jnp.where(before[:, None, :] == place, gate[:, None, :], 0.0)
        weights = spread.reshape(experts * capacity, tokens).astype(BF)
        source = jnp.bitwise_xor(core, s)
        wide = mm(low, fold_of(slots, experts, capacity, source))
        wide = jnp.where(own, wide, 0.0).astype(BF)
        z = mm(wide, weights).astype(BF)
        rows.append(z.reshape(experts // 4, 2, 2 * RANK, tokens))
        if s == 0:
            w_out[...] = weights
            for place_of, e in enumerate(order):
                z_out[place_of * RANK : (place_of + 1) * RANK, :] = z[e * RANK : (e + 1) * RANK]
    count = experts * RANK // 2
    wide = half // CHUNKS
    for piece in range(CHUNKS):
        mine = cot[:, lanes(core * half + piece * wide, wide)]
        other = packed[0:tokens, piece * wide : (piece + 1) * wide]
        for side, target in ((0, keeps[piece]), (1, sends[piece])):
            first = rows[0][:, side].reshape(count, tokens)
            second = rows[1][:, side].reshape(count, tokens)
            target[...] = (mm(first, mine) + mm(second, other)).astype(target.dtype)


def fold_step_kernel(keep, received, kept, sent):
    rows, width = keep.shape
    total = keep[...] + received[...].astype(F32)
    total = total.reshape(rows // (4 * RANK), 2, 2 * RANK, width)
    kept[...] = total[:, 0].reshape(rows // 2, width)
    sent[...] = total[:, 1].reshape(rows // 2, width).astype(sent.dtype)


def last_fold_kernel(keep, received, kept, sent):
    total = keep[...] + received[...].astype(F32)
    kept[...] = total[0:RANK]
    sent[...] = total[RANK:]


def grad_low_kernel(order, where, cot, w, *refs):
    factors, out = refs[:-1], refs[-1]
    me, side = where[0], where[2]
    experts, _, slots = out.shape
    tokens, half = cot.shape[0], factors[0].shape[1]
    capacity = slots // 4
    own_side = cot[:, lanes(side * half, half)]
    far_side = cot[:, lanes((1 - side) * half, half)]
    blocks = []
    for near, far in zip(factors[0::2], factors[1::2]):
        rows = mm(near[...], own_side, 1, 1) + mm(far[...], far_side, 1, 1)
        blocks += [rows[r : r + RANK] for r in range(0, rows.shape[0], RANK)]
    coords = jnp.concatenate([blocks[order.index(e)] for e in range(experts)], axis=0)
    high, low = split(coords)
    picked = mm(high, w[...], 1, 1) + mm(low, w[...], 1, 1)
    picked = jnp.where(own_expert(experts, capacity), picked, 0.0).astype(BF)
    fold = fold_of(slots, experts, capacity, lax.rem(me, 4))
    rows = mm(picked, fold, 1, 1).astype(out.dtype)
    for e in range(experts):
        out[jnp.bitwise_xor(me, e)] = rows[e * RANK : (e + 1) * RANK]


def delta_kernel(where, z, *refs):
    factors, out = refs[:-1], refs[-1]
    half = factors[0].shape[1]
    for flip in range(2):
        total, start = None, 0
        for factor in factors[flip::2]:
            part = mm(z[start : start + factor.shape[0], :], factor[...], 0, 0)
            total = part if total is None else total + part
            start += factor.shape[0]
        side = jnp.bitwise_xor(where[2], flip)
        out[:, lanes(side * half, half)] = total.astype(BF)


def inverse_kernel(a_in, a_out, lows, inv_in, inv_out):
    experts, _, double = lows.shape
    stats = jnp.sum(lows[:, :, double // 2 :].astype(F32), axis=0)
    row = lax.broadcasted_iota(jnp.int32, (RANK, RANK), 0)
    column = lax.broadcasted_iota(jnp.int32, (RANK, RANK), 1)
    eye = (row == column).astype(F32)
    works = []
    for base, factor in ((0, a_in), (3, a_out)):
        pieces = stats[base : base + 1, 0:1] + stats[base + 1 : base + 2, 0:1]
        damp = (pieces + stats[base + 2 : base + 3, 0:1]) / (float(RANK) * experts)
        gram = mm(factor[...], factor[...], 1, 1) + damp * eye
        works.append([gram, eye])
    for j in range(RANK):
        for work in works:
            gram, inverse = work
            pivot = 1.0 / gram[j : j + 1, j : j + 1]
            gram_row, inverse_row = gram[j : j + 1] * pivot, inverse[j : j + 1] * pivot
            scale = gram[:, j : j + 1]
            work[0] = jnp.where(row == j, gram_row, gram - scale * gram_row)
            work[1] = jnp.where(row == j, inverse_row, inverse - scale * inverse_row)
    inv_in[...] = works[0][1]
    inv_out[...] = works[1][1]


def scaled_in_kernel(coords, hidden, inverse, out):
    pieces = []
    for base in range(0, coords.shape[0], 4):
        total = coords[base].astype(F32)
        for q in range(1, 4):
            total = total + coords[base + q].astype(F32)
        pieces.append(total)
    grad_low = jnp.concatenate(pieces, axis=1).astype(BF)
    out[...] = mm(inverse[...], mm(grad_low, hidden[...]), precision=HIGHEST)


def scaled_out_kernel(where, inverse, *refs):
    pieces, out = refs[:-1], refs[-1]
    wide = pieces[0].shape[1]
    half = wide * CHUNKS
    for flip in range(2):
        base = jnp.bitwise_xor(where[1], flip) * half
        for piece in range(CHUNKS):
            rows = mm(inverse[...], pieces[flip * CHUNKS + piece][...], precision=HIGHEST)
            out[:, lanes(base + piece * wide, wide)] = rows


def on_device(hidden_slots, adapter_in, adapter_out, expert_ids, gate_weights, cotangent):
    experts, groups = lax.axis_size("expert"), lax.axis_size("group")
    me, group = lax.axis_index("expert"), lax.axis_index("group")
    where = jnp.stack([me, me % 2, group % 2]).astype(jnp.int32)
    hidden, a_in, a_out = hidden_slots[0], adapter_in[0], adapter_out[0]
    width = a_out.shape[1]
    half = width // 2
    wide = half // CHUNKS
    tokens = cotangent.shape[0]
    capacity = hidden.shape[0] // experts
    struct = jax.ShapeDtypeStruct

    def swap(x, bit):
        return lax.ppermute(x, "expert", [(i, i ^ bit) for i in range(experts)])

    def swap_side(x):
        return lax.ppermute(x, "group", [(i, i ^ 1) for i in range(groups)])

    def spread(x):
        return lax.all_to_all(x, "expert", split_axis=0, concat_axis=0, tiled=True)

    far_bits = []
    bit = 4
    while bit < experts:
        far_bits.append(bit)
        bit *= 2

    (block,) = call(half_factor_kernel, [struct((RANK, half), BF)], [a_out], where)
    order = [0]
    for bit in [2, *reversed(far_bits)]:
        received = swap(block, bit)
        order = order + [e ^ bit for e in order]
        if bit == far_bits[0]:
            near = [block, received]
        else:
            block = jnp.concatenate([block, received], axis=0)
    order = order + [e ^ 1 for e in order]

    packed, own_meta = call(
        pack_tokens_kernel,
        [struct((tokens + 16, half), BF), struct((16, tokens), BF)],
        [cotangent, expert_ids, gate_weights],
        where,
    )
    packed = swap(packed, 1)
    (lows,) = call(
        low_rank_kernel, [struct((experts, RANK, 4 * capacity), BF)], [hidden, a_in, a_out]
    )
    lows = spread(lows)
    inv_in, inv_out = call(
        inverse_kernel, [struct((RANK, RANK), F32)] * 2, [a_in, a_out, lows]
    )

    count = experts * RANK // 2
    z, weights, *parts = call(
        lambda *refs: partial_kernel(order, *refs),
        [struct((experts * RANK, tokens), BF), struct((experts * capacity, tokens), BF)]
        + [struct((count, wide), F32)] * CHUNKS
        + [struct((count, wide), BF)] * CHUNKS,
        [cotangent, packed, own_meta, lows],
        where,
    )
    kept, sent = parts[:CHUNKS], parts[CHUNKS:]
    own_rows, far_rows = [], []
    for piece in range(CHUNKS):
        keep, send, rows = kept[piece], sent[piece], count
        for bit in [2, *far_bits]:
            received = swap(send, bit)
            if bit == far_bits[-1]:
                shapes, step = [struct((RANK, wide), F32)] * 2, last_fold_kernel
            else:
                rows //= 2
                shapes = [struct((rows, wide), F32), struct((rows, wide), BF)]
                step = fold_step_kernel
            keep, send = call(step, shapes, [keep, received])
        own_rows.append(keep)
        far_rows.append(swap(send, 1))

    factors = []
    for block in near:
        factors += [block, swap_side(block)]
    factors = factors + [swap(block, 1) for block in factors]
    (coords,) = call(
        lambda *refs: grad_low_kernel(order, *refs),
        [struct((experts, RANK, 4 * capacity), BF)],
        [cotangent, weights, *factors],
        where,
    )
    coords = spread(coords)
    (delta,) = call(delta_kernel, [struct((tokens, width), BF)], [z, *factors], where)
    (scaled_in,) = call(
        scaled_in_kernel, [struct((RANK, hidden.shape[1]), F32)], [coords, hidden, inv_out]
    )
    (scaled_out,) = call(
        scaled_out_kernel, [struct((RANK, width), F32)], [inv_in, *own_rows, *far_rows], where
    )
    return delta, scaled_in[None], scaled_out[None]


def solution(mesh):
    every = ("group", "expert")
    return jax.shard_map(
        on_device,
        mesh=mesh,
        in_specs=(
            P(every, None, None),
            P("expert", None, None),
            P("expert", None, None),
            P(every, None),
            P(every, None),
            P(every, None),
        ),
        out_specs=(P(every, None), P(every, None, None), P(every, None, None)),
        check_vma=False,
    )
```

time: 141 us -> 111 us (0.79)
  waiting for transfers between devices: 54 us -> 32.1 us
  blocking collectives: 30.4 us -> 14.8 us
  Pallas kernels: 13.5 us -> 21.2 us
  local copies, waits for them, and re-layouts: 14.2 us -> 21.4 us
  starting transfers between devices: 25.2 us -> 20.1 us
  other arithmetic: 2.26 us -> 0.12 us
    all_to_all x6 -> x1, waiting for transfers between devices: 54 us -> 0.01 us  [spread(): return lax.all_to_all(x, 'expert', split_axis=0, concat_axis=0, tiled=True)]
    ppermute x0 -> x18, waiting for transfers between devices: none -> 32.1 us  [the longest x16 24.1 us: swap(): return lax.ppermute(x, 'expert', [(i, i ^ bit) for i in range(experts)])]
    all_to_all x6 -> x1, starting transfers between devices: 25.2 us -> 4.13 us  [spread(): return lax.all_to_all(x, 'expert', split_axis=0, concat_axis=0, tiled=True)]
    all_gather x1 -> x0, blocking collectives: 19.9 us -> none  [on_device(): factor = lax.all_gather(plane_factor, 'z', axis=0, tiled=True)]
    ppermute x0 -> x18, starting transfers between devices: none -> 16 us  [the longest x16 13.9 us: swap(): return lax.ppermute(x, 'expert', [(i, i ^ bit) for i in range(experts)])]
    unnamed x33 -> x74, local copies, waits for them, and re-layouts: 11.3 us -> 21.4 us
    pallas_call x9 -> x15, Pallas kernels: 13.5 us -> 21.2 us  [call(): pl.pallas_call(kernel, out_shape=[jax.ShapeDtypeStruct(o.shape, o.dtype)...]
    all_to_all x1, blocking collectives: 10.5 us -> 14.8 us  [spread(): return lax.all_to_all(x, 'expert', split_axis=0, concat_axis=0, tiled=True)]
  transfers between devices with their start and end apart: 6 -> 19, of which waited for: 5 -> 5; matrix products, arithmetic and copies ran while one was open for 6% -> 1% of each run, Pallas kernels for 4% -> 17%
where the time goes in v2:
time: 111 us
  waiting for transfers between devices  32.1 us (29%)
  local copies, waits for them, and re-layouts  21.4 us (19%)
  Pallas kernels  21.2 us (19%)
  starting transfers between devices  20.1 us (18%)
  blocking collectives  14.8 us (13%)
    ppermute x16, waiting for transfers between devices, swap(): return lax.ppermute(x, 'expert', [(i, i ^ bit) for i in range(experts)])  24.1 us
    unnamed x74, local copies, waits for them, and re-layouts  21.4 us
    pallas_call x15, Pallas kernels, call(): pl.pallas_call(kernel, out_shape=[jax.ShapeDtypeStruct(o.shape, o.dtype)...  21.2 us
    all_to_all x1, blocking collectives, spread(): return lax.all_to_all(x, 'expert', split_axis=0, concat_axis=0, tiled=True)  14.8 us
    ppermute x16, starting transfers between devices, swap(): return lax.ppermute(x, 'expert', [(i, i ^ bit) for i in range(experts)])  13.9 us
    ppermute x2, waiting for transfers between devices, swap_side(): return lax.ppermute(x, 'group', [(i, i ^ 1) for i in range(groups)])  7.96 us
    all_to_all x1, starting transfers between devices, spread(): return lax.all_to_all(x, 'expert', split_axis=0, concat_axis=0, tiled=True)  4.13 us
  transfers between devices with their start and end apart: 19, of which 5 were waited for; matrix products, arithmetic and copies ran while one was open for 1% of the time, Pallas kernels for 17%

profile of v2, /device:TPU:0, one launch (start us, length us, event | category | flops | bytes accessed | tf_op | source)
XLA Modules:
  0.0 110.5 jit_solution(9980810488831228506)
XLA Ops:
  2.2 3.0 %collective-permute-start.1 = (bf16[16,3584]{1,0:T(8,128)(2,1)S(1)}, bf16[16,3584]{1,0:T(8,128)(2,1)S(1)}, u32[]{:S(2)}, u32[]{:S(2)}) collective-permute-start(bf16[16,3584]{1,0:T(8,128)(2,1)S(1)} %shard_map.88), channel_id=1, source_target_pairs={{0,2},{1,3},{2,0},{3,1},{4,6},{5,7},{6,4},{7,5},{8,10},{9,11},{10,... | collective-permute-start | bytes 344072 | tf_op jit(solution)/shard_map/ppermute | solution.py:264
  5.3 3.1 %collective-permute-done.1 = bf16[16,3584]{1,0:T(8,128)(2,1)S(1)} collective-permute-done((bf16[16,3584]{1,0:T(8,128)(2,1)S(1)}, bf16[16,3584]{1,0:T(8,128)(2,1)S(1)}, u32[]{:S(2)}, u32[]{:S(2)}) %collective-permute-start.1) | collective-permute-done | bytes 114720 | tf_op jit(solution)/shard_map/ppermute | solution.py:264
  8.4 2.9 %collective-permute-start.2 = (bf16[32,3584]{1,0:T(8,128)(2,1)S(1)}, bf16[32,3584]{1,0:T(8,128)(2,1)S(1)}, u32[]{:S(2)}, u32[]{:S(2)}) collective-permute-start(bf16[32,3584]{1,0:T(8,128)(2,1)S(1)} %pad_maximum_fusion.1), channel_id=1, source_target_pairs={{0,8},{1,9},{2,10},{3,11},{4,12},{5,13},{6,14},{7,15},{8,0},{9,1},... | collective-permute-start | bytes 688136 | tf_op jit(solution)/shard_map/ppermute | solution.py:264
  12.9 1.5 %copy-done = bf16[128,7168]{1,0:T(8,128)(2,1)S(1)} copy-done((bf16[128,7168]{1,0:T(8,128)(2,1)S(1)}, bf16[128,7168]{1,0:T(8,128)(2,1)}, u32[]{:S(2)}) %copy-start) | copy-done | bytes 1835032
  15.1 6.0 %collective-permute-done.2 = bf16[32,3584]{1,0:T(8,128)(2,1)S(1)} collective-permute-done((bf16[32,3584]{1,0:T(8,128)(2,1)S(1)}, bf16[32,3584]{1,0:T(8,128)(2,1)S(1)}, u32[]{:S(2)}, u32[]{:S(2)}) %collective-permute-start.2) | collective-permute-done | bytes 229408 | tf_op jit(solution)/shard_map/ppermute | solution.py:264
  22.5 14.8 %all_to_all.10.refs_4_.lows = bf16[16,16,128]{2,1,0:T(8,128)(2,1)S(1)} all-to-all(bf16[16,16,128]{2,1,0:T(8,128)(2,1)S(1)} %shard_map.86), channel_id=1, replica_groups=mesh['group'=2,'expert'=16] {'expert'}, dimensions={0} | all-to-all | bytes 131072 | tf_op jit(solution)/shard_map/all_to_all | solution.py:270
  37.3 2.2 %shard_map.87 = (bf16[256,128]{1,0:T(8,128)(2,1)S(1)}, bf16[512,128]{1,0:T(8,128)(2,1)S(1)}, f32[128,1792]{1,0:T(8,128)S(1)}, f32[128,1792]{1,0:T(8,128)S(1)}, b...) custom-call(s32[3]{0:T(128)S(1)} %pad_add_fusion.where.refs_0_, bf16[128,7168]{1,0:T(8,128)(2,1)S(1)} %copy-done.1, ...), custom_call_target="tpu_custom_call" | custom-call | bytes 5885952 | tf_op jit(solution)/shard_map/pallas_call | solution.py:28
  39.7 1.5 %collective-permute-start.3 = (bf16[64,3584]{1,0:T(8,128)(2,1)S(1)}, bf16[64,3584]{1,0:T(8,128)(2,1)S(1)}, u32[]{:S(2)}, u32[]{:S(2)}) collective-permute-start(bf16[64,3584]{1,0:T(8,128)(2,1)S(1)} %pad_maximum_fusion.refs_0_.refs_3_), channel_id=1, source_target_pairs={{0,16},{16,0},{1,17},{17,1},{2,18},{18,2},{3,19},{19,3},{4,20},{20... | collective-permute-start | bytes 1376264 | tf_op jit(solution)/shard_map/ppermute | solution.py:267
  41.7 1.9 %collective-permute-start.10 = (bf16[128,1792]{1,0:T(8,128)(2,1)S(1)}, bf16[128,1792]{1,0:T(8,128)(2,1)S(1)}, u32[]{:S(2)}, u32[]{:S(2)}) collective-permute-start(bf16[128,1792]{1,0:T(8,128)(2,1)S(1)} %get-tuple-element.32), channel_id=1, source_target_pairs={{0,2},{1,3},{2,0},{3,1},{4,6},{5,7},{6,4},{7,5},{8,10},{9,11},{10,... | collective-permute-start | bytes 1376264 | tf_op jit(solution)/shard_map/ppermute | solution.py:264
  43.7 9.4 %collective-permute-done.13.received = bf16[128,1792]{1,0:T(8,128)(2,1)S(1)} collective-permute-done((bf16[128,1792]{1,0:T(8,128)(2,1)S(1)}, bf16[128,1792]{1,0:T(8,128)(2,1)S(1)}, u32[]{:S(2)}, u32[]{:S(2)}) %collective-permute-start.13) | collective-permute-done | bytes 458784 | tf_op jit(solution)/shard_map/ppermute | solution.py:264
  53.8 8.0 %collective-permute-done.5.refs_3_.refs_6_ = bf16[64,3584]{1,0:T(8,128)(2,1)S(1)} collective-permute-done((bf16[64,3584]{1,0:T(8,128)(2,1)S(1)}, bf16[64,3584]{1,0:T(8,128)(2,1)S(1)}, u32[]{:S(2)}, u32[]{:S(2)}) %collective-permute-start.5) | collective-permute-done | bytes 458784 | tf_op jit(solution)/shard_map/ppermute | solution.py:267
  64.5 5.5 %collective-permute-done.11.received = bf16[64,1792]{1,0:T(8,128)(2,1)S(1)} collective-permute-done((bf16[64,1792]{1,0:T(8,128)(2,1)S(1)}, bf16[64,1792]{1,0:T(8,128)(2,1)S(1)}, u32[]{:S(2)}, u32[]{:S(2)}) %collective-permute-start.11) | collective-permute-done | bytes 229408 | tf_op jit(solution)/shard_map/ppermute | solution.py:264
  72.4 2.0 %collective-permute-start.12 = (bf16[32,1792]{1,0:T(8,128)(2,1)}, bf16[32,1792]{1,0:T(8,128)(2,1)}, u32[]{:S(2)}, u32[]{:S(2)}) collective-permute-start(bf16[32,1792]{1,0:T(8,128)(2,1)} %get-tuple-element.36), channel_id=1, source_target_pairs={{0,8},{1,9},{2,10},{3,11},{4,12},{5,13},{6,14},{7,15},{8,0},{9,1},... | collective-permute-start | bytes 344072 | tf_op jit(solution)/shard_map/ppermute | solution.py:264
  74.4 4.2 %shard_map.90 = bf16[16,16,128]{2,1,0:T(8,128)(2,1)} custom-call(s32[3]{0:T(128)S(1)} %copy-done.29, bf16[128,7168]{1,0:T(8,128)(2,1)S(1)} %copy-done.1, bf16[512,128]{1,0:T(8,128)(2,1)S(1)} %get-tuple-element.28.refs_2_, bf16[64,3584]{1,0:T(8,128)(2,1)S(1)} %pad_maximum_fusion.refs_0_.refs_3_, bf16[64,3584]{1,0:T(8,128)(2,1)S(1)} %collective-permute-done.3.refs_1_.refs_4_, ...), custom_call_target="tpu_custom_call" | custom-call | bytes 5701632 | tf_op jit(solution)/shard_map/pallas_call | solution.py:28
  81.8 4.1 %all-to-all-start.1 = ((bf16[16,16,128]{2,1,0:T(8,128)(2,1)}), bf16[16,16,128]{2,1,0:T(8,128)(2,1)S(1)}, u32[]{:S(2)}, u32[]{:S(2)}) async-start(bf16[16,16,128]{2,1,0:T(8,128)(2,1)} %shard_map.90), calls=%async_computation.1 | async-start | bytes 131072 | tf_op jit(solution)/shard_map/all_to_all | solution.py:270
  90.4 1.6 %shard_map.95 = (f32[16,1792]{1,0:T(8,128)S(1)}, f32[16,1792]{1,0:T(8,128)}) custom-call(f32[32,1792]{1,0:T(8,128)S(1)} %copy-done.21, bf16[32,1792]{1,0:T(8,128)(2,1)} %collective-permute-done.12.received), custom_call_target="tpu_custom_call" | custom-call | bytes 573440 | tf_op jit(solution)/shard_map/pallas_call | solution.py:28
  92.7 1.5 %shard_map.91 = (f32[16,16]{1,0:T(8,128)S(1)}, f32[16,16]{1,0:T(8,128)S(1)}) custom-call(bf16[16,2048]{1,0:T(8,128)(2,1)S(1)} %bitcast.14, bf16[16,7168]{1,0:T(8,128)(2,1)S(1)} %bitcast.12, bf16[16,16,128]{2,1,0:T(8,128)(2,1)S(1)} %all_to_all.10.refs_4_.lows), custom_call_target="tpu_custom_call" | custom-call | bytes 362496 | tf_op jit(solution)/shard_map/pallas_call | solution.py:28
  95.5 1.0 copy-done.6
  97.5 1.0 copy-done.10
  98.5 1.0 copy-done.12
  99.6 1.0 copy-done.14
  103.0 3.8 %shard_map.89 = bf16[128,7168]{1,0:T(8,128)(2,1)} custom-call(s32[3]{0:T(128)S(1)} %copy-done.30, bf16[256,128]{1,0:T(8,128)(2,1)S(1)} %copy-done.27, bf16[64,3584]{1,0:T(8,128)(2,1)S(1)} %pad_maximum_fusion.refs_0_.refs_3_, bf16[64,3584]{1,0:T(8,128)(2,1)S(1)} %copy-done.6, bf16[64,3584]{1,0:T(8,128)(2,1)S(1)} %collective-permute-done.4.refs_2_.refs_5_, ...), custom_call_target="tpu_custom_call" | custom-call | bytes 5570560 | tf_op jit(solution)/shard_map/pallas_call | solution.py:28
  106.9 1.2 %shard_map.92 = f32[16,2048]{1,0:T(8,128)} custom-call(bf16[16,16,128]{2,1,0:T(8,128)(2,1)S(1)} %all-to-all-done.1.coords, bf16[512,2048]{1,0:T(8,128)(2,1)S(1)} %bitcast.9, f32[16,16]{1,0:T(8,128)S(1)} %copy-done.35), custom_call_target="tpu_custom_call" | custom-call | bytes 2294784 | tf_op jit(solution)/shard_map/pallas_call | solution.py:28
  108.2 2.4 %shard_map.99 = f32[16,7168]{1,0:T(8,128)} custom-call(s32[3]{0:T(128)S(1)} %copy-done.31, f32[16,16]{1,0:T(8,128)S(1)} %copy-done.33, f32[16,1792]{1,0:T(8,128)S(1)} %copy-done.23, f32[16,1792]{1,0:T(8,128)S(1)} %get-tuple-element.44.refs_1_, f32[16,1792]{1,0:T(8,128)} %collective-permute-done.16.refs_2_, f32[16,1792]{1,0:T(8,128)} %collective-permute-done.17.refs_3_), custom_call_target="tpu_custom_call" | custom-call | bytes 918528 | tf_op jit(solution)/shard_map/pallas_call | solution.py:28
  (107 shorter events, 24.9 us)
Async XLA Ops:
  0.7 36.6 %copy-start.28 = (s32[3]{0:T(128)}, s32[3]{0:T(128)S(1)}, u32[]{:S(2)}) copy-start(s32[3]{0:T(128)S(1)} %pad_add_fusion.where.refs_0_) | copy-start | bytes 40
  2.2 6.2 %collective-permute-start.1 = (bf16[16,3584]{1,0:T(8,128)(2,1)S(1)}, bf16[16,3584]{1,0:T(8,128)(2,1)S(1)}, u32[]{:S(2)}, u32[]{:S(2)}) collective-permute-start(bf16[16,3584]{1,0:T(8,128)(2,1)S(1)} %shard_map.88), channel_id=1, source_target_pairs={{0,2},{1,3},{2,0},{3,1},{4,6},{5,7},{6,4},{7,5},{8,10},{9,11},{10,... | collective-permute-start | bytes 344072 | tf_op jit(solution)/shard_map/ppermute | solution.py:264
  8.4 12.7 %collective-permute-start.2 = (bf16[32,3584]{1,0:T(8,128)(2,1)S(1)}, bf16[32,3584]{1,0:T(8,128)(2,1)S(1)}, u32[]{:S(2)}, u32[]{:S(2)}) collective-permute-start(bf16[32,3584]{1,0:T(8,128)(2,1)S(1)} %pad_maximum_fusion.1), channel_id=1, source_target_pairs={{0,8},{1,9},{2,10},{3,11},{4,12},{5,13},{6,14},{7,15},{8,0},{9,1},... | collective-permute-start | bytes 688136 | tf_op jit(solution)/shard_map/ppermute | solution.py:264
  15.1 22.2 %copy-start.1 = (bf16[128,7168]{1,0:T(8,128)(2,1)S(1)}, bf16[128,7168]{1,0:T(8,128)(2,1)}, u32[]{:S(2)}) copy-start(bf16[128,7168]{1,0:T(8,128)(2,1)} %refs_1_.3) | copy-start | bytes 5505028
  15.1 22.2 %collective-permute-start = (bf16[144,3584]{1,0:T(8,128)(2,1)S(1)}, bf16[144,3584]{1,0:T(8,128)(2,1)S(1)}, u32[]{:S(2)}, u32[]{:S(2)}) collective-permute-start(bf16[144,3584]{1,0:T(8,128)(2,1)S(1)} %get-tuple-element.25), channel_id=1, source_target_pairs={{0,1},{1,0},{2,3},{3,2},{4,5},{5,4},{6,7},{7,6},{8,9},{9,8},{10,11... | collective-permute-start | bytes 3096584 | tf_op jit(solution)/shard_map/ppermute | solution.py:264
  21.1 20.0 %collective-permute-start.4 = (bf16[64,3584]{1,0:T(8,128)(2,1)S(1)}, bf16[64,3584]{1,0:T(8,128)(2,1)S(1)}, u32[]{:S(2)}, u32[]{:S(2)}) collective-permute-start(bf16[64,3584]{1,0:T(8,128)(2,1)S(1)} %pad_maximum_fusion.refs_0_.refs_3_), channel_id=1, source_target_pairs={{0,4},{1,5},{2,6},{3,7},{4,0},{5,1},{6,2},{7,3},{8,12},{9,13},{10,... | collective-permute-start | bytes 1376264 | tf_op jit(solution)/shard_map/ppermute | solution.py:264
  39.5 32.1 %copy-start.26 = (bf16[256,128]{1,0:T(8,128)(2,1)}, bf16[256,128]{1,0:T(8,128)(2,1)S(1)}, u32[]{:S(2)}) copy-start(bf16[256,128]{1,0:T(8,128)(2,1)S(1)} %get-tuple-element.27.z) | copy-start | bytes 196612
  39.5 13.5 %collective-permute-start.13 = (bf16[128,1792]{1,0:T(8,128)(2,1)S(1)}, bf16[128,1792]{1,0:T(8,128)(2,1)S(1)}, u32[]{:S(2)}, u32[]{:S(2)}) collective-permute-start(bf16[128,1792]{1,0:T(8,128)(2,1)S(1)} %get-tuple-element.39), channel_id=1, source_target_pairs={{0,2},{1,3},{2,0},{3,1},{4,6},{5,7},{6,4},{7,5},{8,10},{9,11},{10,... | collective-permute-start | bytes 1376264 | tf_op jit(solution)/shard_map/ppermute | solution.py:264
  39.7 13.6 %collective-permute-start.3 = (bf16[64,3584]{1,0:T(8,128)(2,1)S(1)}, bf16[64,3584]{1,0:T(8,128)(2,1)S(1)}, u32[]{:S(2)}, u32[]{:S(2)}) collective-permute-start(bf16[64,3584]{1,0:T(8,128)(2,1)S(1)} %pad_maximum_fusion.refs_0_.refs_3_), channel_id=1, source_target_pairs={{0,16},{16,0},{1,17},{17,1},{2,18},{18,2},{3,19},{19,3},{4,20},{20... | collective-permute-start | bytes 1376264 | tf_op jit(solution)/shard_map/ppermute | solution.py:267
  41.2 20.6 %collective-permute-start.5 = (bf16[64,3584]{1,0:T(8,128)(2,1)S(1)}, bf16[64,3584]{1,0:T(8,128)(2,1)S(1)}, u32[]{:S(2)}, u32[]{:S(2)}) collective-permute-start(bf16[64,3584]{1,0:T(8,128)(2,1)S(1)} %collective-permute-done.4.refs_2_.refs_5_), channel_id=1, source_target_pairs={{0,16},{16,0},{1,17},{17,1},{2,18},{18,2},{3,19},{19,3},{4,20},{20... | collective-permute-start | bytes 1376264 | tf_op jit(solution)/shard_map/ppermute | solution.py:267
  41.7 20.1 %collective-permute-start.10 = (bf16[128,1792]{1,0:T(8,128)(2,1)S(1)}, bf16[128,1792]{1,0:T(8,128)(2,1)S(1)}, u32[]{:S(2)}, u32[]{:S(2)}) collective-permute-start(bf16[128,1792]{1,0:T(8,128)(2,1)S(1)} %get-tuple-element.32), channel_id=1, source_target_pairs={{0,2},{1,3},{2,0},{3,1},{4,6},{5,7},{6,4},{7,5},{8,10},{9,11},{10,... | collective-permute-start | bytes 1376264 | tf_op jit(solution)/shard_map/ppermute | solution.py:264
  53.0 21.4 %copy-start.29 = (s32[3]{0:T(128)S(1)}, s32[3]{0:T(128)}, u32[]{:S(2)}) copy-start(s32[3]{0:T(128)} %copy-done.28) | copy-start | bytes 40
  53.2 9.3 %collective-permute-start.14 = (bf16[64,1792]{1,0:T(8,128)(2,1)S(1)}, bf16[64,1792]{1,0:T(8,128)(2,1)S(1)}, u32[]{:S(2)}, u32[]{:S(2)}) collective-permute-start(bf16[64,1792]{1,0:T(8,128)(2,1)S(1)} %get-tuple-element.41), channel_id=1, source_target_pairs={{0,4},{1,5},{2,6},{3,7},{4,0},{5,1},{6,2},{7,3},{8,12},{9,13},{10,... | collective-permute-start | bytes 688136 | tf_op jit(solution)/shard_map/ppermute | solution.py:264
  53.3 19.1 %collective-permute-start.6 = (bf16[64,3584]{1,0:T(8,128)(2,1)S(1)}, bf16[64,3584]{1,0:T(8,128)(2,1)S(1)}, u32[]{:S(2)}, u32[]{:S(2)}) collective-permute-start(bf16[64,3584]{1,0:T(8,128)(2,1)S(1)} %pad_maximum_fusion.refs_0_.refs_3_), channel_id=1, source_target_pairs={{0,1},{1,0},{2,3},{3,2},{4,5},{5,4},{6,7},{7,6},{8,9},{9,8},{10,11... | collective-permute-start | bytes 1376264 | tf_op jit(solution)/shard_map/ppermute | solution.py:264
  53.3 21.1 %copy-start.5 = (bf16[64,3584]{1,0:T(8,128)(2,1)}, bf16[64,3584]{1,0:T(8,128)(2,1)S(1)}, u32[]{:S(2)}) copy-start(bf16[64,3584]{1,0:T(8,128)(2,1)S(1)} %collective-permute-done.3.refs_1_.refs_4_) | copy-start | bytes 1376260
  53.3 21.0 %collective-permute-start.8 = (bf16[64,3584]{1,0:T(8,128)(2,1)S(1)}, bf16[64,3584]{1,0:T(8,128)(2,1)S(1)}, u32[]{:S(2)}, u32[]{:S(2)}) collective-permute-start(bf16[64,3584]{1,0:T(8,128)(2,1)S(1)} %collective-permute-done.4.refs_2_.refs_5_), channel_id=1, source_target_pairs={{0,1},{1,0},{2,3},{3,2},{4,5},{5,4},{6,7},{7,6},{8,9},{9,8},{10,11... | collective-permute-start | bytes 1376264 | tf_op jit(solution)/shard_map/ppermute | solution.py:264
  61.8 12.6 %collective-permute-start.7 = (bf16[64,3584]{1,0:T(8,128)(2,1)S(1)}, bf16[64,3584]{1,0:T(8,128)(2,1)S(1)}, u32[]{:S(2)}, u32[]{:S(2)}) collective-permute-start(bf16[64,3584]{1,0:T(8,128)(2,1)S(1)} %collective-permute-done.3.refs_1_.refs_4_), channel_id=1, source_target_pairs={{0,1},{1,0},{2,3},{3,2},{4,5},{5,4},{6,7},{7,6},{8,9},{9,8},{10,11... | collective-permute-start | bytes 1376264 | tf_op jit(solution)/shard_map/ppermute | solution.py:264
  61.8 12.6 %collective-permute-start.9 = (bf16[64,3584]{1,0:T(8,128)(2,1)S(1)}, bf16[64,3584]{1,0:T(8,128)(2,1)S(1)}, u32[]{:S(2)}, u32[]{:S(2)}) collective-permute-start(bf16[64,3584]{1,0:T(8,128)(2,1)S(1)} %collective-permute-done.5.refs_3_.refs_6_), channel_id=1, source_target_pairs={{0,1},{1,0},{2,3},{3,2},{4,5},{5,4},{6,7},{7,6},{8,9},{9,8},{10,11... | collective-permute-start | bytes 1376264 | tf_op jit(solution)/shard_map/ppermute | solution.py:264
  62.4 7.6 %collective-permute-start.11 = (bf16[64,1792]{1,0:T(8,128)(2,1)S(1)}, bf16[64,1792]{1,0:T(8,128)(2,1)S(1)}, u32[]{:S(2)}, u32[]{:S(2)}) collective-permute-start(bf16[64,1792]{1,0:T(8,128)(2,1)S(1)} %get-tuple-element.34), channel_id=1, source_target_pairs={{0,4},{1,5},{2,6},{3,7},{4,0},{5,1},{6,2},{7,3},{8,12},{9,13},{10,... | collective-permute-start | bytes 688136 | tf_op jit(solution)/shard_map/ppermute | solution.py:264
  70.1 15.9 %collective-permute-start.15 = (bf16[32,1792]{1,0:T(8,128)(2,1)}, bf16[32,1792]{1,0:T(8,128)(2,1)S(1)}, u32[]{:S(2)}, u32[]{:S(2)}) collective-permute-start(bf16[32,1792]{1,0:T(8,128)(2,1)} %get-tuple-element.43), channel_id=1, source_target_pairs={{0,8},{1,9},{2,10},{3,11},{4,12},{5,13},{6,14},{7,15},{8,0},{9,1},... | collective-permute-start | bytes 344072 | tf_op jit(solution)/shard_map/ppermute | solution.py:264
  72.4 17.1 %collective-permute-start.12 = (bf16[32,1792]{1,0:T(8,128)(2,1)}, bf16[32,1792]{1,0:T(8,128)(2,1)}, u32[]{:S(2)}, u32[]{:S(2)}) collective-permute-start(bf16[32,1792]{1,0:T(8,128)(2,1)} %get-tuple-element.36), channel_id=1, source_target_pairs={{0,8},{1,9},{2,10},{3,11},{4,12},{5,13},{6,14},{7,15},{8,0},{9,1},... | collective-permute-start | bytes 344072 | tf_op jit(solution)/shard_map/ppermute | solution.py:264
  81.8 25.1 %all-to-all-start.1 = ((bf16[16,16,128]{2,1,0:T(8,128)(2,1)}), bf16[16,16,128]{2,1,0:T(8,128)(2,1)S(1)}, u32[]{:S(2)}, u32[]{:S(2)}) async-start(bf16[16,16,128]{2,1,0:T(8,128)(2,1)} %shard_map.90), calls=%async_computation.1 | async-start | bytes 131072 | tf_op jit(solution)/shard_map/all_to_all | solution.py:270
  89.1 19.1 %collective-permute-start.17 = (f32[16,1792]{1,0:T(8,128)}, f32[16,1792]{1,0:T(8,128)}, u32[]{:S(2)}, u32[]{:S(2)}) collective-permute-start(f32[16,1792]{1,0:T(8,128)} %get-tuple-element.46), channel_id=1, source_target_pairs={{0,1},{1,0},{2,3},{3,2},{4,5},{5,4},{6,7},{7,6},{8,9},{9,8},{10,11... | collective-permute-start | bytes 344072 | tf_op jit(solution)/shard_map/ppermute | solution.py:264
  92.6 15.5 %collective-permute-start.16 = (f32[16,1792]{1,0:T(8,128)}, f32[16,1792]{1,0:T(8,128)}, u32[]{:S(2)}, u32[]{:S(2)}) collective-permute-start(f32[16,1792]{1,0:T(8,128)} %get-tuple-element.45), channel_id=1, source_target_pairs={{0,1},{1,0},{2,3},{3,2},{4,5},{5,4},{6,7},{7,6},{8,9},{9,8},{10,11... | collective-permute-start | bytes 344072 | tf_op jit(solution)/shard_map/ppermute | solution.py:264
  (31 other events, 87.7 us)

commit v3 on v2

--- a/solution.py
+++ b/solution.py
@@ -1,5 +1,6 @@
 import jax
 import jax.numpy as jnp
+import numpy as np
 from jax import lax
 from jax.experimental import pallas as pl
 from jax.experimental.pallas import tpu as pltpu
@@ -10,6 +11,7 @@
 HIGHEST = lax.Precision.HIGHEST
 RANK = 16
 CHUNKS = 2
+MIB = 1024 * 1024
 
 
 def mm(a, b, ca=1, cb=0, precision=None):
@@ -18,21 +20,30 @@
     )
 
 
-def call(kernel, outs, args, scalars=None, flops=0):
-    size = sum(x.size * x.dtype.itemsize for x in args)
-    size += sum(o.size * o.dtype.itemsize for o in outs)
-    specs = [pl.BlockSpec(memory_space=pltpu.VMEM)] * len(args)
+def call(kernel, outs, args, scalars=None, after=(), scratch=(), spaces=None):
+    size = sum(x.size * x.dtype.itemsize for x in [*args, *outs])
+    total = size + sum(np.prod(x.shape) * x.dtype.itemsize for x in scratch if len(getattr(x, "shape", ())) > 1)
+    spaces = spaces or [pltpu.VMEM] * len(args)
+    specs = [pl.BlockSpec(memory_space=space) for space in spaces]
     if scalars is not None:
         args = [scalars, *args]
         specs = [pl.BlockSpec(memory_space=pltpu.SMEM), *specs]
+    used = len(args)
+
+    def body(*refs):
+        kernel(*refs[:used], *refs[used + len(after) :])
+
     return pl.pallas_call(
-        kernel,
+        body,
         out_shape=[jax.ShapeDtypeStruct(o.shape, o.dtype) for o in outs],
-        in_specs=specs,
+        in_specs=specs + [pl.BlockSpec(memory_space=pl.ANY)] * len(after),
         out_specs=[pl.BlockSpec(memory_space=pltpu.VMEM)] * len(outs),
-        compiler_params=pltpu.CompilerParams(vmem_limit_bytes=48 * 1024 * 1024),
-        cost_estimate=pl.CostEstimate(flops=flops, bytes_accessed=size, transcendentals=0),
-    )(*args)
+        scratch_shapes=list(scratch),
+        compiler_params=pltpu.CompilerParams(
+            vmem_limit_bytes=min(60 * MIB, int(8 * MIB + 1.5 * total))
+        ),
+        cost_estimate=pl.CostEstimate(flops=0, bytes_accessed=size, transcendentals=0),
+    )(*args, *after)
 
 
 def split(x):
@@ -44,21 +55,20 @@
     return pl.ds(pl.multiple_of(start, 128), size)
 
 
-def half_factor_kernel(where, a_out, out):
+def half_factor_kernel(where, a_out, out, sem):
     half = out.shape[1]
-    out[...] = a_out[:, lanes(where[2] * half, half)]
-
-
-def pack_tokens_kernel(where, cot, ids, gates, out, own):
+    copy = pltpu.make_async_copy(a_out.at[:, lanes(where[2] * half, half)], out, sem)
+    copy.start()
+    copy.wait()
+
+
+def pack_tokens_kernel(where, cot, ids, gates, out, own, sem):
     tokens, half = cot.shape[0], out.shape[1]
-    out[0:tokens, :] = cot[:, lanes((1 - where[1]) * half, half)]
-    diagonal = (
-        lax.broadcasted_iota(jnp.int32, (tokens, tokens), 0)
-        == lax.broadcasted_iota(jnp.int32, (tokens, tokens), 1)
-    ).astype(BF)
-    id_rows = mm(ids[...].astype(F32).astype(BF), diagonal, 0, 0)
-    gate_rows = mm(gates[...].astype(BF), diagonal, 0, 0)
+    far = lanes((1 - where[1]) * half, half)
+    copy = pltpu.make_async_copy(cot.at[:, far], out.at[0:tokens, :], sem)
+    copy.start()
     row = lax.broadcasted_iota(jnp.int32, (16, tokens), 0)
+    id_rows, gate_rows = ids[...].astype(F32), gates[...].astype(BF).astype(F32)
     meta = jnp.where(row == 0, id_rows[0:1], 0.0)
     meta = jnp.where(row == 1, id_rows[1:2], meta)
     meta = jnp.where(row == 2, gate_rows[0:1], meta)
@@ -66,27 +76,40 @@
     own[...] = meta
     out[tokens : tokens + 16, 0:tokens] = meta
     out[tokens : tokens + 16, tokens:] = jnp.zeros((16, half - tokens), BF)
-
-
-def low_rank_kernel(hidden, a_in, a_out, out):
-    slots = out.shape[2] // 2
-    low = mm(a_in[...], hidden[...], 1, 1).astype(BF)
+    copy.wait()
+
+
+def low_rank_kernel(hidden, a_in, a_out, low, stats_out, rows, sem):
+    copy = pltpu.make_async_copy(hidden, rows, sem)
+    copy.start()
     wide_in, wide_out = a_in[...].astype(F32), a_out[...].astype(F32)
     total_in = jnp.sum(jnp.sum(wide_in * wide_in, axis=1, keepdims=True), axis=0, keepdims=True)
     total_out = jnp.sum(jnp.sum(wide_out * wide_out, axis=1, keepdims=True), axis=0, keepdims=True)
-    row = lax.broadcasted_iota(jnp.int32, (RANK, slots), 0)
-    stats = jnp.zeros((RANK, slots), F32)
+    row = lax.broadcasted_iota(jnp.int32, stats_out.shape, 0)
+    stats = jnp.zeros(stats_out.shape, F32)
     for base, total in ((0, total_in), (3, total_out)):
-        rest = jnp.broadcast_to(total, (RANK, slots))
+        rest = jnp.broadcast_to(total, stats_out.shape)
         for piece in range(3):
             part = rest.astype(BF).astype(F32)
             stats = jnp.where(row == base + piece, part, stats)
             rest = rest - part
-    stats = stats.astype(BF)
+    stats_out[...] = stats.astype(BF)
+    copy.wait()
+    low[...] = mm(a_in[...], rows[...], 1, 1).astype(BF)
+
+
+def pack_low_kernel(low, stats, out):
+    slots = out.shape[2] // 2
     for device in range(out.shape[0]):
         chip = device // 2
         out[device, :, 0:slots] = low[:, chip * slots : (chip + 1) * slots]
-        out[device, :, slots:] = stats
+        out[device, :, slots:] = stats[...]
+
+
+def join_kernel(first, second, out):
+    rows = first.shape[0]
+    out[0:rows, :] = first[...]
+    out[rows:, :] = second[...]
 
 
 def fold_of(slots, experts, capacity, source):
@@ -136,12 +159,13 @@
         source = jnp.bitwise_xor(core, s)
         wide = mm(low, fold_of(slots, experts, capacity, source))
         wide = jnp.where(own, wide, 0.0).astype(BF)
-        z = mm(wide, weights).astype(BF)
+        exact = mm(wide, weights)
+        z = exact.astype(BF)
         rows.append(z.reshape(experts // 4, 2, 2 * RANK, tokens))
         if s == 0:
             w_out[...] = weights
-            for place_of, e in enumerate(order):
-                z_out[place_of * RANK : (place_of + 1) * RANK, :] = z[e * RANK : (e + 1) * RANK]
+            ordered = jnp.concatenate([exact[e * RANK : (e + 1) * RANK] for e in order], axis=0)
+            z_out[...] = ordered.T.astype(BF)
     count = experts * RANK // 2
     wide = half // CHUNKS
     for piece in range(CHUNKS):
@@ -167,39 +191,47 @@
     sent[...] = total[RANK:]
 
 
-def grad_low_kernel(order, where, cot, w, *refs):
-    factors, out = refs[:-1], refs[-1]
+def factor_kernel(order, where, cot, w, z, *refs):
+    count = len(order) * RANK
+    pieces = 8
+    factors, (coords_out, delta, tokens_in, table, sems) = refs[:pieces], refs[pieces:]
     me, side = where[0], where[2]
-    experts, _, slots = out.shape
+    experts, _, slots = coords_out.shape
     tokens, half = cot.shape[0], factors[0].shape[1]
     capacity = slots // 4
-    own_side = cot[:, lanes(side * half, half)]
-    far_side = cot[:, lanes((1 - side) * half, half)]
-    blocks = []
-    for near, far in zip(factors[0::2], factors[1::2]):
-        rows = mm(near[...], own_side, 1, 1) + mm(far[...], far_side, 1, 1)
-        blocks += [rows[r : r + RANK] for r in range(0, rows.shape[0], RANK)]
-    coords = jnp.concatenate([blocks[order.index(e)] for e in range(experts)], axis=0)
+    copies = [pltpu.make_async_copy(cot, tokens_in, sems.at[pieces])]
+    for flip in range(2):
+        start = 0
+        for i, factor in enumerate(factors[flip::2]):
+            size = factor.shape[0]
+            target = table.at[flip, start : start + size, :]
+            copies.append(pltpu.make_async_copy(factor, target, sems.at[4 * flip + i]))
+            start += size
+    for copy in copies:
+        copy.start()
+    for copy in copies[:5]:
+        copy.wait()
+    cut = half // 4
+    coords = jnp.zeros((count, tokens), F32)
+    for flip in range(2):
+        if flip == 1:
+            for copy in copies[5:]:
+                copy.wait()
+        base = jnp.bitwise_xor(side, flip) * half
+        for piece in range(4):
+            block = table[flip, :, piece * cut : (piece + 1) * cut]
+            here = lanes(base + piece * cut, cut)
+            delta[:, here] = mm(z[...], block).astype(BF)
+            coords = coords + mm(block, tokens_in[:, here], 1, 1)
+    blocks = [order.index(e) * RANK for e in range(experts)]
+    coords = jnp.concatenate([coords[b : b + RANK] for b in blocks], axis=0)
     high, low = split(coords)
     picked = mm(high, w[...], 1, 1) + mm(low, w[...], 1, 1)
     picked = jnp.where(own_expert(experts, capacity), picked, 0.0).astype(BF)
     fold = fold_of(slots, experts, capacity, lax.rem(me, 4))
-    rows = mm(picked, fold, 1, 1).astype(out.dtype)
+    rows = mm(picked, fold, 1, 1).astype(coords_out.dtype)
     for e in range(experts):
-        out[jnp.bitwise_xor(me, e)] = rows[e * RANK : (e + 1) * RANK]
-
-
-def delta_kernel(where, z, *refs):
-    factors, out = refs[:-1], refs[-1]
-    half = factors[0].shape[1]
-    for flip in range(2):
-        total, start = None, 0
-        for factor in factors[flip::2]:
-            part = mm(z[start : start + factor.shape[0], :], factor[...], 0, 0)
-            total = part if total is None else total + part
-            start += factor.shape[0]
-        side = jnp.bitwise_xor(where[2], flip)
-        out[:, lanes(side * half, half)] = total.astype(BF)
+        coords_out[jnp.bitwise_xor(me, e)] = rows[e * RANK : (e + 1) * RANK]
 
 
 def inverse_kernel(a_in, a_out, lows, inv_in, inv_out):
@@ -248,6 +280,13 @@
             out[:, lanes(base + piece * wide, wide)] = rows
 
 
+def relative_order(far_bits):
+    order = [0]
+    for bit in [2, *reversed(far_bits), 1]:
+        order = order + [e ^ bit for e in order]
+    return order
+
+
 def on_device(hidden_slots, adapter_in, adapter_out, expert_ids, gate_weights, cotangent):
     experts, groups = lax.axis_size("expert"), lax.axis_size("group")
     me, group = lax.axis_index("expert"), lax.axis_index("group")
@@ -275,42 +314,64 @@
         far_bits.append(bit)
         bit *= 2
 
-    (block,) = call(half_factor_kernel, [struct((RANK, half), BF)], [a_out], where)
-    order = [0]
-    for bit in [2, *reversed(far_bits)]:
-        received = swap(block, bit)
-        order = order + [e ^ bit for e in order]
-        if bit == far_bits[0]:
-            near = [block, received]
-        else:
-            block = jnp.concatenate([block, received], axis=0)
-    order = order + [e ^ 1 for e in order]
-
+    (block,) = call(
+        half_factor_kernel,
+        [struct((RANK, half), BF)],
+        [a_out],
+        where,
+        scratch=[pltpu.SemaphoreType.DMA],
+        spaces=[pl.ANY],
+    )
+    received = swap(block, 2)
     packed, own_meta = call(
         pack_tokens_kernel,
         [struct((tokens + 16, half), BF), struct((16, tokens), BF)],
-        [cotangent, expert_ids, gate_weights],
+        [cotangent, expert_ids.T, gate_weights.T],
         where,
+        scratch=[pltpu.SemaphoreType.DMA],
+        spaces=[pl.ANY, pltpu.VMEM, pltpu.VMEM],
     )
     packed = swap(packed, 1)
+    low, stats = call(
+        low_rank_kernel,
+        [struct((RANK, hidden.shape[0]), BF), struct((RANK, 2 * capacity), BF)],
+        [hidden, a_in, a_out],
+        scratch=[pltpu.VMEM(hidden.shape, BF), pltpu.SemaphoreType.DMA],
+        spaces=[pl.ANY, pltpu.VMEM, pltpu.VMEM],
+    )
+    (block,) = call(
+        join_kernel, [struct((2 * RANK, half), BF)], [block, received], after=[own_meta, low]
+    )
     (lows,) = call(
-        low_rank_kernel, [struct((experts, RANK, 4 * capacity), BF)], [hidden, a_in, a_out]
+        pack_low_kernel,
+        [struct((experts, RANK, 4 * capacity), BF)],
+        [low, stats],
+        after=[block],
     )
     lows = spread(lows)
     inv_in, inv_out = call(
         inverse_kernel, [struct((RANK, RANK), F32)] * 2, [a_in, a_out, lows]
     )
-
     count = experts * RANK // 2
+    full = relative_order(far_bits)
     z, weights, *parts = call(
-        lambda *refs: partial_kernel(order, *refs),
-        [struct((experts * RANK, tokens), BF), struct((experts * capacity, tokens), BF)]
+        lambda *refs: partial_kernel(full, *refs),
+        [struct((tokens, experts * RANK), BF), struct((experts * capacity, tokens), BF)]
         + [struct((count, wide), F32)] * CHUNKS
         + [struct((count, wide), BF)] * CHUNKS,
         [cotangent, packed, own_meta, lows],
         where,
     )
     kept, sent = parts[:CHUNKS], parts[CHUNKS:]
+    for bit in reversed(far_bits):
+        received = swap(block, bit)
+        if bit == far_bits[0]:
+            near = [block, received]
+        else:
+            shape = (2 * block.shape[0], half)
+            (block,) = call(
+                join_kernel, [struct(shape, BF)], [block, received], after=[sent[0]]
+            )
     own_rows, far_rows = [], []
     for piece in range(CHUNKS):
         keep, send, rows = kept[piece], sent[piece], count
@@ -330,14 +391,19 @@
     for block in near:
         factors += [block, swap_side(block)]
     factors = factors + [swap(block, 1) for block in factors]
-    (coords,) = call(
-        lambda *refs: grad_low_kernel(order, *refs),
-        [struct((experts, RANK, 4 * capacity), BF)],
-        [cotangent, weights, *factors],
+    coords, delta = call(
+        lambda *refs: factor_kernel(full, *refs),
+        [struct((experts, RANK, 4 * capacity), BF), struct((tokens, width), BF)],
+        [cotangent, weights, z, *factors],
         where,
+        scratch=[
+            pltpu.VMEM(cotangent.shape, BF),
+            pltpu.VMEM((2, experts * RANK, half), BF),
+            pltpu.SemaphoreType.DMA((9,)),
+        ],
+        spaces=[pl.ANY, pltpu.VMEM, pltpu.VMEM] + [pl.ANY] * 8,
     )
     coords = spread(coords)
-    (delta,) = call(delta_kernel, [struct((tokens, width), BF)], [z, *factors], where)
     (scaled_in,) = call(
         scaled_in_kernel, [struct((RANK, hidden.shape[1]), F32)], [coords, hidden, inv_out]
     )

time: 111 us -> 85.5 us (0.77)
  local copies, waits for them, and re-layouts: 21.4 us -> 4.75 us
  Pallas kernels: 21.2 us -> 15.7 us
  waiting for transfers between devices: 32.1 us -> 27.7 us
  starting transfers between devices: 20.1 us -> 23.7 us
  blocking collectives: 14.8 us -> 12.4 us
    unnamed x74 -> x18, local copies, waits for them, and re-layouts: 21.4 us -> 4.75 us
    ppermute x2, waiting for transfers between devices: 7.96 us -> 0.99 us  [swap_side(): return lax.ppermute(x, 'group', [(i, i ^ 1) for i in range(groups)])]
    pallas_call x15 -> x17, Pallas kernels: 21.2 us -> 15.7 us  [call(): pl.pallas_call(body, out_shape=[jax.ShapeDtypeStruct(o.shape, o.dtype) fo...]
    all_to_all x1, waiting for transfers between devices: 0.01 us -> 2.67 us  [spread(): return lax.all_to_all(x, 'expert', split_axis=0, concat_axis=0, tiled=True)]
    all_to_all x1, blocking collectives: 14.8 us -> 12.4 us  [spread(): return lax.all_to_all(x, 'expert', split_axis=0, concat_axis=0, tiled=True)]
    ppermute x16, starting transfers between devices: 13.9 us -> 16.2 us  [swap(): return lax.ppermute(x, 'expert', [(i, i ^ bit) for i in range(experts)])]
  transfers between devices with their start and end apart: 19 -> 19, of which waited for: 5 -> 6; matrix products, arithmetic and copies ran while one was open for 1% -> 0% of each run, Pallas kernels for 17% -> 16%
where the time goes in v3:
time: 85.5 us; the launch traced here: 85.2 us
  waiting for transfers between devices  27.7 us (32%)
  starting transfers between devices  23.7 us (28%)
  Pallas kernels  15.7 us (18%)
  blocking collectives  12.4 us (15%)
  local copies, waits for them, and re-layouts  4.75 us (6%)
    ppermute x16, waiting for transfers between devices, swap(): return lax.ppermute(x, 'expert', [(i, i ^ bit) for i in range(experts)])  24 us
    ppermute x16, starting transfers between devices, swap(): return lax.ppermute(x, 'expert', [(i, i ^ bit) for i in range(experts)])  16.2 us
    pallas_call x17, Pallas kernels, call(): pl.pallas_call(body, out_shape=[jax.ShapeDtypeStruct(o.shape, o.dtype) fo...  15.7 us
    all_to_all x1, blocking collectives, spread(): return lax.all_to_all(x, 'expert', split_axis=0, concat_axis=0, tiled=True)  12.4 us
    unnamed x18, local copies, waits for them, and re-layouts  4.75 us
    all_to_all x1, starting transfers between devices, spread(): return lax.all_to_all(x, 'expert', split_axis=0, concat_axis=0, tiled=True)  4.53 us
    ppermute x2, starting transfers between devices, swap_side(): return lax.ppermute(x, 'group', [(i, i ^ 1) for i in range(groups)])  2.99 us
    all_to_all x1, waiting for transfers between devices, spread(): return lax.all_to_all(x, 'expert', split_axis=0, concat_axis=0, tiled=True)  2.67 us
  transfers between devices with their start and end apart: 19, of which 6 were waited for; matrix products, arithmetic and copies ran while one was open for 0% of the time, Pallas kernels for 16%

profile of v3, /device:TPU:0, one launch (start us, length us, event | category | flops | bytes accessed | tf_op | source)
XLA Modules:
  0.0 85.2 jit_solution(5700569608724568907)
XLA Ops:
  0.7 1.5 %copy-done = bf16[128,7168]{1,0:T(8,128)(2,1)S(1)} copy-done((bf16[128,7168]{1,0:T(8,128)(2,1)S(1)}, bf16[128,7168]{1,0:T(8,128)(2,1)}, u32[]{:S(2)}) %copy-start) | copy-done | bytes 1835032
  6.3 2.6 %collective-permute-start.1 = (bf16[16,3584]{1,0:T(8,128)(2,1)S(1)}, bf16[16,3584]{1,0:T(8,128)(2,1)S(1)}, u32[]{:S(2)}, u32[]{:S(2)}) collective-permute-start(bf16[16,3584]{1,0:T(8,128)(2,1)S(1)} %shard_map.87.refs_0_), channel_id=1, source_target_pairs={{0,2},{1,3},{2,0},{3,1},{4,6},{5,7},{6,4},{7,5},{8,10},{9,11},{10,... | collective-permute-start | bytes 344072 | tf_op jit(solution)/shard_map/ppermute | solution.py:303
  8.9 0.9 %copy-done.4 = bf16[1,16,7168]{2,1,0:T(8,128)(2,1)S(1)} copy-done((bf16[1,16,7168]{2,1,0:T(8,128)(2,1)S(1)}, bf16[1,16,7168]{2,1,0:T(8,128)(2,1)}, u32[]{:S(2)}) %copy-start.4) | copy-done | bytes 229400
  9.9 1.0 %shard_map.86 = (bf16[16,512]{1,0:T(8,128)(2,1)S(1)}, bf16[16,64]{1,0:T(8,128)(2,1)S(1)}) custom-call(bf16[512,2048]{1,0:T(8,128)(2,1)S(1)} %bitcast.10, bf16[16,2048]{1,0:T(8,128)(2,1)S(1)} %bitcast.15, bf16[16,7168]{1,0:T(8,128)(2,1)S(1)} %bitcast.13), custom_call_target="tpu_custom_call" | custom-call | bytes 2410496 | tf_op jit(solution)/shard_map/pallas_call | solution.py:36
  10.9 1.9 %collective-permute-done.1.refs_1_ = bf16[16,3584]{1,0:T(8,128)(2,1)S(1)} collective-permute-done((bf16[16,3584]{1,0:T(8,128)(2,1)S(1)}, bf16[16,3584]{1,0:T(8,128)(2,1)S(1)}, u32[]{:S(2)}, u32[]{:S(2)}) %collective-permute-start.1) | collective-permute-done | bytes 114720 | tf_op jit(solution)/shard_map/ppermute | solution.py:303
  12.8 2.9 %collective-permute-start.2 = (bf16[32,3584]{1,0:T(8,128)(2,1)S(1)}, bf16[32,3584]{1,0:T(8,128)(2,1)S(1)}, u32[]{:S(2)}, u32[]{:S(2)}) collective-permute-start(bf16[32,3584]{1,0:T(8,128)(2,1)S(1)} %shard_map.88.refs_2_.refs_0_), channel_id=1, source_target_pairs={{0,8},{1,9},{2,10},{3,11},{4,12},{5,13},{6,14},{7,15},{8,0},{9,1},... | collective-permute-start | bytes 688136 | tf_op jit(solution)/shard_map/ppermute | solution.py:303
  15.8 12.4 %all_to_all.10.refs_4_.refs_2_ = bf16[16,16,128]{2,1,0:T(8,128)(2,1)S(1)} all-to-all(bf16[16,16,128]{2,1,0:T(8,128)(2,1)S(1)} %shard_map.89), channel_id=1, replica_groups=mesh['group'=2,'expert'=16] {'expert'}, dimensions={0} | all-to-all | bytes 131072 | tf_op jit(solution)/shard_map/all_to_all | solution.py:309
  28.2 2.2 %shard_map.90 = (bf16[128,256]{1,0:T(8,128)(2,1)S(1)}, bf16[512,128]{1,0:T(8,128)(2,1)S(1)}, f32[128,1792]{1,0:T(8,128)S(1)}, f32[128,1792]{1,0:T(8,128)S(1)}, b...) custom-call(s32[3]{0:T(128)S(1)} %pad_add_fusion.refs_0_, bf16[128,7168]{1,0:T(8,128)(2,1)S(1)} %copy-done.1, ...), custom_call_target="tpu_custom_call" | custom-call | bytes 5885952 | tf_op jit(solution)/shard_map/pallas_call | solution.py:36
  32.0 1.2 %collective-permute-start.10 = (bf16[128,1792]{1,0:T(8,128)(2,1)S(1)}, bf16[128,1792]{1,0:T(8,128)(2,1)S(1)}, u32[]{:S(2)}, u32[]{:S(2)}) collective-permute-start(bf16[128,1792]{1,0:T(8,128)(2,1)S(1)} %get-tuple-element.35.refs_2_), channel_id=1, source_target_pairs={{0,2},{1,3},{2,0},{3,1},{4,6},{5,7},{6,4},{7,5},{8,10},{9,11},{10,... | collective-permute-start | bytes 1376264 | tf_op jit(solution)/shard_map/ppermute | solution.py:303
  33.2 1.5 %collective-permute-start.3 = (bf16[64,3584]{1,0:T(8,128)(2,1)S(1)}, bf16[64,3584]{1,0:T(8,128)(2,1)S(1)}, u32[]{:S(2)}, u32[]{:S(2)}) collective-permute-start(bf16[64,3584]{1,0:T(8,128)(2,1)S(1)} %shard_map.91.refs_4_), channel_id=1, source_target_pairs={{0,16},{16,0},{1,17},{17,1},{2,18},{18,2},{3,19},{19,3},{4,20},{20... | collective-permute-start | bytes 1376264 | tf_op jit(solution)/shard_map/ppermute | solution.py:306
  34.7 8.4 %collective-permute-done.4.refs_6_ = bf16[64,3584]{1,0:T(8,128)(2,1)S(1)} collective-permute-done((bf16[64,3584]{1,0:T(8,128)(2,1)S(1)}, bf16[64,3584]{1,0:T(8,128)(2,1)S(1)}, u32[]{:S(2)}, u32[]{:S(2)}) %collective-permute-start.4) | collective-permute-done | bytes 458784 | tf_op jit(solution)/shard_map/ppermute | solution.py:303
  43.1 1.5 %collective-permute-start.5 = (bf16[64,3584]{1,0:T(8,128)(2,1)S(1)}, bf16[64,3584]{1,0:T(8,128)(2,1)S(1)}, u32[]{:S(2)}, u32[]{:S(2)}) collective-permute-start(bf16[64,3584]{1,0:T(8,128)(2,1)S(1)} %collective-permute-done.4.refs_6_), channel_id=1, source_target_pairs={{0,16},{16,0},{1,17},{17,1},{2,18},{18,2},{3,19},{19,3},{4,20},{20... | collective-permute-start | bytes 1376264 | tf_op jit(solution)/shard_map/ppermute | solution.py:306
  44.7 1.4 %collective-permute-start.14 = (bf16[64,1792]{1,0:T(8,128)(2,1)S(1)}, bf16[64,1792]{1,0:T(8,128)(2,1)S(1)}, u32[]{:S(2)}, u32[]{:S(2)}) collective-permute-start(bf16[64,1792]{1,0:T(8,128)(2,1)S(1)} %get-tuple-element.49), channel_id=1, source_target_pairs={{0,4},{1,5},{2,6},{3,7},{4,0},{5,1},{6,2},{7,3},{8,12},{9,13},{10,... | collective-permute-start | bytes 688136 | tf_op jit(solution)/shard_map/ppermute | solution.py:303
  46.1 7.1 %collective-permute-done.10.refs_1_ = bf16[128,1792]{1,0:T(8,128)(2,1)S(1)} collective-permute-done((bf16[128,1792]{1,0:T(8,128)(2,1)S(1)}, bf16[128,1792]{1,0:T(8,128)(2,1)S(1)}, u32[]{:S(2)}, u32[]{:S(2)}) %collective-permute-start.10) | collective-permute-done | bytes 458784 | tf_op jit(solution)/shard_map/ppermute | solution.py:303
  53.8 1.0 %collective-permute-done.5.refs_7_ = bf16[64,3584]{1,0:T(8,128)(2,1)S(1)} collective-permute-done((bf16[64,3584]{1,0:T(8,128)(2,1)S(1)}, bf16[64,3584]{1,0:T(8,128)(2,1)S(1)}, u32[]{:S(2)}, u32[]{:S(2)}) %collective-permute-start.5) | collective-permute-done | bytes 458784 | tf_op jit(solution)/shard_map/ppermute | solution.py:306
  54.9 1.4 %collective-permute-start.11 = (bf16[64,1792]{1,0:T(8,128)(2,1)S(1)}, bf16[64,1792]{1,0:T(8,128)(2,1)S(1)}, u32[]{:S(2)}, u32[]{:S(2)}) collective-permute-start(bf16[64,1792]{1,0:T(8,128)(2,1)S(1)} %get-tuple-element.42), channel_id=1, source_target_pairs={{0,4},{1,5},{2,6},{3,7},{4,0},{5,1},{6,2},{7,3},{8,12},{9,13},{10,... | collective-permute-start | bytes 688136 | tf_op jit(solution)/shard_map/ppermute | solution.py:303
  56.4 6.6 %collective-permute-done.11.refs_1_ = bf16[64,1792]{1,0:T(8,128)(2,1)S(1)} collective-permute-done((bf16[64,1792]{1,0:T(8,128)(2,1)S(1)}, bf16[64,1792]{1,0:T(8,128)(2,1)S(1)}, u32[]{:S(2)}, u32[]{:S(2)}) %collective-permute-start.11) | collective-permute-done | bytes 229408 | tf_op jit(solution)/shard_map/ppermute | solution.py:303
  63.0 3.4 %collective-permute-start.15 = (bf16[32,1792]{1,0:T(8,128)(2,1)S(1)}, bf16[32,1792]{1,0:T(8,128)(2,1)S(1)}, u32[]{:S(2)}, u32[]{:S(2)}) collective-permute-start(bf16[32,1792]{1,0:T(8,128)(2,1)S(1)} %get-tuple-element.51), channel_id=1, source_target_pairs={{0,8},{1,9},{2,10},{3,11},{4,12},{5,13},{6,14},{7,15},{8,0},{9,1},... | collective-permute-start | bytes 344072 | tf_op jit(solution)/shard_map/ppermute | solution.py:303
  66.5 6.0 %shard_map.92 = (bf16[16,16,128]{2,1,0:T(8,128)(2,1)}, bf16[128,7168]{1,0:T(8,128)(2,1)}) custom-call(s32[3]{0:T(128)S(1)} %pad_add_fusion.refs_0_, bf16[128,7168]{1,0:T(8,128)(2,1)S(1)} %copy-done.1, bf16[512,128]{1,0:T(8,128)(2,1)S(1)} %get-tuple-element.33.refs_2_, bf16[128,256]{1,0:T(8,128)(2,1)S(1)} %get-tuple-element.34.refs_3_, ...), custom_call_target="tpu_custom_call" | custom-call | bytes 7602176 | tf_op jit(solution)/shard_map/pallas_call | solution.py:36
  72.5 4.5 %all-to-all-start.1 = ((bf16[16,16,128]{2,1,0:T(8,128)(2,1)}), bf16[16,16,128]{2,1,0:T(8,128)(2,1)S(1)}, u32[]{:S(2)}, u32[]{:S(2)}) async-start(bf16[16,16,128]{2,1,0:T(8,128)(2,1)} %get-tuple-element.37), calls=%async_computation.1 | async-start | bytes 131072 | tf_op jit(solution)/shard_map/all_to_all | solution.py:309
  77.8 1.5 %shard_map.93 = (f32[16,16]{1,0:T(8,128)S(1)}, f32[16,16]{1,0:T(8,128)S(1)}) custom-call(bf16[16,2048]{1,0:T(8,128)(2,1)S(1)} %bitcast.16, bf16[16,7168]{1,0:T(8,128)(2,1)S(1)} %bitcast.14, bf16[16,16,128]{2,1,0:T(8,128)(2,1)S(1)} %all_to_all.10.refs_4_.refs_2_), custom_call_target="tpu_custom_call" | custom-call | bytes 362496 | tf_op jit(solution)/shard_map/pallas_call | solution.py:36
  79.4 1.9 %shard_map.101 = f32[16,7168]{1,0:T(8,128)} custom-call(s32[3]{0:T(128)S(1)} %pad_add_fusion.refs_0_, f32[16,16]{1,0:T(8,128)S(1)} %get-tuple-element.39.refs_1_, f32[16,1792]{1,0:T(8,128)S(1)} %get-tuple-element.45.refs_2_, f32[16,1792]{1,0:T(8,128)S(1)} %get-tuple-element.52.refs_3_, f32[16,1792]{1,0:T(8,128)S(1)} %collective-permute-done.16.refs_4_, ...), custom_call_target="tpu_custom_call" | custom-call | bytes 918528 | tf_op jit(solution)/shard_map/pallas_call | solution.py:36
  81.3 2.7 %all-to-all-done.1.refs_0_ = bf16[16,16,128]{2,1,0:T(8,128)(2,1)S(1)} async-done(((bf16[16,16,128]{2,1,0:T(8,128)(2,1)}), bf16[16,16,128]{2,1,0:T(8,128)(2,1)S(1)}, u32[]{:S(2)}, u32[]{:S(2)}) %all-to-all-start.1) | async-done | bytes 65568 | tf_op jit(solution)/shard_map/all_to_all | solution.py:309
  84.0 1.2 %shard_map.94 = f32[16,2048]{1,0:T(8,128)} custom-call(bf16[16,16,128]{2,1,0:T(8,128)(2,1)S(1)} %all-to-all-done.1.refs_0_, bf16[512,2048]{1,0:T(8,128)(2,1)S(1)} %bitcast.11, f32[16,16]{1,0:T(8,128)S(1)} %get-tuple-element.38.refs_2_), custom_call_target="tpu_custom_call" | custom-call | bytes 2294784 | tf_op jit(solution)/shard_map/pallas_call | solution.py:36
  (51 shorter events, 7.6 us)
Async XLA Ops:
  0.6 8.3 %copy-start.6 = (bf16[1,16,2048]{2,1,0:T(8,128)(2,1)S(1)}, bf16[1,16,2048]{2,1,0:T(8,128)(2,1)}, u32[]{:S(2)}) copy-start(bf16[1,16,2048]{2,1,0:T(8,128)(2,1)} %param.7) | copy-start | bytes 196612
  0.7 1.5 %copy-start = (bf16[128,7168]{1,0:T(8,128)(2,1)S(1)}, bf16[128,7168]{1,0:T(8,128)(2,1)}, u32[]{:S(2)}) copy-start(bf16[128,7168]{1,0:T(8,128)(2,1)} %refs_1_.5) | copy-start | bytes 5505028
  3.6 5.3 %copy-start.2 = (bf16[1,512,2048]{2,1,0:T(8,128)(2,1)S(1)}, bf16[1,512,2048]{2,1,0:T(8,128)(2,1)}, u32[]{:S(2)}) copy-start(bf16[1,512,2048]{2,1,0:T(8,128)(2,1)} %param.6) | copy-start | bytes 6291460
  4.2 23.9 %collective-permute-start = (bf16[144,3584]{1,0:T(8,128)(2,1)S(1)}, bf16[144,3584]{1,0:T(8,128)(2,1)S(1)}, u32[]{:S(2)}, u32[]{:S(2)}) collective-permute-start(bf16[144,3584]{1,0:T(8,128)(2,1)S(1)} %get-tuple-element.29), channel_id=1, source_target_pairs={{0,1},{1,0},{2,3},{3,2},{4,5},{5,4},{6,7},{7,6},{8,9},{9,8},{10,11... | collective-permute-start | bytes 3096584 | tf_op jit(solution)/shard_map/ppermute | solution.py:303
  5.7 22.5 %copy-start.1 = (bf16[128,7168]{1,0:T(8,128)(2,1)S(1)}, bf16[128,7168]{1,0:T(8,128)(2,1)}, u32[]{:S(2)}) copy-start(bf16[128,7168]{1,0:T(8,128)(2,1)} %refs_1_.5) | copy-start | bytes 5505028
  6.3 6.4 %collective-permute-start.1 = (bf16[16,3584]{1,0:T(8,128)(2,1)S(1)}, bf16[16,3584]{1,0:T(8,128)(2,1)S(1)}, u32[]{:S(2)}, u32[]{:S(2)}) collective-permute-start(bf16[16,3584]{1,0:T(8,128)(2,1)S(1)} %shard_map.87.refs_0_), channel_id=1, source_target_pairs={{0,2},{1,3},{2,0},{3,1},{4,6},{5,7},{6,4},{7,5},{8,10},{9,11},{10,... | collective-permute-start | bytes 344072 | tf_op jit(solution)/shard_map/ppermute | solution.py:303
  12.8 17.6 %collective-permute-start.2 = (bf16[32,3584]{1,0:T(8,128)(2,1)S(1)}, bf16[32,3584]{1,0:T(8,128)(2,1)S(1)}, u32[]{:S(2)}, u32[]{:S(2)}) collective-permute-start(bf16[32,3584]{1,0:T(8,128)(2,1)S(1)} %shard_map.88.refs_2_.refs_0_), channel_id=1, source_target_pairs={{0,8},{1,9},{2,10},{3,11},{4,12},{5,13},{6,14},{7,15},{8,0},{9,1},... | collective-permute-start | bytes 688136 | tf_op jit(solution)/shard_map/ppermute | solution.py:303
  30.4 12.6 %collective-permute-start.4 = (bf16[64,3584]{1,0:T(8,128)(2,1)S(1)}, bf16[64,3584]{1,0:T(8,128)(2,1)S(1)}, u32[]{:S(2)}, u32[]{:S(2)}) collective-permute-start(bf16[64,3584]{1,0:T(8,128)(2,1)S(1)} %shard_map.91.refs_4_), channel_id=1, source_target_pairs={{0,4},{1,5},{2,6},{3,7},{4,0},{5,1},{6,2},{7,3},{8,12},{9,13},{10,... | collective-permute-start | bytes 1376264 | tf_op jit(solution)/shard_map/ppermute | solution.py:303
  31.2 13.4 %collective-permute-start.13 = (bf16[128,1792]{1,0:T(8,128)(2,1)S(1)}, bf16[128,1792]{1,0:T(8,128)(2,1)S(1)}, u32[]{:S(2)}, u32[]{:S(2)}) collective-permute-start(bf16[128,1792]{1,0:T(8,128)(2,1)S(1)} %get-tuple-element.47), channel_id=1, source_target_pairs={{0,2},{1,3},{2,0},{3,1},{4,6},{5,7},{6,4},{7,5},{8,10},{9,11},{10,... | collective-permute-start | bytes 1376264 | tf_op jit(solution)/shard_map/ppermute | solution.py:303
  32.0 21.2 %collective-permute-start.10 = (bf16[128,1792]{1,0:T(8,128)(2,1)S(1)}, bf16[128,1792]{1,0:T(8,128)(2,1)S(1)}, u32[]{:S(2)}, u32[]{:S(2)}) collective-permute-start(bf16[128,1792]{1,0:T(8,128)(2,1)S(1)} %get-tuple-element.35.refs_2_), channel_id=1, source_target_pairs={{0,2},{1,3},{2,0},{3,1},{4,6},{5,7},{6,4},{7,5},{8,10},{9,11},{10,... | collective-permute-start | bytes 1376264 | tf_op jit(solution)/shard_map/ppermute | solution.py:303
  33.2 20.1 %collective-permute-start.3 = (bf16[64,3584]{1,0:T(8,128)(2,1)S(1)}, bf16[64,3584]{1,0:T(8,128)(2,1)S(1)}, u32[]{:S(2)}, u32[]{:S(2)}) collective-permute-start(bf16[64,3584]{1,0:T(8,128)(2,1)S(1)} %shard_map.91.refs_4_), channel_id=1, source_target_pairs={{0,16},{16,0},{1,17},{17,1},{2,18},{18,2},{3,19},{19,3},{4,20},{20... | collective-permute-start | bytes 1376264 | tf_op jit(solution)/shard_map/ppermute | solution.py:306
  43.1 11.7 %collective-permute-start.5 = (bf16[64,3584]{1,0:T(8,128)(2,1)S(1)}, bf16[64,3584]{1,0:T(8,128)(2,1)S(1)}, u32[]{:S(2)}, u32[]{:S(2)}) collective-permute-start(bf16[64,3584]{1,0:T(8,128)(2,1)S(1)} %collective-permute-done.4.refs_6_), channel_id=1, source_target_pairs={{0,16},{16,0},{1,17},{17,1},{2,18},{18,2},{3,19},{19,3},{4,20},{20... | collective-permute-start | bytes 1376264 | tf_op jit(solution)/shard_map/ppermute | solution.py:306
  44.7 10.2 %collective-permute-start.14 = (bf16[64,1792]{1,0:T(8,128)(2,1)S(1)}, bf16[64,1792]{1,0:T(8,128)(2,1)S(1)}, u32[]{:S(2)}, u32[]{:S(2)}) collective-permute-start(bf16[64,1792]{1,0:T(8,128)(2,1)S(1)} %get-tuple-element.49), channel_id=1, source_target_pairs={{0,4},{1,5},{2,6},{3,7},{4,0},{5,1},{6,2},{7,3},{8,12},{9,13},{10,... | collective-permute-start | bytes 688136 | tf_op jit(solution)/shard_map/ppermute | solution.py:303
  46.1 20.3 %collective-permute-start.6 = (bf16[64,3584]{1,0:T(8,128)(2,1)S(1)}, bf16[64,3584]{1,0:T(8,128)(2,1)S(1)}, u32[]{:S(2)}, u32[]{:S(2)}) collective-permute-start(bf16[64,3584]{1,0:T(8,128)(2,1)S(1)} %shard_map.91.refs_4_), channel_id=1, source_target_pairs={{0,1},{1,0},{2,3},{3,2},{4,5},{5,4},{6,7},{7,6},{8,9},{9,8},{10,11... | collective-permute-start | bytes 1376264 | tf_op jit(solution)/shard_map/ppermute | solution.py:303
  53.3 13.2 %collective-permute-start.8 = (bf16[64,3584]{1,0:T(8,128)(2,1)S(1)}, bf16[64,3584]{1,0:T(8,128)(2,1)S(1)}, u32[]{:S(2)}, u32[]{:S(2)}) collective-permute-start(bf16[64,3584]{1,0:T(8,128)(2,1)S(1)} %collective-permute-done.4.refs_6_), channel_id=1, source_target_pairs={{0,1},{1,0},{2,3},{3,2},{4,5},{5,4},{6,7},{7,6},{8,9},{9,8},{10,11... | collective-permute-start | bytes 1376264 | tf_op jit(solution)/shard_map/ppermute | solution.py:303
  53.3 13.2 %collective-permute-start.7 = (bf16[64,3584]{1,0:T(8,128)(2,1)S(1)}, bf16[64,3584]{1,0:T(8,128)(2,1)S(1)}, u32[]{:S(2)}, u32[]{:S(2)}) collective-permute-start(bf16[64,3584]{1,0:T(8,128)(2,1)S(1)} %collective-permute-done.3.refs_5_), channel_id=1, source_target_pairs={{0,1},{1,0},{2,3},{3,2},{4,5},{5,4},{6,7},{7,6},{8,9},{9,8},{10,11... | collective-permute-start | bytes 1376264 | tf_op jit(solution)/shard_map/ppermute | solution.py:303
  54.8 11.7 %collective-permute-start.9 = (bf16[64,3584]{1,0:T(8,128)(2,1)S(1)}, bf16[64,3584]{1,0:T(8,128)(2,1)S(1)}, u32[]{:S(2)}, u32[]{:S(2)}) collective-permute-start(bf16[64,3584]{1,0:T(8,128)(2,1)S(1)} %collective-permute-done.5.refs_7_), channel_id=1, source_target_pairs={{0,1},{1,0},{2,3},{3,2},{4,5},{5,4},{6,7},{7,6},{8,9},{9,8},{10,11... | collective-permute-start | bytes 1376264 | tf_op jit(solution)/shard_map/ppermute | solution.py:303
  54.9 8.1 %collective-permute-start.11 = (bf16[64,1792]{1,0:T(8,128)(2,1)S(1)}, bf16[64,1792]{1,0:T(8,128)(2,1)S(1)}, u32[]{:S(2)}, u32[]{:S(2)}) collective-permute-start(bf16[64,1792]{1,0:T(8,128)(2,1)S(1)} %get-tuple-element.42), channel_id=1, source_target_pairs={{0,4},{1,5},{2,6},{3,7},{4,0},{5,1},{6,2},{7,3},{8,12},{9,13},{10,... | collective-permute-start | bytes 688136 | tf_op jit(solution)/shard_map/ppermute | solution.py:303
  63.0 14.1 %collective-permute-start.15 = (bf16[32,1792]{1,0:T(8,128)(2,1)S(1)}, bf16[32,1792]{1,0:T(8,128)(2,1)S(1)}, u32[]{:S(2)}, u32[]{:S(2)}) collective-permute-start(bf16[32,1792]{1,0:T(8,128)(2,1)S(1)} %get-tuple-element.51), channel_id=1, source_target_pairs={{0,8},{1,9},{2,10},{3,11},{4,12},{5,13},{6,14},{7,15},{8,0},{9,1},... | collective-permute-start | bytes 344072 | tf_op jit(solution)/shard_map/ppermute | solution.py:303
  66.4 11.2 %collective-permute-start.12 = (bf16[32,1792]{1,0:T(8,128)(2,1)S(1)}, bf16[32,1792]{1,0:T(8,128)(2,1)S(1)}, u32[]{:S(2)}, u32[]{:S(2)}) collective-permute-start(bf16[32,1792]{1,0:T(8,128)(2,1)S(1)} %get-tuple-element.44), channel_id=1, source_target_pairs={{0,8},{1,9},{2,10},{3,11},{4,12},{5,13},{6,14},{7,15},{8,0},{9,1},... | collective-permute-start | bytes 344072 | tf_op jit(solution)/shard_map/ppermute | solution.py:303
  66.5 11.3 %copy-start.5 = (bf16[1,16,7168]{2,1,0:T(8,128)(2,1)S(1)}, bf16[1,16,7168]{2,1,0:T(8,128)(2,1)}, u32[]{:S(2)}) copy-start(bf16[1,16,7168]{2,1,0:T(8,128)(2,1)} %param.8) | copy-start | bytes 688132
  72.5 11.4 %all-to-all-start.1 = ((bf16[16,16,128]{2,1,0:T(8,128)(2,1)}), bf16[16,16,128]{2,1,0:T(8,128)(2,1)S(1)}, u32[]{:S(2)}, u32[]{:S(2)}) async-start(bf16[16,16,128]{2,1,0:T(8,128)(2,1)} %get-tuple-element.37), calls=%async_computation.1 | async-start | bytes 131072 | tf_op jit(solution)/shard_map/all_to_all | solution.py:309
  77.1 2.2 %collective-permute-start.17 = (f32[16,1792]{1,0:T(8,128)S(1)}, f32[16,1792]{1,0:T(8,128)S(1)}, u32[]{:S(2)}, u32[]{:S(2)}) collective-permute-start(f32[16,1792]{1,0:T(8,128)S(1)} %get-tuple-element.54), channel_id=1, source_target_pairs={{0,1},{1,0},{2,3},{3,2},{4,5},{5,4},{6,7},{7,6},{8,9},{9,8},{10,11... | collective-permute-start | bytes 344072 | tf_op jit(solution)/shard_map/ppermute | solution.py:303
  77.6 1.7 %collective-permute-start.16 = (f32[16,1792]{1,0:T(8,128)S(1)}, f32[16,1792]{1,0:T(8,128)S(1)}, u32[]{:S(2)}, u32[]{:S(2)}) collective-permute-start(f32[16,1792]{1,0:T(8,128)S(1)} %get-tuple-element.53), channel_id=1, source_target_pairs={{0,1},{1,0},{2,3},{3,2},{4,5},{5,4},{6,7},{7,6},{8,9},{9,8},{10,11... | collective-permute-start | bytes 344072 | tf_op jit(solution)/shard_map/ppermute | solution.py:303
  (4 other events, 3.2 us)

commit v4 on v3

v4 whole, which is shorter than its diff:
```python
import jax
import jax.numpy as jnp
import numpy as np
from jax import lax
from jax.experimental import pallas as pl
from jax.experimental.pallas import tpu as pltpu
from jax.sharding import PartitionSpec as P

BF = jnp.bfloat16
F32 = jnp.float32
HIGHEST = lax.Precision.HIGHEST
RANK = 16
CHUNKS = 2
HBM = pltpu.HBM
VMEM = pltpu.VMEM
DMA = pltpu.SemaphoreType.DMA
MIB = 1024 * 1024


def mm(a, b, ca=1, cb=0, precision=None):
    return lax.dot_general(
        a, b, (((ca,), (cb,)), ((), ())), preferred_element_type=F32, precision=precision
    )


def call(
    kernel, outs, args, scalars=None, after=(), scratch=(), spaces=None, out_spaces=None, alias=None, limit=None
):
    size = sum(x.size * x.dtype.itemsize for x in [*args, *outs])
    total = size + sum(
        np.prod(x.shape) * x.dtype.itemsize for x in scratch if len(getattr(x, "shape", ())) > 1
    )
    specs = [pl.BlockSpec(memory_space=space) for space in spaces or [VMEM] * len(args)]
    out_spaces = out_spaces or [VMEM] * len(outs)
    if scalars is not None:
        args = [scalars, *args]
        specs = [pl.BlockSpec(memory_space=pltpu.SMEM), *specs]
    used = len(args)

    def body(*refs):
        kernel(*refs[:used], *refs[used + len(after) :])

    return pl.pallas_call(
        body,
        out_shape=[jax.ShapeDtypeStruct(o.shape, o.dtype) for o in outs],
        in_specs=specs + [pl.BlockSpec(memory_space=pl.ANY)] * len(after),
        out_specs=[pl.BlockSpec(memory_space=space) for space in out_spaces],
        scratch_shapes=list(scratch),
        input_output_aliases=alias or {},
        compiler_params=pltpu.CompilerParams(
            vmem_limit_bytes=limit or min(60 * MIB, int(8 * MIB + 1.5 * total))
        ),
        cost_estimate=pl.CostEstimate(flops=0, bytes_accessed=size, transcendentals=0),
    )(*args, *after)


def split(x):
    high = x.astype(BF)
    return high, (x - high.astype(F32)).astype(BF)


def lanes(start, size):
    return pl.ds(pl.multiple_of(start, 128), size)


def low_rank_kernel(hidden, a_in, a_out, low_out, stats_out, hidden_in, a_in_in, a_out_in, sems):
    slots = stats_out.shape[1]
    pieces = 4
    rows = hidden.shape[0] // pieces
    copies = [
        pltpu.make_async_copy(a_in, a_in_in, sems.at[pieces]),
        pltpu.make_async_copy(a_out, a_out_in, sems.at[pieces + 1]),
    ]
    for i in range(pieces):
        part = pl.ds(i * rows, rows)
        copies.append(pltpu.make_async_copy(hidden.at[part], hidden_in.at[part], sems.at[i]))
    for copy in copies:
        copy.start()
    copies[0].wait()
    copies[1].wait()
    row = lax.broadcasted_iota(jnp.int32, (RANK, slots), 0)
    stats = jnp.zeros((RANK, slots), F32)
    for base, factor in ((0, a_in_in), (3, a_out_in)):
        square = jnp.square(factor[...].astype(F32))
        rest = jnp.sum(jnp.sum(square, axis=1, keepdims=True), axis=0, keepdims=True)
        rest = jnp.broadcast_to(rest, (RANK, slots))
        for piece in range(3):
            part = rest.astype(BF).astype(F32)
            stats = jnp.where(row == base + piece, part, stats)
            rest = rest - part
    stats_out[...] = stats.astype(BF)
    for i in range(pieces):
        copies[2 + i].wait()
        part = slice(i * rows, (i + 1) * rows)
        low_out[:, part] = mm(a_in_in[...], hidden_in[part, :], 1, 1).astype(BF)


def pack_low_kernel(low, stats, out):
    slots = out.shape[2] // 2
    for device in range(out.shape[0]):
        chip = device // 2
        out[device, :, 0:slots] = low[:, chip * slots : (chip + 1) * slots]
        out[device, :, slots:] = stats[...]


def join_kernel(*refs):
    pieces, out = refs[:-1], refs[-1]
    start = 0
    for piece in pieces:
        out[start : start + piece.shape[0], :] = piece[...]
        start += piece.shape[0]


def fold_of(slots, experts, capacity, source):
    column = lax.broadcasted_iota(jnp.int32, (slots, experts * capacity), 1)
    row = lax.broadcasted_iota(jnp.int32, (slots, experts * capacity), 0)
    return (row == source * capacity + lax.rem(column, capacity)).astype(BF)


def own_expert(experts, capacity):
    shape = (experts * RANK, experts * capacity)
    row = lax.div(lax.broadcasted_iota(jnp.int32, shape, 0), RANK)
    column = lax.div(lax.broadcasted_iota(jnp.int32, shape, 1), capacity)
    return row == column


def relative_experts(order_size, tokens, me):
    row = lax.broadcasted_iota(jnp.int32, (order_size, tokens), 0)
    return jnp.bitwise_xor(row, me).astype(F32)


def partial_kernel(order, where, cot, packed, own_meta, far_meta, lows, z_out, w_out, *outs):
    keeps, sends = outs[:CHUNKS], outs[CHUNKS : 2 * CHUNKS]
    own_in, sem = outs[2 * CHUNKS :]
    me, core = where[0], where[1]
    experts, tokens = lows.shape[0], cot.shape[0]
    slots = lows.shape[2] // 2
    capacity = slots // 2
    half = packed.shape[1]
    copy = pltpu.make_async_copy(cot.at[:, lanes(core * half, half)], own_in, sem)
    copy.start()
    low = jnp.concatenate(
        [lows[jnp.bitwise_xor(me, e)][:, 0:slots] for e in range(experts)], axis=0
    )
    own = own_expert(experts, capacity)
    expert = relative_experts(experts, tokens, me)
    earlier = (
        lax.broadcasted_iota(jnp.int32, (tokens, tokens), 0)
        < lax.broadcasted_iota(jnp.int32, (tokens, tokens), 1)
    ).astype(BF)
    place = lax.broadcasted_iota(jnp.int32, (experts, capacity, tokens), 1).astype(F32)
    rows = []
    for s in range(2):
        meta = (own_meta if s == 0 else far_meta)[...].astype(F32)
        first = (meta[0:1] == expert).astype(F32)
        second = (meta[1:2] == expert).astype(F32)
        before = mm((first + second).astype(BF), earlier)
        gate = first * meta[2:3] + second * meta[3:4]
        spread = jnp.where(before[:, None, :] == place, gate[:, None, :], 0.0)
        weights = spread.reshape(experts * capacity, tokens).astype(BF)
        source = jnp.bitwise_xor(core, s)
        wide = mm(low, fold_of(slots, experts, capacity, source))
        wide = jnp.where(own, wide, 0.0).astype(BF)
        exact = mm(wide, weights)
        z = exact.astype(BF)
        rows.append(z.reshape(experts // 4, 2, 2 * RANK, tokens))
        if s == 0:
            w_out[...] = weights
            ordered = jnp.concatenate([exact[e * RANK : (e + 1) * RANK] for e in order], axis=0)
            z_out[...] = ordered.T.astype(BF)
    count = experts * RANK // 2
    copy.wait()
    base = 0
    for keep, send in zip(keeps, sends):
        here = slice(base, base + keep.shape[1])
        base += keep.shape[1]
        for side, target in ((0, keep), (1, send)):
            first = rows[0][:, side].reshape(count, tokens)
            second = rows[1][:, side].reshape(count, tokens)
            total = mm(first, own_in[:, here]) + mm(second, packed[:, here])
            target[...] = total.astype(target.dtype)


def fold_step_kernel(received, keep, *refs):
    sends, kept = refs[received:-1], refs[-1]
    rows, width = keep.shape
    radix = 1 + len(sends)
    total = keep[...]
    for more in refs[:received]:
        total = total + more[...].astype(F32)
    total = total.reshape(rows // (2 * RANK * radix), radix, 2 * RANK, width)
    kept[...] = total[:, 0].reshape(kept.shape)
    for i, send in enumerate(sends):
        send[...] = total[:, i + 1].reshape(send.shape).astype(send.dtype)


def last_fold_kernel(keep, *refs):
    received, (kept, sent) = refs[:-2], refs[-2:]
    total = keep[...]
    for more in received:
        total = total + more[...].astype(F32)
    kept[...] = total[0:RANK]
    sent[...] = total[RANK:]


def factor_half(flip, side, cot, z, factors, delta, scratch):
    tokens_in, table, result, sems = scratch
    tokens, half = tokens_in.shape
    lane = lanes(jnp.bitwise_xor(side, flip) * half, half)
    copies = [pltpu.make_async_copy(cot.at[:, lane], tokens_in, sems.at[len(factors)])]
    start = 0
    for i, factor in enumerate(factors):
        size = factor.shape[0]
        target = table.at[start : start + size, :]
        copies.append(pltpu.make_async_copy(factor, target, sems.at[i]))
        start += size
    for copy in copies:
        copy.start()
    for copy in copies:
        copy.wait()
    cut = half // 4
    coords = jnp.zeros((start, tokens), F32)
    copies = []
    for piece in range(4):
        here = slice(piece * cut, (piece + 1) * cut)
        result[:, here] = mm(z[...], table[:, here]).astype(BF)
        target = delta.at[:, lanes(jnp.bitwise_xor(side, flip) * half + piece * cut, cut)]
        copies.append(pltpu.make_async_copy(result.at[:, here], target, sems.at[piece]))
        copies[-1].start()
        coords = coords + mm(table[:, here], tokens_in[:, here], 1, 1)
    return coords, copies


def near_kernel(where, cot, z, *refs):
    factors, (coords_out, delta), scratch = refs[:-6], refs[-6:-4], refs[-4:]
    coords_out[...], copies = factor_half(0, where[2], cot, z, factors, delta, scratch)
    for copy in copies:
        copy.wait()


def far_kernel(order, where, cot, z, w, near, _, *refs):
    factors, (coords_out, delta), scratch = refs[:-6], refs[-6:-4], refs[-4:]
    experts, _, slots = coords_out.shape
    capacity = slots // 4
    coords, copies = factor_half(1, where[2], cot, z, factors, delta, scratch)
    coords = coords + near[...]
    blocks = [order.index(e) * RANK for e in range(experts)]
    coords = jnp.concatenate([coords[b : b + RANK] for b in blocks], axis=0)
    high, low = split(coords)
    picked = mm(high, w[...], 1, 1) + mm(low, w[...], 1, 1)
    picked = jnp.where(own_expert(experts, capacity), picked, 0.0).astype(BF)
    fold = fold_of(slots, experts, capacity, lax.rem(where[0], 4))
    rows = mm(picked, fold, 1, 1).astype(coords_out.dtype)
    for e in range(experts):
        coords_out[jnp.bitwise_xor(where[0], e)] = rows[e * RANK : (e + 1) * RANK]
    for copy in copies:
        copy.wait()


def inverse_kernel(a_in, a_out, lows, inv_in, inv_out):
    experts, _, double = lows.shape
    stats = jnp.sum(lows[:, :, double // 2 :].astype(F32), axis=0)
    row = lax.broadcasted_iota(jnp.int32, (RANK, RANK), 0)
    column = lax.broadcasted_iota(jnp.int32, (RANK, RANK), 1)
    eye = (row == column).astype(F32)
    works = []
    for base, factor in ((0, a_in), (3, a_out)):
        pieces = stats[base : base + 1, 0:1] + stats[base + 1 : base + 2, 0:1]
        damp = (pieces + stats[base + 2 : base + 3, 0:1]) / (float(RANK) * experts)
        gram = mm(factor[...], factor[...], 1, 1) + damp * eye
        works.append([gram, eye])
    for j in range(RANK):
        for work in works:
            gram, inverse = work
            pivot = 1.0 / gram[j : j + 1, j : j + 1]
            gram_row, inverse_row = gram[j : j + 1] * pivot, inverse[j : j + 1] * pivot
            scale = gram[:, j : j + 1]
            work[0] = jnp.where(row == j, gram_row, gram - scale * gram_row)
            work[1] = jnp.where(row == j, inverse_row, inverse - scale * inverse_row)
    inv_in[...] = works[0][1]
    inv_out[...] = works[1][1]


def scaled_in_kernel(coords, hidden, inverse, out):
    pieces = []
    for base in range(0, coords.shape[0], 4):
        total = coords[base].astype(F32)
        for q in range(1, 4):
            total = total + coords[base + q].astype(F32)
        pieces.append(total)
    grad_low = jnp.concatenate(pieces, axis=1).astype(BF)
    out[...] = mm(inverse[...], mm(grad_low, hidden[...]), precision=HIGHEST)


def scaled_out_kernel(where, inverse, *refs):
    pieces, out = refs[:-1], refs[-1]
    half = out.shape[1] // 2
    for flip in range(2):
        base = jnp.bitwise_xor(where[1], flip) * half
        for piece in pieces[flip * CHUNKS : (flip + 1) * CHUNKS]:
            rows = mm(inverse[...], piece[...], precision=HIGHEST)
            out[:, lanes(base, piece.shape[1])] = rows
            base = base + piece.shape[1]


def radix_groups(experts):
    groups, bit = [], 4
    while bit < experts:
        radix = min(4, experts // bit)
        groups.append([bit * k for k in range(1, radix)])
        bit *= radix
    return groups


def relative_order(bits):
    order = [0]
    for bit in bits:
        order = order + [e ^ bit for e in order]
    return order


def on_device(hidden_slots, adapter_in, adapter_out, expert_ids, gate_weights, cotangent):
    experts, groups = lax.axis_size("expert"), lax.axis_size("group")
    me, group = lax.axis_index("expert"), lax.axis_index("group")
    where = jnp.stack([me, me % 2, group % 2]).astype(jnp.int32)
    hidden, a_in, a_out = hidden_slots[0], adapter_in[0], adapter_out[0]
    width = a_out.shape[1]
    half = width // 2
    tokens = cotangent.shape[0]
    capacity = hidden.shape[0] // experts
    struct = jax.ShapeDtypeStruct

    def swap(x, bit):
        return lax.ppermute(x, "expert", [(i, i ^ bit) for i in range(experts)])

    def swap_side(x):
        return lax.ppermute(x, "group", [(i, i ^ 1) for i in range(groups)])

    def spread(x):
        return lax.all_to_all(x, "expert", split_axis=0, concat_axis=0, tiled=True)

    groups_z = radix_groups(experts)
    far_bits = [1 << i for i in reversed(range(2, experts.bit_length() - 1))]
    full = relative_order([2, *far_bits, 1])

    block = lax.dynamic_slice_in_dim(a_out, (group % 2) * half, half, axis=1)
    received = swap(block, 2)
    low, stats = call(
        low_rank_kernel,
        [struct((RANK, hidden.shape[0]), BF), struct((RANK, 2 * capacity), BF)],
        [hidden, a_in, a_out],
        scratch=[
            VMEM(hidden.shape, BF),
            VMEM(a_in.shape, BF),
            VMEM(a_out.shape, BF),
            DMA((6,)),
        ],
        spaces=[HBM] * 3,
        limit=63 * MIB,
    )
    far_tokens = lax.dynamic_slice_in_dim(cotangent, (1 - me % 2) * half, half, axis=1)
    far_tokens = swap(far_tokens, 1)
    own_meta = jnp.concatenate(
        [expert_ids.T.astype(BF), gate_weights.T.astype(BF), jnp.zeros((12, tokens), BF)], axis=0
    )
    far_meta = swap(own_meta, 1)
    (block,) = call(
        join_kernel, [struct((2 * RANK, half), BF)], [block, received], after=[low]
    )
    (lows,) = call(
        pack_low_kernel,
        [struct((experts, RANK, 4 * capacity), BF)],
        [low, stats],
        after=[block],
    )
    lows = spread(lows)
    inv_in, inv_out = call(
        inverse_kernel, [struct((RANK, RANK), F32)] * 2, [a_in, a_out, lows]
    )
    count = experts * RANK // 2
    for bit in far_bits:
        received = swap(block, bit)
        if bit == far_bits[-1]:
            near = [block, received]
        else:
            (block,) = call(
                join_kernel,
                [struct((2 * block.shape[0], half), BF)],
                [block, received],
                after=[lows],
            )
    tiles = half // 128
    wides = [128 * (tiles // 2), half - 128 * (tiles // 2)]
    z, weights, *parts = call(
        lambda *refs: partial_kernel(full, *refs),
        [struct((tokens, experts * RANK), BF), struct((experts * capacity, tokens), BF)]
        + [struct((count, wide), F32) for wide in wides]
        + [struct((count, wide), BF) for wide in wides],
        [cotangent, far_tokens, own_meta, far_meta, lows],
        where,
        after=[near[0]],
        scratch=[VMEM((tokens, half), BF), DMA],
        spaces=[HBM, VMEM, VMEM, VMEM, VMEM],
    )
    kept, sent = parts[:CHUNKS], parts[CHUNKS:]
    near[1:] = call(
        join_kernel, [struct(near[1].shape, BF)], [near[1]], after=[sent[0]]
    )
    factors, far = list(near), [swap_side(block) for block in near]

    factors += [swap(block, 1) for block in near]
    far += [swap(block, 1) for block in far]
    scratch = [
        VMEM((tokens, half), BF),
        VMEM((experts * RANK, half), BF),
        VMEM((tokens, half), BF),
        DMA((2 * len(near) + 1,)),
    ]
    near_coords, delta = call(
        near_kernel,
        [struct((experts * RANK, tokens), F32), struct((tokens, width), BF)],
        [cotangent, z, *factors],
        where,
        scratch=scratch,
        spaces=[HBM, VMEM] + [HBM] * len(factors),
        out_spaces=[VMEM, HBM],
    )
    coords, delta = call(
        lambda *refs: far_kernel(full, *refs),
        [struct((experts, RANK, 4 * capacity), BF), struct((tokens, width), BF)],
        [cotangent, z, weights, near_coords, delta, *far],
        where,
        scratch=scratch,
        spaces=[HBM, VMEM, VMEM, VMEM, HBM] + [HBM] * len(far),
        out_spaces=[VMEM, HBM],
        alias={5: 1},
    )
    own_rows, far_rows = [], []
    for piece in range(CHUNKS):
        keep, rows, wide = kept[piece], count, wides[piece]
        received = [swap(sent[piece], 2)]
        for group in groups_z:
            radix = 1 + len(group)
            rows //= radix
            if piece == 0:
                total = keep
                for more in received:
                    total = total + more.astype(F32)
                total = total.reshape(rows // (2 * RANK), radix, 2 * RANK, wide)
                keep = total[:, 0].reshape(rows, wide)
                sends = [total[:, k].reshape(rows, wide).astype(BF) for k in range(1, radix)]
            else:
                *sends, keep = call(
                    lambda keep, *refs, n=len(received): fold_step_kernel(n, keep, *refs),
                    [struct((rows, wide), BF)] * len(group) + [struct((rows, wide), F32)],
                    [keep, *received],
                    after=[near_coords, far[1]],
                )
            received = [swap(send, k) for send, k in zip(sends, group)]
        if piece == 0:
            for more in received:
                keep = keep + more.astype(F32)
            keep, send = keep[:RANK], keep[RANK:]
        else:
            keep, send = call(
                last_fold_kernel,
                [struct((RANK, wide), F32)] * 2,
                [keep, *received],
                after=[coords],
            )
        own_rows.append(keep)
        far_rows.append(swap(send, 1))

    coords = spread(coords)
    (scaled_in,) = call(
        scaled_in_kernel, [struct((RANK, hidden.shape[1]), F32)], [coords, hidden, inv_out]
    )
    (scaled_out,) = call(
        scaled_out_kernel, [struct((RANK, width), F32)], [inv_in, *own_rows, *far_rows], where
    )
    return delta, scaled_in[None], scaled_out[None]


def solution(mesh):
    every = ("group", "expert")
    return jax.shard_map(
        on_device,
        mesh=mesh,
        in_specs=(
            P(every, None, None),
            P("expert", None, None),
            P("expert", None, None),
            P(every, None),
            P(every, None),
            P(every, None),
        ),
        out_specs=(P(every, None), P(every, None, None), P(every, None, None)),
        check_vma=False,
    )
```

time: 85.5 us -> 78.1 us (0.913)
  blocking collectives: 12.4 us -> 0 us
  starting transfers between devices: 23.7 us -> 31.6 us
  waiting for transfers between devices: 27.7 us -> 20 us
  Pallas kernels: 15.7 us -> 19.2 us
  other arithmetic: 0.08 us -> 1.05 us
    ppermute x16 -> x19, waiting for transfers between devices: 24 us -> 9.59 us  [swap(): return lax.ppermute(x, 'expert', [(i, i ^ bit) for i in range(experts)])]
    all_to_all x1 -> x0, blocking collectives: 12.4 us -> none  [spread(): return lax.all_to_all(x, 'expert', split_axis=0, concat_axis=0, tiled=True)]
    all_to_all x1 -> x2, waiting for transfers between devices: 2.67 us -> 8.28 us  [spread(): return lax.all_to_all(x, 'expert', split_axis=0, concat_axis=0, tiled=True)]
    all_to_all x1 -> x2, starting transfers between devices: 4.53 us -> 9.04 us  [spread(): return lax.all_to_all(x, 'expert', split_axis=0, concat_axis=0, tiled=True)]
    pallas_call x17 -> x13, Pallas kernels: 15.7 us -> 19.2 us  [call(): pl.pallas_call(body, out_shape=[jax.ShapeDtypeStruct(o.shape, o.dtype) fo...]
    ppermute x16 -> x19, starting transfers between devices: 16.2 us -> 19.5 us  [swap(): return lax.ppermute(x, 'expert', [(i, i ^ bit) for i in range(experts)])]
    unnamed x18, local copies, waits for them, and re-layouts: 4.75 us -> 1.59 us
    dynamic_slice x0 -> x2, local copies, waits for them, and re-layouts: none -> 2.26 us  [the longest x1 2.25 us: on_device(): lax.dynamic_slice_in_dim(cotangent, (1 - me % 2) * half, half, axis=1)]
  transfers between devices with their start and end apart: 19 -> 23, of which waited for: 6 -> 7; matrix products, arithmetic and copies ran while one was open for 0% -> 3% of each run, Pallas kernels for 16% -> 23%
where the time goes in v4:
time: 78.1 us; the launch traced here: 77.6 us
  starting transfers between devices  31.6 us (40%)
  waiting for transfers between devices  20 us (26%)
  Pallas kernels  19.2 us (25%)
  local copies, waits for them, and re-layouts  4.93 us (6%)
  other arithmetic  1.05 us (1%)
  between operations  0.88 us (1%)
    ppermute x19, starting transfers between devices, swap(): return lax.ppermute(x, 'expert', [(i, i ^ bit) for i in range(experts)])  19.5 us
    pallas_call x13, Pallas kernels, call(): pl.pallas_call(body, out_shape=[jax.ShapeDtypeStruct(o.shape, o.dtype) fo...  19.2 us
    ppermute x19, waiting for transfers between devices, swap(): return lax.ppermute(x, 'expert', [(i, i ^ bit) for i in range(experts)])  9.59 us
    all_to_all x2, starting transfers between devices, spread(): return lax.all_to_all(x, 'expert', split_axis=0, concat_axis=0, tiled=True)  9.04 us
    all_to_all x2, waiting for transfers between devices, spread(): return lax.all_to_all(x, 'expert', split_axis=0, concat_axis=0, tiled=True)  8.28 us
    ppermute x2, starting transfers between devices, swap_side(): return lax.ppermute(x, 'group', [(i, i ^ 1) for i in range(groups)])  3.05 us
    dynamic_slice x1, local copies, waits for them, and re-layouts, on_device(): lax.dynamic_slice_in_dim(cotangent, (1 - me % 2) * half, half, axis=1)  2.25 us
    ppermute x2, waiting for transfers between devices, swap_side(): return lax.ppermute(x, 'group', [(i, i ^ 1) for i in range(groups)])  2.11 us
  transfers between devices with their start and end apart: 23, of which 7 were waited for; matrix products, arithmetic and copies ran while one was open for 3% of the time, Pallas kernels for 23%

profile of v4, /device:TPU:0, one launch (start us, length us, event | category | flops | bytes accessed | tf_op | source)
XLA Modules:
  0.0 77.6 jit_solution(11644943361403310837)
XLA Ops:
  0.7 2.3 %constant_dynamic-slice_fusion = bf16[128,3584]{1,0:T(8,128)(2,1)} fusion(bf16[128,7168]{1,0:T(8,128)(2,1)} %refs_1_.5, s32[]{:T(128)S(6)} %select_n.23), kind=kLoop, calls=%fused_computation.13 | loop fusion | bytes 1835012 | tf_op jit(solution)/shard_map/dynamic_slice | solution.py:361
  3.4 2.6 %collective-permute-start.2 = (bf16[16,3584]{1,0:T(8,128)(2,1)S(1)}, bf16[16,3584]{1,0:T(8,128)(2,1)S(1)}, u32[]{:S(2)}, u32[]{:S(2)}) collective-permute-start(bf16[16,3584]{1,0:T(8,128)(2,1)S(1)} %dynamic-slice_bitcast_fusion.refs_0_), channel_id=1, source_target_pairs={{0,2},{1,3},{2,0},{3,1},{4,6},{5,7},{6,4},{7,5},{8,10},{9,11},{10,... | collective-permute-start | bytes 344072 | tf_op jit(solution)/shard_map/ppermute | solution.py:334
  6.1 3.4 %shard_map.85 = (bf16[16,512]{1,0:T(8,128)(2,1)}, bf16[16,64]{1,0:T(8,128)(2,1)}) custom-call(bf16[512,2048]{1,0:T(8,128)(2,1)} %bitcast.29, bf16[16,2048]{1,0:T(8,128)(2,1)} %bitcast.33, bf16[16,7168]{1,0:T(8,128)(2,1)} %bitcast.31), custom_call_target="tpu_custom_call" | custom-call | bytes 2410496 | tf_op jit(solution)/shard_map/pallas_call | solution.py:43
  10.7 2.8 %collective-permute-start.3 = (bf16[32,3584]{1,0:T(8,128)(2,1)S(1)}, bf16[32,3584]{1,0:T(8,128)(2,1)S(1)}, u32[]{:S(2)}, u32[]{:S(2)}) collective-permute-start(bf16[32,3584]{1,0:T(8,128)(2,1)S(1)} %shard_map.86.refs_2_.refs_0_), channel_id=1, source_target_pairs={{0,8},{1,9},{2,10},{3,11},{4,12},{5,13},{6,14},{7,15},{8,0},{9,1},... | collective-permute-start | bytes 688136 | tf_op jit(solution)/shard_map/ppermute | solution.py:334
  14.9 3.9 %all-to-all-start = ((bf16[16,16,128]{2,1,0:T(8,128)(2,1)}), bf16[16,16,128]{2,1,0:T(8,128)(2,1)S(1)}, u32[]{:S(2)}, u32[]{:S(2)}) async-start(bf16[16,16,128]{2,1,0:T(8,128)(2,1)} %shard_map.87), calls=%async_computation | async-start | bytes 131072 | tf_op jit(solution)/shard_map/all_to_all | solution.py:340
  19.3 6.6 %all-to-all-done.refs_2_.refs_5_ = bf16[16,16,128]{2,1,0:T(8,128)(2,1)S(1)} async-done(((bf16[16,16,128]{2,1,0:T(8,128)(2,1)}), bf16[16,16,128]{2,1,0:T(8,128)(2,1)S(1)}, u32[]{:S(2)}, u32[]{:S(2)}) %all-to-all-start) | async-done | bytes 65568 | tf_op jit(solution)/shard_map/all_to_all | solution.py:340
  26.7 3.0 %shard_map.89 = (bf16[128,256]{1,0:T(8,128)(2,1)S(1)}, bf16[512,128]{1,0:T(8,128)(2,1)S(1)}, f32[128,1792]{1,0:T(8,128)S(1)}, f32[128,1792]{1,0:T(8,128)S(1)}, b...) custom-call(s32[3]{0:T(128)S(1)} %pad_add_fusion.refs_0_, bf16[128,7168]{1,0:T(8,128)(2,1)S(1)} %copy-done, ...), custom_call_target="tpu_custom_call" | custom-call | bytes 5775360 | tf_op jit(solution)/shard_map/pallas_call | solution.py:43
  30.7 1.5 %collective-permute-start.7 = (bf16[64,3584]{1,0:T(8,128)(2,1)S(1)}, bf16[64,3584]{1,0:T(8,128)(2,1)S(1)}, u32[]{:S(2)}, u32[]{:S(2)}) collective-permute-start(bf16[64,3584]{1,0:T(8,128)(2,1)S(1)} %shard_map.88.refs_6_.refs_3_), channel_id=1, source_target_pairs={{0,16},{16,0},{1,17},{17,1},{2,18},{18,2},{3,19},{19,3},{4,20},{20... | collective-permute-start | bytes 1376264 | tf_op jit(solution)/shard_map/ppermute | solution.py:337
  32.1 6.4 %collective-permute-done.4.refs_0_ = bf16[64,3584]{1,0:T(8,128)(2,1)S(1)} collective-permute-done((bf16[64,3584]{1,0:T(8,128)(2,1)S(1)}, bf16[64,3584]{1,0:T(8,128)(2,1)S(1)}, u32[]{:S(2)}, u32[]{:S(2)}) %collective-permute-start.4) | collective-permute-done | bytes 458784 | tf_op jit(solution)/shard_map/ppermute | solution.py:334
  38.7 1.6 %collective-permute-start.8 = (bf16[64,3584]{1,0:T(8,128)(2,1)S(1)}, bf16[64,3584]{1,0:T(8,128)(2,1)S(1)}, u32[]{:S(2)}, u32[]{:S(2)}) collective-permute-start(bf16[64,3584]{1,0:T(8,128)(2,1)S(1)} %shard_map.90.refs_4_), channel_id=1, source_target_pairs={{0,16},{16,0},{1,17},{17,1},{2,18},{18,2},{3,19},{19,3},{4,20},{20... | collective-permute-start | bytes 1376264 | tf_op jit(solution)/shard_map/ppermute | solution.py:337
  40.2 1.8 %collective-permute-done.11 = bf16[128,1792]{1,0:T(8,128)(2,1)S(1)} collective-permute-done((bf16[128,1792]{1,0:T(8,128)(2,1)S(1)}, bf16[128,1792]{1,0:T(8,128)(2,1)S(1)}, u32[]{:S(2)}, u32[]{:S(2)}) %collective-permute-start.11) | collective-permute-done | bytes 458784 | tf_op jit(solution)/shard_map/ppermute | solution.py:334
  43.0 1.3 %collective-permute-start.12 = (bf16[32,1792]{1,0:T(8,128)(2,1)S(1)}, bf16[32,1792]{1,0:T(8,128)(2,1)S(1)}, u32[]{:S(2)}, u32[]{:S(2)}) collective-permute-start(bf16[32,1792]{1,0:T(8,128)(2,1)S(1)} %get-tuple-element.43), channel_id=1, source_target_pairs={{0,4},{1,5},{2,6},{3,7},{4,0},{5,1},{6,2},{7,3},{8,12},{9,13},{10,... | collective-permute-start | bytes 344072 | tf_op jit(solution)/shard_map/ppermute | solution.py:334
  44.4 3.0 %collective-permute-start.13 = (bf16[32,1792]{1,0:T(8,128)(2,1)S(1)}, bf16[32,1792]{1,0:T(8,128)(2,1)S(1)}, u32[]{:S(2)}, u32[]{:S(2)}) collective-permute-start(bf16[32,1792]{1,0:T(8,128)(2,1)S(1)} %get-tuple-element.45), channel_id=1, source_target_pairs={{0,8},{1,9},{2,10},{3,11},{4,12},{5,13},{6,14},{7,15},{8,0},{9,1},... | collective-permute-start | bytes 344072 | tf_op jit(solution)/shard_map/ppermute | solution.py:334
  48.1 3.2 %shard_map.91 = (f32[256,128]{1,0:T(8,128)S(1)}, bf16[128,7168]{1,0:T(8,128)(2,1)}) custom-call(s32[3]{0:T(128)S(1)} %pad_add_fusion.refs_0_, bf16[128,7168]{1,0:T(8,128)(2,1)S(1)} %copy-done, bf16[128,256]{1,0:T(8,128)(2,1)S(1)} %get-tuple-element.25.refs_2_, bf16[64,3584]{1,0:T(8,128)(2,1)S(1)} %shard_map.88.refs_6_.refs_3_, ...), custom_call_target="tpu_custom_call" | custom-call | bytes 5701632 | tf_op jit(solution)/shard_map/pallas_call | solution.py:43
  51.3 2.1 %collective-permute-done.8.refs_7_.refs_3_ = bf16[64,3584]{1,0:T(8,128)(2,1)S(1)} collective-permute-done((bf16[64,3584]{1,0:T(8,128)(2,1)S(1)}, bf16[64,3584]{1,0:T(8,128)(2,1)S(1)}, u32[]{:S(2)}, u32[]{:S(2)}) %collective-permute-start.8) | collective-permute-done | bytes 458784 | tf_op jit(solution)/shard_map/ppermute | solution.py:337
  53.5 1.4 %collective-permute-start.16 = (bf16[32,1792]{1,0:T(8,128)(2,1)S(1)}, bf16[32,1792]{1,0:T(8,128)(2,1)S(1)}, u32[]{:S(2)}, u32[]{:S(2)}) collective-permute-start(bf16[32,1792]{1,0:T(8,128)(2,1)S(1)} %get-tuple-element.38), channel_id=1, source_target_pairs={{0,4},{1,5},{2,6},{3,7},{4,0},{5,1},{6,2},{7,3},{8,12},{9,13},{10,... | collective-permute-start | bytes 344072 | tf_op jit(solution)/shard_map/ppermute | solution.py:334
  54.9 2.4 %collective-permute-start.17 = (bf16[32,1792]{1,0:T(8,128)(2,1)S(1)}, bf16[32,1792]{1,0:T(8,128)(2,1)S(1)}, u32[]{:S(2)}, u32[]{:S(2)}) collective-permute-start(bf16[32,1792]{1,0:T(8,128)(2,1)S(1)} %get-tuple-element.39), channel_id=1, source_target_pairs={{0,8},{1,9},{2,10},{3,11},{4,12},{5,13},{6,14},{7,15},{8,0},{9,1},... | collective-permute-start | bytes 344072 | tf_op jit(solution)/shard_map/ppermute | solution.py:334
  57.3 1.3 %collective-permute-start.18 = (bf16[32,1792]{1,0:T(8,128)(2,1)S(1)}, bf16[32,1792]{1,0:T(8,128)(2,1)S(1)}, u32[]{:S(2)}, u32[]{:S(2)}) collective-permute-start(bf16[32,1792]{1,0:T(8,128)(2,1)S(1)} %get-tuple-element.40), channel_id=1, source_target_pairs={{0,12},{1,13},{2,14},{3,15},{4,8},{5,9},{6,10},{7,11},{8,4},{9,5},... | collective-permute-start | bytes 344072 | tf_op jit(solution)/shard_map/ppermute | solution.py:334
  60.4 3.9 %shard_map.92 = (bf16[16,16,128]{2,1,0:T(8,128)(2,1)}, bf16[128,7168]{1,0:T(8,128)(2,1)}) custom-call(s32[3]{0:T(128)S(1)} %pad_add_fusion.refs_0_, bf16[128,7168]{1,0:T(8,128)(2,1)S(1)} %copy-done, bf16[128,256]{1,0:T(8,128)(2,1)S(1)} %get-tuple-element.25.refs_2_, bf16[512,128]{1,0:T(8,128)(2,1)S(1)} %get-tuple-element.26.refs_3_, ...), custom_call_target="tpu_custom_call", output_to_operand_aliasing={{1}: (5, {})} | custom-call | bytes 7733248 | tf_op jit(solution)/shard_map/pallas_call | solution.py:43
  64.3 5.2 %all-to-all-start.1 = ((bf16[16,16,128]{2,1,0:T(8,128)(2,1)}), bf16[16,16,128]{2,1,0:T(8,128)(2,1)S(1)}, u32[]{:S(2)}, u32[]{:S(2)}) async-start(bf16[16,16,128]{2,1,0:T(8,128)(2,1)} %get-tuple-element.31.refs_4_), calls=%async_computation.1 | async-start | bytes 131072 | tf_op jit(solution)/shard_map/all_to_all | solution.py:340
  71.2 1.5 %shard_map.93 = (f32[16,16]{1,0:T(8,128)S(1)}, f32[16,16]{1,0:T(8,128)S(1)}) custom-call(bf16[16,2048]{1,0:T(8,128)(2,1)S(1)} %bitcast.34, bf16[16,7168]{1,0:T(8,128)(2,1)S(1)} %bitcast.32, bf16[16,16,128]{2,1,0:T(8,128)(2,1)S(1)} %all-to-all-done.refs_2_.refs_5_), custom_call_target="tpu_custom_call" | custom-call | bytes 362496 | tf_op jit(solution)/shard_map/pallas_call | solution.py:43
  72.8 1.9 %shard_map.97 = f32[16,7168]{1,0:T(8,128)} custom-call(s32[3]{0:T(128)S(1)} %pad_add_fusion.refs_0_, f32[16,16]{1,0:T(8,128)S(1)} %get-tuple-element.33.refs_1_, f32[16,1792]{1,0:T(8,128)S(1)} %get-tuple-element.47.refs_2_, f32[16,1792]{1,0:T(8,128)S(1)} %get-tuple-element.41.refs_3_, f32[16,1792]{1,0:T(8,128)S(1)} %collective-permute-done.19.refs_4_, ...), custom_call_target="tpu_custom_call" | custom-call | bytes 918528 | tf_op jit(solution)/shard_map/pallas_call | solution.py:43
  74.7 1.7 %all-to-all-done.1.refs_0_ = bf16[16,16,128]{2,1,0:T(8,128)(2,1)S(1)} async-done(((bf16[16,16,128]{2,1,0:T(8,128)(2,1)}), bf16[16,16,128]{2,1,0:T(8,128)(2,1)S(1)}, u32[]{:S(2)}, u32[]{:S(2)}) %all-to-all-start.1) | async-done | bytes 65568 | tf_op jit(solution)/shard_map/all_to_all | solution.py:340
  76.4 1.2 %shard_map.94 = f32[16,2048]{1,0:T(8,128)} custom-call(bf16[16,16,128]{2,1,0:T(8,128)(2,1)S(1)} %all-to-all-done.1.refs_0_, bf16[512,2048]{1,0:T(8,128)(2,1)S(1)} %bitcast.30, f32[16,16]{1,0:T(8,128)S(1)} %get-tuple-element.32.refs_2_), custom_call_target="tpu_custom_call" | custom-call | bytes 2294784 | tf_op jit(solution)/shard_map/pallas_call | solution.py:43
  (66 shorter events, 10.9 us)
Async XLA Ops:
  2.9 23.8 %collective-permute-start = (bf16[128,3584]{1,0:T(8,128)(2,1)}, bf16[128,3584]{1,0:T(8,128)(2,1)}, u32[]{:S(2)}, u32[]{:S(2)}) collective-permute-start(bf16[128,3584]{1,0:T(8,128)(2,1)} %constant_dynamic-slice_fusion), channel_id=1, source_target_pairs={{0,1},{1,0},{2,3},{3,2},{4,5},{5,4},{6,7},{7,6},{8,9},{9,8},{10,11... | collective-permute-start | bytes 2752520 | tf_op jit(solution)/shard_map/ppermute | solution.py:334
  3.4 6.4 %collective-permute-start.2 = (bf16[16,3584]{1,0:T(8,128)(2,1)S(1)}, bf16[16,3584]{1,0:T(8,128)(2,1)S(1)}, u32[]{:S(2)}, u32[]{:S(2)}) collective-permute-start(bf16[16,3584]{1,0:T(8,128)(2,1)S(1)} %dynamic-slice_bitcast_fusion.refs_0_), channel_id=1, source_target_pairs={{0,2},{1,3},{2,0},{3,1},{4,6},{5,7},{6,4},{7,5},{8,10},{9,11},{10,... | collective-permute-start | bytes 344072 | tf_op jit(solution)/shard_map/ppermute | solution.py:334
  9.5 17.2 %copy-start = (bf16[128,7168]{1,0:T(8,128)(2,1)S(1)}, bf16[128,7168]{1,0:T(8,128)(2,1)}, u32[]{:S(2)}) copy-start(bf16[128,7168]{1,0:T(8,128)(2,1)} %refs_1_.5) | copy-start | bytes 5505028
  10.7 15.2 %collective-permute-start.3 = (bf16[32,3584]{1,0:T(8,128)(2,1)S(1)}, bf16[32,3584]{1,0:T(8,128)(2,1)S(1)}, u32[]{:S(2)}, u32[]{:S(2)}) collective-permute-start(bf16[32,3584]{1,0:T(8,128)(2,1)S(1)} %shard_map.86.refs_2_.refs_0_), channel_id=1, source_target_pairs={{0,8},{1,9},{2,10},{3,11},{4,12},{5,13},{6,14},{7,15},{8,0},{9,1},... | collective-permute-start | bytes 688136 | tf_op jit(solution)/shard_map/ppermute | solution.py:334
  14.9 11.0 %all-to-all-start = ((bf16[16,16,128]{2,1,0:T(8,128)(2,1)}), bf16[16,16,128]{2,1,0:T(8,128)(2,1)S(1)}, u32[]{:S(2)}, u32[]{:S(2)}) async-start(bf16[16,16,128]{2,1,0:T(8,128)(2,1)} %shard_map.87), calls=%async_computation | async-start | bytes 131072 | tf_op jit(solution)/shard_map/all_to_all | solution.py:340
  18.8 7.8 %collective-permute-start.1 = (bf16[16,128]{1,0:T(8,128)(2,1)S(1)}, bf16[16,128]{1,0:T(8,128)(2,1)S(1)}, u32[]{:S(2)}, u32[]{:S(2)}) collective-permute-start(bf16[16,128]{1,0:T(8,128)(2,1)S(1)} %maximum_maximum_fusion.refs_3_), channel_id=1, source_target_pairs={{0,1},{1,0},{2,3},{3,2},{4,5},{5,4},{6,7},{7,6},{8,9},{9,8},{10,11... | collective-permute-start | bytes 12296 | tf_op jit(solution)/shard_map/ppermute | solution.py:334
  26.0 12.6 %collective-permute-start.4 = (bf16[64,3584]{1,0:T(8,128)(2,1)S(1)}, bf16[64,3584]{1,0:T(8,128)(2,1)S(1)}, u32[]{:S(2)}, u32[]{:S(2)}) collective-permute-start(bf16[64,3584]{1,0:T(8,128)(2,1)S(1)} %shard_map.88.refs_6_.refs_3_), channel_id=1, source_target_pairs={{0,4},{1,5},{2,6},{3,7},{4,0},{5,1},{6,2},{7,3},{8,12},{9,13},{10,... | collective-permute-start | bytes 1376264 | tf_op jit(solution)/shard_map/ppermute | solution.py:334
  29.7 12.3 %collective-permute-start.11 = (bf16[128,1792]{1,0:T(8,128)(2,1)S(1)}, bf16[128,1792]{1,0:T(8,128)(2,1)S(1)}, u32[]{:S(2)}, u32[]{:S(2)}) collective-permute-start(bf16[128,1792]{1,0:T(8,128)(2,1)S(1)} %get-tuple-element.27.refs_1_), channel_id=1, source_target_pairs={{0,2},{1,3},{2,0},{3,1},{4,6},{5,7},{6,4},{7,5},{8,10},{9,11},{10,... | collective-permute-start | bytes 1376264 | tf_op jit(solution)/shard_map/ppermute | solution.py:334
  30.7 12.4 %collective-permute-start.5 = (bf16[64,3584]{1,0:T(8,128)(2,1)S(1)}, bf16[64,3584]{1,0:T(8,128)(2,1)S(1)}, u32[]{:S(2)}, u32[]{:S(2)}) collective-permute-start(bf16[64,3584]{1,0:T(8,128)(2,1)S(1)} %shard_map.88.refs_6_.refs_3_), channel_id=1, source_target_pairs={{0,1},{1,0},{2,3},{3,2},{4,5},{5,4},{6,7},{7,6},{8,9},{9,8},{10,11... | collective-permute-start | bytes 1376264 | tf_op jit(solution)/shard_map/ppermute | solution.py:334
  30.7 13.7 %collective-permute-start.7 = (bf16[64,3584]{1,0:T(8,128)(2,1)S(1)}, bf16[64,3584]{1,0:T(8,128)(2,1)S(1)}, u32[]{:S(2)}, u32[]{:S(2)}) collective-permute-start(bf16[64,3584]{1,0:T(8,128)(2,1)S(1)} %shard_map.88.refs_6_.refs_3_), channel_id=1, source_target_pairs={{0,16},{16,0},{1,17},{17,1},{2,18},{18,2},{3,19},{19,3},{4,20},{20... | collective-permute-start | bytes 1376264 | tf_op jit(solution)/shard_map/ppermute | solution.py:337
  38.6 8.7 %collective-permute-start.6 = (bf16[64,3584]{1,0:T(8,128)(2,1)S(1)}, bf16[64,3584]{1,0:T(8,128)(2,1)S(1)}, u32[]{:S(2)}, u32[]{:S(2)}) collective-permute-start(bf16[64,3584]{1,0:T(8,128)(2,1)S(1)} %shard_map.90.refs_4_), channel_id=1, source_target_pairs={{0,1},{1,0},{2,3},{3,2},{4,5},{5,4},{6,7},{7,6},{8,9},{9,8},{10,11... | collective-permute-start | bytes 1376264 | tf_op jit(solution)/shard_map/ppermute | solution.py:334
  38.7 14.7 %collective-permute-start.8 = (bf16[64,3584]{1,0:T(8,128)(2,1)S(1)}, bf16[64,3584]{1,0:T(8,128)(2,1)S(1)}, u32[]{:S(2)}, u32[]{:S(2)}) collective-permute-start(bf16[64,3584]{1,0:T(8,128)(2,1)S(1)} %shard_map.90.refs_4_), channel_id=1, source_target_pairs={{0,16},{16,0},{1,17},{17,1},{2,18},{18,2},{3,19},{19,3},{4,20},{20... | collective-permute-start | bytes 1376264 | tf_op jit(solution)/shard_map/ppermute | solution.py:337
  42.0 11.4 %collective-permute-start.15 = (bf16[128,1792]{1,0:T(8,128)(2,1)S(1)}, bf16[128,1792]{1,0:T(8,128)(2,1)S(1)}, u32[]{:S(2)}, u32[]{:S(2)}) collective-permute-start(bf16[128,1792]{1,0:T(8,128)(2,1)S(1)} %get-tuple-element.36), channel_id=1, source_target_pairs={{0,2},{1,3},{2,0},{3,1},{4,6},{5,7},{6,4},{7,5},{8,10},{9,11},{10,... | collective-permute-start | bytes 1376264 | tf_op jit(solution)/shard_map/ppermute | solution.py:334
  43.0 11.9 %collective-permute-start.12 = (bf16[32,1792]{1,0:T(8,128)(2,1)S(1)}, bf16[32,1792]{1,0:T(8,128)(2,1)S(1)}, u32[]{:S(2)}, u32[]{:S(2)}) collective-permute-start(bf16[32,1792]{1,0:T(8,128)(2,1)S(1)} %get-tuple-element.43), channel_id=1, source_target_pairs={{0,4},{1,5},{2,6},{3,7},{4,0},{5,1},{6,2},{7,3},{8,12},{9,13},{10,... | collective-permute-start | bytes 344072 | tf_op jit(solution)/shard_map/ppermute | solution.py:334
  44.4 13.0 %collective-permute-start.13 = (bf16[32,1792]{1,0:T(8,128)(2,1)S(1)}, bf16[32,1792]{1,0:T(8,128)(2,1)S(1)}, u32[]{:S(2)}, u32[]{:S(2)}) collective-permute-start(bf16[32,1792]{1,0:T(8,128)(2,1)S(1)} %get-tuple-element.45), channel_id=1, source_target_pairs={{0,8},{1,9},{2,10},{3,11},{4,12},{5,13},{6,14},{7,15},{8,0},{9,1},... | collective-permute-start | bytes 344072 | tf_op jit(solution)/shard_map/ppermute | solution.py:334
  47.4 11.3 %collective-permute-start.14 = (bf16[32,1792]{1,0:T(8,128)(2,1)S(1)}, bf16[32,1792]{1,0:T(8,128)(2,1)S(1)}, u32[]{:S(2)}, u32[]{:S(2)}) collective-permute-start(bf16[32,1792]{1,0:T(8,128)(2,1)S(1)} %get-tuple-element.44), channel_id=1, source_target_pairs={{0,12},{1,13},{2,14},{3,15},{4,8},{5,9},{6,10},{7,11},{8,4},{9,5},... | collective-permute-start | bytes 344072 | tf_op jit(solution)/shard_map/ppermute | solution.py:334
  53.4 5.9 %collective-permute-start.9 = (bf16[64,3584]{1,0:T(8,128)(2,1)S(1)}, bf16[64,3584]{1,0:T(8,128)(2,1)S(1)}, u32[]{:S(2)}, u32[]{:S(2)}) collective-permute-start(bf16[64,3584]{1,0:T(8,128)(2,1)S(1)} %collective-permute-done.7.refs_6_), channel_id=1, source_target_pairs={{0,1},{1,0},{2,3},{3,2},{4,5},{5,4},{6,7},{7,6},{8,9},{9,8},{10,11... | collective-permute-start | bytes 1376264 | tf_op jit(solution)/shard_map/ppermute | solution.py:334
  53.5 17.4 %collective-permute-start.16 = (bf16[32,1792]{1,0:T(8,128)(2,1)S(1)}, bf16[32,1792]{1,0:T(8,128)(2,1)S(1)}, u32[]{:S(2)}, u32[]{:S(2)}) collective-permute-start(bf16[32,1792]{1,0:T(8,128)(2,1)S(1)} %get-tuple-element.38), channel_id=1, source_target_pairs={{0,4},{1,5},{2,6},{3,7},{4,0},{5,1},{6,2},{7,3},{8,12},{9,13},{10,... | collective-permute-start | bytes 344072 | tf_op jit(solution)/shard_map/ppermute | solution.py:334
  54.9 16.0 %collective-permute-start.17 = (bf16[32,1792]{1,0:T(8,128)(2,1)S(1)}, bf16[32,1792]{1,0:T(8,128)(2,1)S(1)}, u32[]{:S(2)}, u32[]{:S(2)}) collective-permute-start(bf16[32,1792]{1,0:T(8,128)(2,1)S(1)} %get-tuple-element.39), channel_id=1, source_target_pairs={{0,8},{1,9},{2,10},{3,11},{4,12},{5,13},{6,14},{7,15},{8,0},{9,1},... | collective-permute-start | bytes 344072 | tf_op jit(solution)/shard_map/ppermute | solution.py:334
  57.3 13.6 %collective-permute-start.18 = (bf16[32,1792]{1,0:T(8,128)(2,1)S(1)}, bf16[32,1792]{1,0:T(8,128)(2,1)S(1)}, u32[]{:S(2)}, u32[]{:S(2)}) collective-permute-start(bf16[32,1792]{1,0:T(8,128)(2,1)S(1)} %get-tuple-element.40), channel_id=1, source_target_pairs={{0,12},{1,13},{2,14},{3,15},{4,8},{5,9},{6,10},{7,11},{8,4},{9,5},... | collective-permute-start | bytes 344072 | tf_op jit(solution)/shard_map/ppermute | solution.py:334
  58.6 1.8 %collective-permute-start.10 = (bf16[64,3584]{1,0:T(8,128)(2,1)S(1)}, bf16[64,3584]{1,0:T(8,128)(2,1)S(1)}, u32[]{:S(2)}, u32[]{:S(2)}) collective-permute-start(bf16[64,3584]{1,0:T(8,128)(2,1)S(1)} %collective-permute-done.8.refs_7_.refs_3_), channel_id=1, source_target_pairs={{0,1},{1,0},{2,3},{3,2},{4,5},{5,4},{6,7},{7,6},{8,9},{9,8},{10,11... | collective-permute-start | bytes 1376264 | tf_op jit(solution)/shard_map/ppermute | solution.py:334
  64.3 12.1 %all-to-all-start.1 = ((bf16[16,16,128]{2,1,0:T(8,128)(2,1)}), bf16[16,16,128]{2,1,0:T(8,128)(2,1)S(1)}, u32[]{:S(2)}, u32[]{:S(2)}) async-start(bf16[16,16,128]{2,1,0:T(8,128)(2,1)} %get-tuple-element.31.refs_4_), calls=%async_computation.1 | async-start | bytes 131072 | tf_op jit(solution)/shard_map/all_to_all | solution.py:340
  70.5 2.3 %collective-permute-start.19 = (f32[16,1792]{1,0:T(8,128)S(1)}, f32[16,1792]{1,0:T(8,128)S(1)}, u32[]{:S(2)}, u32[]{:S(2)}) collective-permute-start(f32[16,1792]{1,0:T(8,128)S(1)} %get-tuple-element.46), channel_id=1, source_target_pairs={{0,1},{1,0},{2,3},{3,2},{4,5},{5,4},{6,7},{7,6},{8,9},{9,8},{10,11... | collective-permute-start | bytes 344072 | tf_op jit(solution)/shard_map/ppermute | solution.py:334
  71.0 1.7 %collective-permute-start.20 = (f32[16,1792]{1,0:T(8,128)S(1)}, f32[16,1792]{1,0:T(8,128)S(1)}, u32[]{:S(2)}, u32[]{:S(2)}) collective-permute-start(f32[16,1792]{1,0:T(8,128)S(1)} %get-tuple-element.42), channel_id=1, source_target_pairs={{0,1},{1,0},{2,3},{3,2},{4,5},{5,4},{6,7},{7,6},{8,9},{9,8},{10,11... | collective-permute-start | bytes 344072 | tf_op jit(solution)/shard_map/ppermute | solution.py:334
  (8 other events, 55.6 us)

commit v5 on v4

v5 whole, which is shorter than its diff:
```python
import jax
import jax.numpy as jnp
import numpy as np
from jax import lax
from jax.experimental import pallas as pl
from jax.experimental.pallas import tpu as pltpu
from jax.sharding import PartitionSpec as P
BF = jnp.bfloat16
F32 = jnp.float32
HIGHEST = lax.Precision.HIGHEST
RANK = 16
CHUNKS = 2
HBM = pltpu.HBM
VMEM = pltpu.VMEM
DMA = pltpu.SemaphoreType.DMA
MIB = 1024 * 1024


def mm(a, b, ca=1, cb=0, precision=None):
    return lax.dot_general(a, b, (((ca,), (cb,)), ((), ())), preferred_element_type=F32, precision=precision)


def call(kernel, outs, args, scalars=None, after=(), scratch=(), spaces=None, out_spaces=None, alias=None, limit=None):
    size = sum((x.size * x.dtype.itemsize for x in [*args, *outs]))
    total = size + sum((np.prod(x.shape) * x.dtype.itemsize for x in scratch if hasattr(x.dtype, 'itemsize')))
    specs = [pl.BlockSpec(memory_space=space) for space in spaces or [VMEM] * len(args)]
    out_spaces = out_spaces or [VMEM] * len(outs)
    if scalars is not None:
        args = [scalars, *args]
        specs = [pl.BlockSpec(memory_space=pltpu.SMEM), *specs]
    used = len(args)

    def body(*refs):
        kernel(*refs[:used], *refs[used + len(after):])
    return pl.pallas_call(body, out_shape=[jax.ShapeDtypeStruct(o.shape, o.dtype) for o in outs], in_specs=specs + [pl.BlockSpec(memory_space=pl.ANY)] * len(after), out_specs=[pl.BlockSpec(memory_space=space) for space in out_spaces], scratch_shapes=list(scratch), input_output_aliases=alias or {}, compiler_params=pltpu.CompilerParams(vmem_limit_bytes=limit or min(60 * MIB, int(8 * MIB + 1.5 * total))), cost_estimate=pl.CostEstimate(flops=0, bytes_accessed=size, transcendentals=0))(*args, *after)


def split(x):
    high = x.astype(BF)
    return (high, (x - high.astype(F32)).astype(BF))


def lanes(start, size):
    return pl.ds(pl.multiple_of(start, 128), size)


def low_rank_kernel(hidden, a_in, a_out, low_out, stats_out, hidden_in, a_in_in, a_out_in, sems):
    slots = stats_out.shape[1]
    pieces = 4
    rows = hidden.shape[0] // pieces
    copies = [pltpu.make_async_copy(a_in, a_in_in, sems.at[pieces]), pltpu.make_async_copy(a_out, a_out_in, sems.at[pieces + 1])]
    for i in range(pieces):
        part = pl.ds(i * rows, rows)
        copies.append(pltpu.make_async_copy(hidden.at[part], hidden_in.at[part], sems.at[i]))
    for copy in copies:
        copy.start()
    copies[0].wait()
    copies[1].wait()
    row = lax.broadcasted_iota(jnp.int32, (RANK, slots), 0)
    stats = jnp.zeros((RANK, slots), F32)
    for base, factor in ((0, a_in_in), (3, a_out_in)):
        square = jnp.square(factor[...].astype(F32))
        rest = jnp.sum(jnp.sum(square, axis=1, keepdims=True), axis=0, keepdims=True)
        rest = jnp.broadcast_to(rest, (RANK, slots))
        for piece in range(3):
            part = rest.astype(BF).astype(F32)
            stats = jnp.where(row == base + piece, part, stats)
            rest = rest - part
    stats_out[...] = stats.astype(BF)
    for i in range(pieces):
        copies[2 + i].wait()
        part = slice(i * rows, (i + 1) * rows)
        low_out[:, part] = mm(a_in_in[...], hidden_in[part, :], 1, 1).astype(BF)


def pack_low_kernel(low, stats, out):
    slots = out.shape[2] // 2
    for device in range(out.shape[0]):
        chip = device // 2
        out[device, :, 0:slots] = low[:, chip * slots:(chip + 1) * slots]
        out[device, :, slots:] = stats[...]


def join_kernel(*refs):
    pieces, out = (refs[:-1], refs[-1])
    start = 0
    for piece in pieces:
        out[start:start + piece.shape[0], :] = piece[...]
        start += piece.shape[0]


def fold_of(slots, experts, capacity, source):
    column = lax.broadcasted_iota(jnp.int32, (slots, experts * capacity), 1)
    row = lax.broadcasted_iota(jnp.int32, (slots, experts * capacity), 0)
    return (row == source * capacity + lax.rem(column, capacity)).astype(BF)


def own_expert(experts, capacity):
    shape = (experts * RANK, experts * capacity)
    row = lax.div(lax.broadcasted_iota(jnp.int32, shape, 0), RANK)
    column = lax.div(lax.broadcasted_iota(jnp.int32, shape, 1), capacity)
    return row == column


def relative_experts(order_size, tokens, me):
    row = lax.broadcasted_iota(jnp.int32, (order_size, tokens), 0)
    return jnp.bitwise_xor(row, me).astype(F32)


def weights_of(where, order, own_meta, far_meta, lows, z_out, w_out):
    me, core = (where[0], where[1])
    experts, tokens = (lows.shape[0], own_meta.shape[1])
    slots = lows.shape[2] // 2
    capacity = slots // 2
    low = jnp.concatenate([lows[jnp.bitwise_xor(me, e)][:, 0:slots] for e in range(experts)], axis=0)
    own = own_expert(experts, capacity)
    expert = relative_experts(experts, tokens, me)
    earlier = (lax.broadcasted_iota(jnp.int32, (tokens, tokens), 0) < lax.broadcasted_iota(jnp.int32, (tokens, tokens), 1)).astype(BF)
    place = lax.broadcasted_iota(jnp.int32, (experts, capacity, tokens), 1).astype(F32)
    rows = []
    for s in range(2):
        meta = (own_meta if s == 0 else far_meta)[...].astype(F32)
        first = (meta[0:1] == expert).astype(F32)
        second = (meta[1:2] == expert).astype(F32)
        before = mm((first + second).astype(BF), earlier)
        gate = first * meta[2:3] + second * meta[3:4]
        spread = jnp.where(before[:, None, :] == place, gate[:, None, :], 0.0)
        weights = spread.reshape(experts * capacity, tokens).astype(BF)
        source = jnp.bitwise_xor(core, s)
        wide = mm(low, fold_of(slots, experts, capacity, source))
        wide = jnp.where(own, wide, 0.0).astype(BF)
        exact = mm(wide, weights)
        rows.append(exact.astype(BF))
        if s == 0:
            w_out[...] = weights
            ordered = jnp.concatenate([exact[e * RANK:(e + 1) * RANK] for e in order], axis=0)
            z_out[...] = ordered.T.astype(BF)
    return rows


def product_of(rows, own_in, far_in, here, keep, send):
    count, tokens = (keep.shape[0], rows[0].shape[1])
    groups = rows[0].shape[0] // (4 * RANK)
    for side, target in ((0, keep), (1, send)):
        first, second = (r.reshape(groups, 2, 2 * RANK, tokens)[:, side].reshape(count, tokens) for r in rows)
        total = mm(first, own_in[:, here]) + mm(second, far_in[:, here])
        target[...] = total.astype(target.dtype)


def token_copies(where, cot, packed, own_in, far_in, sems):
    half = own_in.shape[1]
    here = lanes(where[1] * half, half)
    copies = [pltpu.make_async_copy(cot.at[:, here], own_in, sems.at[0])]
    source = packed if packed.shape[1] == half else packed.at[:, here]
    copies.append(pltpu.make_async_copy(source, far_in, sems.at[1]))
    for copy in copies:
        copy.start()
    return copies


def partial_kernel(order, where, cot, packed, own_meta, far_meta, lows, z_out, w_out, *outs):
    keeps, sends = (outs[:CHUNKS], outs[CHUNKS:2 * CHUNKS])
    own_in, far_in, sems = outs[2 * CHUNKS:]
    copies = token_copies(where, cot, packed, own_in, far_in, sems)
    rows = weights_of(where, order, own_meta, far_meta, lows, z_out, w_out)
    for copy in copies:
        copy.wait()
    base = 0
    for keep, send in zip(keeps, sends):
        here = slice(base, base + keep.shape[1])
        base += keep.shape[1]
        product_of(rows, own_in, far_in, here, keep, send)


def fold_step_kernel(received, keep, *refs):
    sends, kept = (refs[received:-1], refs[-1])
    rows, width = keep.shape
    radix = 1 + len(sends)
    total = keep[...]
    for more in refs[:received]:
        total = total + more[...].astype(F32)
    total = total.reshape(rows // (2 * RANK * radix), radix, 2 * RANK, width)
    kept[...] = total[:, 0].reshape(kept.shape)
    for i, send in enumerate(sends):
        send[...] = total[:, i + 1].reshape(send.shape).astype(send.dtype)


def last_fold_kernel(keep, *refs):
    received, (kept, sent) = (refs[:-2], refs[-2:])
    total = keep[...]
    for more in received:
        total = total + more[...].astype(F32)
    kept[...] = total[0:RANK]
    sent[...] = total[RANK:]


def factor_half(flip, side, cot, z, factors, delta, scratch):
    tokens_in, table, result, sems = scratch
    pieces, tokens, cut = tokens_in.shape
    base = jnp.bitwise_xor(side, flip) * (pieces * cut)
    copies = []
    for piece in range(pieces):
        moves = [(cot.at[:, lanes(base + piece * cut, cut)], tokens_in.at[piece])]
        start = 0
        for factor in factors:
            size = factor.shape[0]
            source = factor.at[:, piece * cut:(piece + 1) * cut]
            moves.append((source, table.at[piece, start:start + size, :]))
            start += size
        copies.append([pltpu.make_async_copy(source, target, sems.at[piece, i]) for i, (source, target) in enumerate(moves)])
        for copy in copies[-1]:
            copy.start()
    coords = jnp.zeros((start, tokens), F32)
    writes = []
    for piece in range(pieces):
        for copy in copies[piece]:
            copy.wait()
        block = table[piece]
        result[piece] = mm(z[...], block).astype(BF)
        target = delta.at[:, lanes(base + piece * cut, cut)]
        writes.append(pltpu.make_async_copy(result.at[piece], target, sems.at[piece, len(factors) + 1]))
        writes[-1].start()
        coords = coords + mm(block, tokens_in[piece], 1, 1)
    return (coords, writes)


def near_kernel(where, cot, z, *refs):
    factors, (coords_out, delta), scratch = (refs[:-6], refs[-6:-4], refs[-4:])
    coords_out[...], copies = factor_half(0, where[2], cot, z, factors, delta, scratch)
    for copy in copies:
        copy.wait()


def far_kernel(order, where, cot, z, w, near, _, *refs):
    factors, (coords_out, delta), scratch = (refs[:-6], refs[-6:-4], refs[-4:])
    experts, _, slots = coords_out.shape
    capacity = slots // 4
    coords, copies = factor_half(1, where[2], cot, z, factors, delta, scratch)
    coords = coords + near[...]
    blocks = [order.index(e) * RANK for e in range(experts)]
    coords = jnp.concatenate([coords[b:b + RANK] for b in blocks], axis=0)
    high, low = split(coords)
    picked = mm(high, w[...], 1, 1) + mm(low, w[...], 1, 1)
    picked = jnp.where(own_expert(experts, capacity), picked, 0.0).astype(BF)
    fold = fold_of(slots, experts, capacity, lax.rem(where[0], 4))
    rows = mm(picked, fold, 1, 1).astype(coords_out.dtype)
    for e in range(experts):
        coords_out[jnp.bitwise_xor(where[0], e)] = rows[e * RANK:(e + 1) * RANK]
    for copy in copies:
        copy.wait()


def inverse_kernel(a_in, a_out, lows, inv_in, inv_out):
    experts, _, double = lows.shape
    stats = jnp.sum(lows[:, :, double // 2:].astype(F32), axis=0)
    row = lax.broadcasted_iota(jnp.int32, (RANK, RANK), 0)
    column = lax.broadcasted_iota(jnp.int32, (RANK, RANK), 1)
    eye = (row == column).astype(F32)
    works = []
    for base, factor in ((0, a_in), (3, a_out)):
        pieces = stats[base:base + 1, 0:1] + stats[base + 1:base + 2, 0:1]
        damp = (pieces + stats[base + 2:base + 3, 0:1]) / (float(RANK) * experts)
        gram = mm(factor[...], factor[...], 1, 1) + damp * eye
        works.append([gram, eye])
    for j in range(RANK):
        for work in works:
            gram, inverse = work
            pivot = 1.0 / gram[j:j + 1, j:j + 1]
            gram_row, inverse_row = (gram[j:j + 1] * pivot, inverse[j:j + 1] * pivot)
            scale = gram[:, j:j + 1]
            work[0] = jnp.where(row == j, gram_row, gram - scale * gram_row)
            work[1] = jnp.where(row == j, inverse_row, inverse - scale * inverse_row)
    inv_in[...] = works[0][1]
    inv_out[...] = works[1][1]


def scaled_in_kernel(coords, hidden, inverse, out):
    pieces = []
    for base in range(0, coords.shape[0], 4):
        total = coords[base].astype(F32)
        for q in range(1, 4):
            total = total + coords[base + q].astype(F32)
        pieces.append(total)
    grad_low = jnp.concatenate(pieces, axis=1).astype(BF)
    out[...] = mm(inverse[...], mm(grad_low, hidden[...]), precision=HIGHEST)


def scaled_out_kernel(where, inverse, *refs):
    pieces, (out, rows, sems) = (refs[:-3], refs[-3:])
    half = out.shape[1] // 2
    copies, starts = ([], [0, 0])
    for i, piece in enumerate(pieces):
        flip, width = (i % 2, piece.shape[1])
        base = jnp.bitwise_xor(where[1], flip) * half + starts[flip]
        starts[flip] += width
        rows[i, :, 0:width] = mm(inverse[...], piece[...], precision=HIGHEST)
        target = out.at[:, lanes(base, width)]
        copies.append(pltpu.make_async_copy(rows.at[i, :, 0:width], target, sems.at[i]))
        copies[-1].start()
    for copy in copies:
        copy.wait()


def radix_groups(experts, most):
    groups, bit = ([], 4)
    while bit < experts:
        radix = min(most, experts // bit)
        groups.append([bit * k for k in range(1, radix)])
        bit *= radix
    return groups


def relative_order(bits):
    order = [0]
    for bit in bits:
        order = order + [e ^ bit for e in order]
    return order


def on_device(hidden_slots, adapter_in, adapter_out, expert_ids, gate_weights, cotangent):
    experts, groups = (lax.axis_size('expert'), lax.axis_size('group'))
    me, group = (lax.axis_index('expert'), lax.axis_index('group'))
    where = jnp.stack([me, me % 2, group % 2]).astype(jnp.int32)
    hidden, a_in, a_out = (hidden_slots[0], adapter_in[0], adapter_out[0])
    width = a_out.shape[1]
    half = width // 2
    tokens = cotangent.shape[0]
    capacity = hidden.shape[0] // experts
    struct = jax.ShapeDtypeStruct

    def swap(x, bit):
        return lax.ppermute(x, 'expert', [(i, i ^ bit) for i in range(experts)])

    def swap_side(x):
        return lax.ppermute(x, 'group', [(i, i ^ 1) for i in range(groups)])

    def spread(x):
        return lax.all_to_all(x, 'expert', split_axis=0, concat_axis=0, tiled=True)
    groups_z = radix_groups(experts, 4)
    groups_of = [radix_groups(experts, 2 if 0 & 1 << p else 4) for p in range(2)]
    far_bits = [1 << i for i in reversed(range(2, experts.bit_length() - 1))]
    full = relative_order([2, *far_bits, 1])
    block = jnp.where(group % 2 == 0, a_out[:, :half], a_out[:, half:])
    received = swap(block, 2)
    low, stats = call(low_rank_kernel, [struct((RANK, hidden.shape[0]), BF), struct((RANK, 2 * capacity), BF)], [hidden, a_in, a_out], scratch=[VMEM(hidden.shape, BF), VMEM(a_in.shape, BF), VMEM(a_out.shape, BF), DMA((6,))], spaces=[HBM] * 3, limit=63 * MIB)
    far_tokens = swap(cotangent, 1)
    own_meta = jnp.concatenate([expert_ids.T.astype(BF), gate_weights.T.astype(BF), jnp.zeros((12, tokens), BF)], axis=0)
    far_meta = swap(own_meta, 1)
    block, = call(join_kernel, [struct((2 * RANK, half), BF)], [block, received], after=[low])
    lows, = call(pack_low_kernel, [struct((experts, RANK, 4 * capacity), BF)], [low, stats], after=[block])
    lows = spread(lows)
    inv_in, inv_out = call(inverse_kernel, [struct((RANK, RANK), F32)] * 2, [a_in, a_out, lows])
    count = experts * RANK // 2

    def planes_of(block, gate):
        for bit in far_bits:
            received = swap(block, bit)
            if bit == far_bits[-1]:
                return ([block, received], last)
            last = [block, received]
            block, = call(join_kernel, [struct((2 * block.shape[0], half), BF)], last, after=gate)
    gate_inv = []
    early = []
    near, last = planes_of(block, [lows] + gate_inv)
    early = [near[0]]
    tiles = half // 128
    wides = [128 * (tiles * 14 // 28), half - 128 * (tiles * 14 // 28)]
    token_args = [cotangent, far_tokens, own_meta, far_meta, lows]
    token_scratch = [VMEM((tokens, half), BF), VMEM((tokens, half), BF), DMA((2,))]
    shapes = [struct((tokens, experts * RANK), BF), struct((experts * capacity, tokens), BF)]
    far_space = pl.ANY
    z, weights, *parts = call(lambda *refs: partial_kernel(full, *refs), shapes + [struct((count, wide), F32) for wide in wides] + [struct((count, wide), BF) for wide in wides], token_args, where, after=early, scratch=token_scratch, spaces=[HBM, far_space, VMEM, VMEM, VMEM])
    kept, sent = (parts[:CHUNKS], parts[CHUNKS:])

    def fold_y(piece, gate):
        group = groups_of[piece][0]
        wide = wides[piece]
        rows = count // (1 + len(group))
        return list(call(lambda keep, *refs: fold_step_kernel(1, keep, *refs), [struct((rows, wide), BF)] * len(group) + [struct((rows, wide), F32)], [kept[piece], swap(sent[piece], 2)], after=gate))
    far = [swap_side(near[0])]
    fold_a = []
    gate = [sent[0], inv_in]
    gate = gate + [far[-1]]
    near[1:] = call(join_kernel, [struct(near[1].shape, BF)], [near[1]], after=gate)
    factors = list(near)
    far.append(swap_side(near[1]))
    factors += [swap(block, 1) for block in near]
    far += [swap(block, 1) for block in far]
    cuts = 2
    scratch = [VMEM((cuts, tokens, half // cuts), BF), VMEM((cuts, experts * RANK, half // cuts), BF), VMEM((cuts, tokens, half // cuts), BF), DMA((cuts, 2 * len(far) + 2))]
    near_coords, delta = call(near_kernel, [struct((experts * RANK, tokens), F32), struct((tokens, width), BF)], [cotangent, z, *factors], where, after=[], scratch=scratch, spaces=[HBM, VMEM] + [HBM] * len(factors), out_spaces=[VMEM, HBM])
    own_rows, far_rows, ends = ([], [], [])
    gates_b = {0: [], 1: [near_coords], 2: [near_coords, far[len(far) // 2 - 1]], 3: [near_coords, far[-1]], 4: [inv_in], 5: [far[len(far) // 2 - 1]], 6: [near_coords, inv_in]}
    folds = [fold_a, fold_y(1, gates_b[2])]
    for piece in range(CHUNKS):
        rows, wide = (count, wides[piece])
        keep = kept[piece]
        for n, group in enumerate(groups_of[piece]):
            radix = 1 + len(group)
            rows //= radix
            if n == 0 and folds[piece]:
                *sends, keep = folds[piece]
            else:
                total = keep
                for more in received if n else [swap(sent[piece], 2)]:
                    total = total + more.astype(F32)
                total = total.reshape(rows // (2 * RANK), radix, 2 * RANK, wide)
                keep = total[:, 0].reshape(rows, wide)
                sends = [total[:, k].reshape(rows, wide).astype(BF) for k in range(1, radix)]
            received = [swap(send, k) for send, k in zip(sends, group)]
        ends.append((keep, received))
        if piece == 0:
            for more in received:
                keep = keep + more.astype(F32)
            own_rows.append(keep[:RANK])
            far_rows.append(swap(keep[RANK:], 1))
    gate_far = [[], [folds[1][-1]], [own_rows[0]], [folds[1][-1], own_rows[0]]][0]
    coords, delta = call(lambda *refs: far_kernel(full, *refs), [struct((experts, RANK, 4 * capacity), BF), struct((tokens, width), BF)], [cotangent, z, weights, near_coords, delta, *far], where, after=gate_far, scratch=scratch, spaces=[HBM, VMEM, VMEM, VMEM, HBM] + [HBM] * len(far), out_spaces=[VMEM, HBM], alias={5: 1})
    keep, received = ends[1]
    keep, send = call(last_fold_kernel, [struct((RANK, wides[1]), F32)] * 2, [keep, *received], after=[coords])
    own_rows.append(keep)
    far_rows.append(swap(send, 1))
    coords = spread(coords)
    pieces = [rows for pair in zip(own_rows, far_rows) for rows in pair]
    scaled_out, = call(scaled_out_kernel, [struct((RANK, width), F32)], [inv_in, *pieces], where, scratch=[VMEM((len(pieces), RANK, max(wides)), F32), DMA((len(pieces),))], out_spaces=[HBM])
    scaled_in, = call(scaled_in_kernel, [struct((RANK, hidden.shape[1]), F32)], [coords, hidden, inv_out])
    return (delta, scaled_in[None], scaled_out[None])


def solution(mesh):
    every = ('group', 'expert')
    return jax.shard_map(on_device, mesh=mesh, in_specs=(P(every, None, None), P('expert', None, None), P('expert', None, None), P(every, None), P(every, None), P(every, None)), out_specs=(P(every, None), P(every, None, None), P(every, None, None)), check_vma=False)
```

time: 78.1 us -> 75.4 us (0.965)
  local copies, waits for them, and re-layouts: 4.93 us -> 1.73 us
  waiting for transfers between devices: 20 us -> 22 us
  Pallas kernels: 19.2 us -> 18.1 us
    dynamic_slice x2 -> x0, local copies, waits for them, and re-layouts: 2.26 us -> none  [the longest x1 2.25 us: on_device(): lax.dynamic_slice_in_dim(cotangent, (1 - me % 2) * half, half, axis=1)]
    ppermute x19, waiting for transfers between devices: 9.59 us -> 11.4 us  [swap(): return lax.ppermute(x, 'expert', [(i, i ^ bit) for i in range(experts)])]
    all_to_all x2, waiting for transfers between devices: 8.28 us -> 9.62 us  [spread(): return lax.all_to_all(x, 'expert', split_axis=0, concat_axis=0, tiled=True)]
    all_to_all x2, starting transfers between devices: 9.04 us -> 7.9 us  [spread(): return lax.all_to_all(x, 'expert', split_axis=0, concat_axis=0, tiled=True)]
    ppermute x2, waiting for transfers between devices: 2.11 us -> 0.98 us  [swap_side(): return lax.ppermute(x, 'group', [(i, i ^ 1) for i in range(groups)])]
    pallas_call x13, Pallas kernels: 19.2 us -> 18.1 us  [call(): pl.pallas_call(body, out_shape=[jax.ShapeDtypeStruct(o.shape, o.dtype) fo...]
    select_n x0 -> x1, other arithmetic: none -> 0.97 us  [on_device(): block = jnp.where(group % 2 == 0, a_out[:, :half], a_out[:, half:])]
    slice x1, local copies, waits for them, and re-layouts: 0.97 us -> 0.02 us  [on_device(): far_rows.append(swap(keep[RANK:], 1))]
  transfers between devices with their start and end apart: 23 -> 23, of which waited for: 7 -> 11; matrix products, arithmetic and copies ran while one was open for 3% -> 2% of each run, Pallas kernels for 23% -> 22%
where the time goes in v5:
time: 75.4 us; the launch traced here: 75 us
  starting transfers between devices  30.9 us (41%)
  waiting for transfers between devices  22 us (29%)
  Pallas kernels  18.1 us (24%)
  local copies, waits for them, and re-layouts  1.73 us (2%)
  other arithmetic  1.33 us (2%)
  between operations  0.87 us (1%)
    ppermute x19, starting transfers between devices, swap(): return lax.ppermute(x, 'expert', [(i, i ^ bit) for i in range(experts)])  20 us
    pallas_call x13, Pallas kernels, call(): pl.pallas_call(body, out_shape=[jax.ShapeDtypeStruct(o.shape, o.dtype) fo...  18.1 us
    ppermute x19, waiting for transfers between devices, swap(): return lax.ppermute(x, 'expert', [(i, i ^ bit) for i in range(experts)])  11.4 us
    all_to_all x2, waiting for transfers between devices, spread(): return lax.all_to_all(x, 'expert', split_axis=0, concat_axis=0, tiled=True)  9.62 us
    all_to_all x2, starting transfers between devices, spread(): return lax.all_to_all(x, 'expert', split_axis=0, concat_axis=0, tiled=True)  7.9 us
    ppermute x2, starting transfers between devices, swap_side(): return lax.ppermute(x, 'group', [(i, i ^ 1) for i in range(groups)])  3.05 us
    unnamed x16, local copies, waits for them, and re-layouts  1.61 us
  transfers between devices with their start and end apart: 23, of which 11 were waited for; matrix products, arithmetic and copies ran while one was open for 2% of the time, Pallas kernels for 22%

profile of v5, /device:TPU:0, one launch (start us, length us, event | category | flops | bytes accessed | tf_op | source)
XLA Modules:
  0.0 75.0 jit_solution(14967661491037558948)
XLA Ops:
  2.1 2.6 %collective-permute-start.2 = (bf16[16,3584]{1,0:T(8,128)(2,1)S(1)}, bf16[16,3584]{1,0:T(8,128)(2,1)S(1)}, u32[]{:S(2)}, u32[]{:S(2)}) collective-permute-start(bf16[16,3584]{1,0:T(8,128)(2,1)S(1)} %slice_select_fusion.refs_0_), channel_id=1, source_target_pairs={{0,2},{1,3},{2,0},{3,1},{4,6},{5,7},{6,4},{7,5},{8,10},{9,11},{10,... | collective-permute-start | bytes 344072 | tf_op jit(solution)/shard_map/ppermute | solution.py:332
  4.8 3.4 %shard_map.85 = (bf16[16,512]{1,0:T(8,128)(2,1)}, bf16[16,64]{1,0:T(8,128)(2,1)}) custom-call(bf16[512,2048]{1,0:T(8,128)(2,1)} %bitcast.27, bf16[16,2048]{1,0:T(8,128)(2,1)} %bitcast.32, bf16[16,7168]{1,0:T(8,128)(2,1)} %bitcast.30), custom_call_target="tpu_custom_call" | custom-call | bytes 2410496 | tf_op jit(solution)/shard_map/pallas_call | solution.py:35
  9.5 2.7 %collective-permute-start.3 = (bf16[32,3584]{1,0:T(8,128)(2,1)S(1)}, bf16[32,3584]{1,0:T(8,128)(2,1)S(1)}, u32[]{:S(2)}, u32[]{:S(2)}) collective-permute-start(bf16[32,3584]{1,0:T(8,128)(2,1)S(1)} %shard_map.86.refs_2_.refs_0_), channel_id=1, source_target_pairs={{0,8},{1,9},{2,10},{3,11},{4,12},{5,13},{6,14},{7,15},{8,0},{9,1},... | collective-permute-start | bytes 688136 | tf_op jit(solution)/shard_map/ppermute | solution.py:332
  13.7 3.9 %all-to-all-start = ((bf16[16,16,128]{2,1,0:T(8,128)(2,1)}), bf16[16,16,128]{2,1,0:T(8,128)(2,1)S(1)}, u32[]{:S(2)}, u32[]{:S(2)}) async-start(bf16[16,16,128]{2,1,0:T(8,128)(2,1)} %shard_map.87), calls=%async_computation | async-start | bytes 131072 | tf_op jit(solution)/shard_map/all_to_all | solution.py:338
  18.1 6.5 %all-to-all-done.refs_2_.refs_5_ = bf16[16,16,128]{2,1,0:T(8,128)(2,1)S(1)} async-done(((bf16[16,16,128]{2,1,0:T(8,128)(2,1)}), bf16[16,16,128]{2,1,0:T(8,128)(2,1)S(1)}, u32[]{:S(2)}, u32[]{:S(2)}) %all-to-all-start) | async-done | bytes 65568 | tf_op jit(solution)/shard_map/all_to_all | solution.py:338
  25.4 1.5 %collective-permute-start.5 = (bf16[64,3584]{1,0:T(8,128)(2,1)S(1)}, bf16[64,3584]{1,0:T(8,128)(2,1)S(1)}, u32[]{:S(2)}, u32[]{:S(2)}) collective-permute-start(bf16[64,3584]{1,0:T(8,128)(2,1)S(1)} %shard_map.88.refs_6_.refs_3_), channel_id=1, source_target_pairs={{0,16},{16,0},{1,17},{17,1},{2,18},{18,2},{3,19},{19,3},{4,20},{20... | collective-permute-start | bytes 1376264 | tf_op jit(solution)/shard_map/ppermute | solution.py:335
  27.0 3.2 %shard_map.89 = (bf16[128,256]{1,0:T(8,128)(2,1)S(1)}, bf16[512,128]{1,0:T(8,128)(2,1)S(1)}, f32[128,1792]{1,0:T(8,128)S(1)}, f32[128,1792]{1,0:T(8,128)S(1)}, b...) custom-call(s32[3]{0:T(128)S(1)} %pad_add_fusion.refs_0_, bf16[128,7168]{1,0:T(8,128)(2,1)S(1)} %copy-done, ...), custom_call_target="tpu_custom_call" | custom-call | bytes 6692864 | tf_op jit(solution)/shard_map/pallas_call | solution.py:35
  31.1 1.6 %shard_map.90 = (f32[16,16]{1,0:T(8,128)S(1)}, f32[16,16]{1,0:T(8,128)S(1)}) custom-call(bf16[16,2048]{1,0:T(8,128)(2,1)S(1)} %bitcast.33, bf16[16,7168]{1,0:T(8,128)(2,1)S(1)} %bitcast.31, bf16[16,16,128]{2,1,0:T(8,128)(2,1)S(1)} %all-to-all-done.refs_2_.refs_5_), custom_call_target="tpu_custom_call" | custom-call | bytes 362496 | tf_op jit(solution)/shard_map/pallas_call | solution.py:35
  32.8 4.5 %collective-permute-done.4.refs_0_ = bf16[64,3584]{1,0:T(8,128)(2,1)S(1)} collective-permute-done((bf16[64,3584]{1,0:T(8,128)(2,1)S(1)}, bf16[64,3584]{1,0:T(8,128)(2,1)S(1)}, u32[]{:S(2)}, u32[]{:S(2)}) %collective-permute-start.4) | collective-permute-done | bytes 458784 | tf_op jit(solution)/shard_map/ppermute | solution.py:332
  37.8 1.6 %collective-permute-start.8 = (bf16[64,3584]{1,0:T(8,128)(2,1)S(1)}, bf16[64,3584]{1,0:T(8,128)(2,1)S(1)}, u32[]{:S(2)}, u32[]{:S(2)}) collective-permute-start(bf16[64,3584]{1,0:T(8,128)(2,1)S(1)} %shard_map.91.refs_4_), channel_id=1, source_target_pairs={{0,16},{16,0},{1,17},{17,1},{2,18},{18,2},{3,19},{19,3},{4,20},{20... | collective-permute-start | bytes 1376264 | tf_op jit(solution)/shard_map/ppermute | solution.py:335
  40.1 2.2 %collective-permute-done.11 = bf16[128,1792]{1,0:T(8,128)(2,1)S(1)} collective-permute-done((bf16[128,1792]{1,0:T(8,128)(2,1)S(1)}, bf16[128,1792]{1,0:T(8,128)(2,1)S(1)}, u32[]{:S(2)}, u32[]{:S(2)}) %collective-permute-start.11) | collective-permute-done | bytes 458784 | tf_op jit(solution)/shard_map/ppermute | solution.py:332
  42.5 1.4 %collective-permute-start.12 = (bf16[32,1792]{1,0:T(8,128)(2,1)S(1)}, bf16[32,1792]{1,0:T(8,128)(2,1)S(1)}, u32[]{:S(2)}, u32[]{:S(2)}) collective-permute-start(bf16[32,1792]{1,0:T(8,128)(2,1)S(1)} %get-tuple-element.43), channel_id=1, source_target_pairs={{0,4},{1,5},{2,6},{3,7},{4,0},{5,1},{6,2},{7,3},{8,12},{9,13},{10,... | collective-permute-start | bytes 344072 | tf_op jit(solution)/shard_map/ppermute | solution.py:332
  44.0 2.5 %collective-permute-start.13 = (bf16[32,1792]{1,0:T(8,128)(2,1)S(1)}, bf16[32,1792]{1,0:T(8,128)(2,1)S(1)}, u32[]{:S(2)}, u32[]{:S(2)}) collective-permute-start(bf16[32,1792]{1,0:T(8,128)(2,1)S(1)} %get-tuple-element.45), channel_id=1, source_target_pairs={{0,8},{1,9},{2,10},{3,11},{4,12},{5,13},{6,14},{7,15},{8,0},{9,1},... | collective-permute-start | bytes 344072 | tf_op jit(solution)/shard_map/ppermute | solution.py:332
  47.5 2.5 %shard_map.92 = (f32[256,128]{1,0:T(8,128)S(1)}, bf16[128,7168]{1,0:T(8,128)(2,1)}) custom-call(s32[3]{0:T(128)S(1)} %pad_add_fusion.refs_0_, bf16[128,7168]{1,0:T(8,128)(2,1)S(1)} %copy-done, bf16[128,256]{1,0:T(8,128)(2,1)S(1)} %get-tuple-element.25.refs_2_, bf16[64,3584]{1,0:T(8,128)(2,1)S(1)} %shard_map.88.refs_6_.refs_3_, ...), custom_call_target="tpu_custom_call" | custom-call | bytes 5701632 | tf_op jit(solution)/shard_map/pallas_call | solution.py:35
  50.7 1.4 %collective-permute-done.16.refs_1_ = bf16[128,1792]{1,0:T(8,128)(2,1)S(1)} collective-permute-done((bf16[128,1792]{1,0:T(8,128)(2,1)S(1)}, bf16[128,1792]{1,0:T(8,128)(2,1)S(1)}, u32[]{:S(2)}, u32[]{:S(2)}) %collective-permute-start.16) | collective-permute-done | bytes 458784 | tf_op jit(solution)/shard_map/ppermute | solution.py:332
  52.1 1.4 %collective-permute-start.17 = (bf16[32,1792]{1,0:T(8,128)(2,1)S(1)}, bf16[32,1792]{1,0:T(8,128)(2,1)S(1)}, u32[]{:S(2)}, u32[]{:S(2)}) collective-permute-start(bf16[32,1792]{1,0:T(8,128)(2,1)S(1)} %get-tuple-element.38), channel_id=1, source_target_pairs={{0,4},{1,5},{2,6},{3,7},{4,0},{5,1},{6,2},{7,3},{8,12},{9,13},{10,... | collective-permute-start | bytes 344072 | tf_op jit(solution)/shard_map/ppermute | solution.py:332
  53.6 2.5 %collective-permute-start.18 = (bf16[32,1792]{1,0:T(8,128)(2,1)S(1)}, bf16[32,1792]{1,0:T(8,128)(2,1)S(1)}, u32[]{:S(2)}, u32[]{:S(2)}) collective-permute-start(bf16[32,1792]{1,0:T(8,128)(2,1)S(1)} %get-tuple-element.39), channel_id=1, source_target_pairs={{0,8},{1,9},{2,10},{3,11},{4,12},{5,13},{6,14},{7,15},{8,0},{9,1},... | collective-permute-start | bytes 344072 | tf_op jit(solution)/shard_map/ppermute | solution.py:332
  56.1 1.5 %collective-permute-start.19 = (bf16[32,1792]{1,0:T(8,128)(2,1)S(1)}, bf16[32,1792]{1,0:T(8,128)(2,1)S(1)}, u32[]{:S(2)}, u32[]{:S(2)}) collective-permute-start(bf16[32,1792]{1,0:T(8,128)(2,1)S(1)} %get-tuple-element.40), channel_id=1, source_target_pairs={{0,12},{1,13},{2,14},{3,15},{4,8},{5,9},{6,10},{7,11},{8,4},{9,5},... | collective-permute-start | bytes 344072 | tf_op jit(solution)/shard_map/ppermute | solution.py:332
  57.7 1.7 %collective-permute-done.10.refs_9_ = bf16[64,3584]{1,0:T(8,128)(2,1)S(1)} collective-permute-done((bf16[64,3584]{1,0:T(8,128)(2,1)S(1)}, bf16[64,3584]{1,0:T(8,128)(2,1)S(1)}, u32[]{:S(2)}, u32[]{:S(2)}) %collective-permute-start.10) | collective-permute-done | bytes 458784 | tf_op jit(solution)/shard_map/ppermute | solution.py:332
  59.5 3.4 %shard_map.93 = (bf16[16,16,128]{2,1,0:T(8,128)(2,1)}, bf16[128,7168]{1,0:T(8,128)(2,1)}) custom-call(s32[3]{0:T(128)S(1)} %pad_add_fusion.refs_0_, bf16[128,7168]{1,0:T(8,128)(2,1)S(1)} %copy-done, bf16[128,256]{1,0:T(8,128)(2,1)S(1)} %get-tuple-element.25.refs_2_, bf16[512,128]{1,0:T(8,128)(2,1)S(1)} %get-tuple-element.26.refs_3_, ...), custom_call_target="tpu_custom_call", output_to_operand_aliasing={{1}: (5, {})} | custom-call | bytes 7733248 | tf_op jit(solution)/shard_map/pallas_call | solution.py:35
  62.8 4.0 %all-to-all-start.1 = ((bf16[16,16,128]{2,1,0:T(8,128)(2,1)}), bf16[16,16,128]{2,1,0:T(8,128)(2,1)S(1)}, u32[]{:S(2)}, u32[]{:S(2)}) async-start(bf16[16,16,128]{2,1,0:T(8,128)(2,1)} %get-tuple-element.32.refs_4_), calls=%async_computation.1 | async-start | bytes 131072 | tf_op jit(solution)/shard_map/all_to_all | solution.py:338
  68.8 1.9 %shard_map.97 = f32[16,7168]{1,0:T(8,128)} custom-call(s32[3]{0:T(128)S(1)} %pad_add_fusion.refs_0_, f32[16,16]{1,0:T(8,128)S(1)} %get-tuple-element.28.refs_2_.refs_1_, f32[16,1792]{1,0:T(8,128)S(1)} %get-tuple-element.47.refs_2_, f32[16,1792]{1,0:T(8,128)S(1)} %collective-permute-done.15.refs_3_, f32[16,1792]{1,0:T(8,128)S(1)} %get-tuple-element.41.refs_4_, ...), custom_call_target="tpu_custom_call" | custom-call | bytes 918528 | tf_op jit(solution)/shard_map/pallas_call | solution.py:35
  70.7 3.1 %all-to-all-done.1.refs_0_ = bf16[16,16,128]{2,1,0:T(8,128)(2,1)S(1)} async-done(((bf16[16,16,128]{2,1,0:T(8,128)(2,1)}), bf16[16,16,128]{2,1,0:T(8,128)(2,1)S(1)}, u32[]{:S(2)}, u32[]{:S(2)}) %all-to-all-start.1) | async-done | bytes 65568 | tf_op jit(solution)/shard_map/all_to_all | solution.py:338
  73.7 1.2 %shard_map.94 = f32[16,2048]{1,0:T(8,128)} custom-call(bf16[16,16,128]{2,1,0:T(8,128)(2,1)S(1)} %all-to-all-done.1.refs_0_, bf16[512,2048]{1,0:T(8,128)(2,1)S(1)} %bitcast.28, f32[16,16]{1,0:T(8,128)S(1)} %get-tuple-element.33.refs_2_), custom_call_target="tpu_custom_call" | custom-call | bytes 2294784 | tf_op jit(solution)/shard_map/pallas_call | solution.py:35
  (63 shorter events, 11.8 us)
Async XLA Ops:
  0.7 26.3 %collective-permute-start = (bf16[128,7168]{1,0:T(8,128)(2,1)}, bf16[128,7168]{1,0:T(8,128)(2,1)}, u32[]{:S(2)}, u32[]{:S(2)}) collective-permute-start(bf16[128,7168]{1,0:T(8,128)(2,1)} %refs_1_.5), channel_id=1, source_target_pairs={{0,1},{1,0},{2,3},{3,2},{4,5},{5,4},{6,7},{7,6},{8,9},{9,8},{10,11... | collective-permute-start | bytes 5505032 | tf_op jit(solution)/shard_map/ppermute | solution.py:332
  2.1 6.4 %collective-permute-start.2 = (bf16[16,3584]{1,0:T(8,128)(2,1)S(1)}, bf16[16,3584]{1,0:T(8,128)(2,1)S(1)}, u32[]{:S(2)}, u32[]{:S(2)}) collective-permute-start(bf16[16,3584]{1,0:T(8,128)(2,1)S(1)} %slice_select_fusion.refs_0_), channel_id=1, source_target_pairs={{0,2},{1,3},{2,0},{3,1},{4,6},{5,7},{6,4},{7,5},{8,10},{9,11},{10,... | collective-permute-start | bytes 344072 | tf_op jit(solution)/shard_map/ppermute | solution.py:332
  8.2 18.8 %copy-start = (bf16[128,7168]{1,0:T(8,128)(2,1)S(1)}, bf16[128,7168]{1,0:T(8,128)(2,1)}, u32[]{:S(2)}) copy-start(bf16[128,7168]{1,0:T(8,128)(2,1)} %refs_1_.5) | copy-start | bytes 5505028
  9.5 15.2 %collective-permute-start.3 = (bf16[32,3584]{1,0:T(8,128)(2,1)S(1)}, bf16[32,3584]{1,0:T(8,128)(2,1)S(1)}, u32[]{:S(2)}, u32[]{:S(2)}) collective-permute-start(bf16[32,3584]{1,0:T(8,128)(2,1)S(1)} %shard_map.86.refs_2_.refs_0_), channel_id=1, source_target_pairs={{0,8},{1,9},{2,10},{3,11},{4,12},{5,13},{6,14},{7,15},{8,0},{9,1},... | collective-permute-start | bytes 688136 | tf_op jit(solution)/shard_map/ppermute | solution.py:332
  13.7 11.0 %all-to-all-start = ((bf16[16,16,128]{2,1,0:T(8,128)(2,1)}), bf16[16,16,128]{2,1,0:T(8,128)(2,1)S(1)}, u32[]{:S(2)}, u32[]{:S(2)}) async-start(bf16[16,16,128]{2,1,0:T(8,128)(2,1)} %shard_map.87), calls=%async_computation | async-start | bytes 131072 | tf_op jit(solution)/shard_map/all_to_all | solution.py:338
  17.7 9.3 %collective-permute-start.1 = (bf16[16,128]{1,0:T(8,128)(2,1)S(1)}, bf16[16,128]{1,0:T(8,128)(2,1)S(1)}, u32[]{:S(2)}, u32[]{:S(2)}) collective-permute-start(bf16[16,128]{1,0:T(8,128)(2,1)S(1)} %maximum_maximum_fusion.refs_3_), channel_id=1, source_target_pairs={{0,1},{1,0},{2,3},{3,2},{4,5},{5,4},{6,7},{7,6},{8,9},{9,8},{10,11... | collective-permute-start | bytes 12296 | tf_op jit(solution)/shard_map/ppermute | solution.py:332
  24.7 12.6 %collective-permute-start.4 = (bf16[64,3584]{1,0:T(8,128)(2,1)S(1)}, bf16[64,3584]{1,0:T(8,128)(2,1)S(1)}, u32[]{:S(2)}, u32[]{:S(2)}) collective-permute-start(bf16[64,3584]{1,0:T(8,128)(2,1)S(1)} %shard_map.88.refs_6_.refs_3_), channel_id=1, source_target_pairs={{0,4},{1,5},{2,6},{3,7},{4,0},{5,1},{6,2},{7,3},{8,12},{9,13},{10,... | collective-permute-start | bytes 1376264 | tf_op jit(solution)/shard_map/ppermute | solution.py:332
  25.4 12.3 %collective-permute-start.5 = (bf16[64,3584]{1,0:T(8,128)(2,1)S(1)}, bf16[64,3584]{1,0:T(8,128)(2,1)S(1)}, u32[]{:S(2)}, u32[]{:S(2)}) collective-permute-start(bf16[64,3584]{1,0:T(8,128)(2,1)S(1)} %shard_map.88.refs_6_.refs_3_), channel_id=1, source_target_pairs={{0,16},{16,0},{1,17},{17,1},{2,18},{18,2},{3,19},{19,3},{4,20},{20... | collective-permute-start | bytes 1376264 | tf_op jit(solution)/shard_map/ppermute | solution.py:335
  30.2 12.1 %collective-permute-start.11 = (bf16[128,1792]{1,0:T(8,128)(2,1)S(1)}, bf16[128,1792]{1,0:T(8,128)(2,1)S(1)}, u32[]{:S(2)}, u32[]{:S(2)}) collective-permute-start(bf16[128,1792]{1,0:T(8,128)(2,1)S(1)} %get-tuple-element.27.refs_1_), channel_id=1, source_target_pairs={{0,2},{1,3},{2,0},{3,1},{4,6},{5,7},{6,4},{7,5},{8,10},{9,11},{10,... | collective-permute-start | bytes 1376264 | tf_op jit(solution)/shard_map/ppermute | solution.py:332
  32.7 11.3 %collective-permute-start.6 = (bf16[64,3584]{1,0:T(8,128)(2,1)S(1)}, bf16[64,3584]{1,0:T(8,128)(2,1)S(1)}, u32[]{:S(2)}, u32[]{:S(2)}) collective-permute-start(bf16[64,3584]{1,0:T(8,128)(2,1)S(1)} %shard_map.88.refs_6_.refs_3_), channel_id=1, source_target_pairs={{0,1},{1,0},{2,3},{3,2},{4,5},{5,4},{6,7},{7,6},{8,9},{9,8},{10,11... | collective-permute-start | bytes 1376264 | tf_op jit(solution)/shard_map/ppermute | solution.py:332
  37.7 8.8 %collective-permute-start.7 = (bf16[64,3584]{1,0:T(8,128)(2,1)S(1)}, bf16[64,3584]{1,0:T(8,128)(2,1)S(1)}, u32[]{:S(2)}, u32[]{:S(2)}) collective-permute-start(bf16[64,3584]{1,0:T(8,128)(2,1)S(1)} %shard_map.91.refs_4_), channel_id=1, source_target_pairs={{0,1},{1,0},{2,3},{3,2},{4,5},{5,4},{6,7},{7,6},{8,9},{9,8},{10,11... | collective-permute-start | bytes 1376264 | tf_op jit(solution)/shard_map/ppermute | solution.py:332
  37.8 12.9 %collective-permute-start.8 = (bf16[64,3584]{1,0:T(8,128)(2,1)S(1)}, bf16[64,3584]{1,0:T(8,128)(2,1)S(1)}, u32[]{:S(2)}, u32[]{:S(2)}) collective-permute-start(bf16[64,3584]{1,0:T(8,128)(2,1)S(1)} %shard_map.91.refs_4_), channel_id=1, source_target_pairs={{0,16},{16,0},{1,17},{17,1},{2,18},{18,2},{3,19},{19,3},{4,20},{20... | collective-permute-start | bytes 1376264 | tf_op jit(solution)/shard_map/ppermute | solution.py:335
  39.3 12.7 %collective-permute-start.16 = (bf16[128,1792]{1,0:T(8,128)(2,1)S(1)}, bf16[128,1792]{1,0:T(8,128)(2,1)S(1)}, u32[]{:S(2)}, u32[]{:S(2)}) collective-permute-start(bf16[128,1792]{1,0:T(8,128)(2,1)S(1)} %get-tuple-element.36), channel_id=1, source_target_pairs={{0,2},{1,3},{2,0},{3,1},{4,6},{5,7},{6,4},{7,5},{8,10},{9,11},{10,... | collective-permute-start | bytes 1376264 | tf_op jit(solution)/shard_map/ppermute | solution.py:332
  42.5 11.1 %collective-permute-start.12 = (bf16[32,1792]{1,0:T(8,128)(2,1)S(1)}, bf16[32,1792]{1,0:T(8,128)(2,1)S(1)}, u32[]{:S(2)}, u32[]{:S(2)}) collective-permute-start(bf16[32,1792]{1,0:T(8,128)(2,1)S(1)} %get-tuple-element.43), channel_id=1, source_target_pairs={{0,4},{1,5},{2,6},{3,7},{4,0},{5,1},{6,2},{7,3},{8,12},{9,13},{10,... | collective-permute-start | bytes 344072 | tf_op jit(solution)/shard_map/ppermute | solution.py:332
  44.0 12.1 %collective-permute-start.13 = (bf16[32,1792]{1,0:T(8,128)(2,1)S(1)}, bf16[32,1792]{1,0:T(8,128)(2,1)S(1)}, u32[]{:S(2)}, u32[]{:S(2)}) collective-permute-start(bf16[32,1792]{1,0:T(8,128)(2,1)S(1)} %get-tuple-element.45), channel_id=1, source_target_pairs={{0,8},{1,9},{2,10},{3,11},{4,12},{5,13},{6,14},{7,15},{8,0},{9,1},... | collective-permute-start | bytes 344072 | tf_op jit(solution)/shard_map/ppermute | solution.py:332
  46.5 11.2 %collective-permute-start.14 = (bf16[32,1792]{1,0:T(8,128)(2,1)S(1)}, bf16[32,1792]{1,0:T(8,128)(2,1)S(1)}, u32[]{:S(2)}, u32[]{:S(2)}) collective-permute-start(bf16[32,1792]{1,0:T(8,128)(2,1)S(1)} %get-tuple-element.44), channel_id=1, source_target_pairs={{0,12},{1,13},{2,14},{3,15},{4,8},{5,9},{6,10},{7,11},{8,4},{9,5},... | collective-permute-start | bytes 344072 | tf_op jit(solution)/shard_map/ppermute | solution.py:332
  50.7 7.0 %collective-permute-start.9 = (bf16[64,3584]{1,0:T(8,128)(2,1)S(1)}, bf16[64,3584]{1,0:T(8,128)(2,1)S(1)}, u32[]{:S(2)}, u32[]{:S(2)}) collective-permute-start(bf16[64,3584]{1,0:T(8,128)(2,1)S(1)} %collective-permute-done.5.refs_3_.refs_6_), channel_id=1, source_target_pairs={{0,1},{1,0},{2,3},{3,2},{4,5},{5,4},{6,7},{7,6},{8,9},{9,8},{10,11... | collective-permute-start | bytes 1376264 | tf_op jit(solution)/shard_map/ppermute | solution.py:332
  52.1 15.2 %collective-permute-start.17 = (bf16[32,1792]{1,0:T(8,128)(2,1)S(1)}, bf16[32,1792]{1,0:T(8,128)(2,1)S(1)}, u32[]{:S(2)}, u32[]{:S(2)}) collective-permute-start(bf16[32,1792]{1,0:T(8,128)(2,1)S(1)} %get-tuple-element.38), channel_id=1, source_target_pairs={{0,4},{1,5},{2,6},{3,7},{4,0},{5,1},{6,2},{7,3},{8,12},{9,13},{10,... | collective-permute-start | bytes 344072 | tf_op jit(solution)/shard_map/ppermute | solution.py:332
  53.6 13.8 %collective-permute-start.18 = (bf16[32,1792]{1,0:T(8,128)(2,1)S(1)}, bf16[32,1792]{1,0:T(8,128)(2,1)S(1)}, u32[]{:S(2)}, u32[]{:S(2)}) collective-permute-start(bf16[32,1792]{1,0:T(8,128)(2,1)S(1)} %get-tuple-element.39), channel_id=1, source_target_pairs={{0,8},{1,9},{2,10},{3,11},{4,12},{5,13},{6,14},{7,15},{8,0},{9,1},... | collective-permute-start | bytes 344072 | tf_op jit(solution)/shard_map/ppermute | solution.py:332
  56.1 11.2 %collective-permute-start.19 = (bf16[32,1792]{1,0:T(8,128)(2,1)S(1)}, bf16[32,1792]{1,0:T(8,128)(2,1)S(1)}, u32[]{:S(2)}, u32[]{:S(2)}) collective-permute-start(bf16[32,1792]{1,0:T(8,128)(2,1)S(1)} %get-tuple-element.40), channel_id=1, source_target_pairs={{0,12},{1,13},{2,14},{3,15},{4,8},{5,9},{6,10},{7,11},{8,4},{9,5},... | collective-permute-start | bytes 344072 | tf_op jit(solution)/shard_map/ppermute | solution.py:332
  57.6 1.8 %collective-permute-start.10 = (bf16[64,3584]{1,0:T(8,128)(2,1)S(1)}, bf16[64,3584]{1,0:T(8,128)(2,1)S(1)}, u32[]{:S(2)}, u32[]{:S(2)}) collective-permute-start(bf16[64,3584]{1,0:T(8,128)(2,1)S(1)} %collective-permute-done.8.refs_7_.refs_3_), channel_id=1, source_target_pairs={{0,1},{1,0},{2,3},{3,2},{4,5},{5,4},{6,7},{7,6},{8,9},{9,8},{10,11... | collective-permute-start | bytes 1376264 | tf_op jit(solution)/shard_map/ppermute | solution.py:332
  62.8 10.9 %all-to-all-start.1 = ((bf16[16,16,128]{2,1,0:T(8,128)(2,1)}), bf16[16,16,128]{2,1,0:T(8,128)(2,1)S(1)}, u32[]{:S(2)}, u32[]{:S(2)}) async-start(bf16[16,16,128]{2,1,0:T(8,128)(2,1)} %get-tuple-element.32.refs_4_), calls=%async_computation.1 | async-start | bytes 131072 | tf_op jit(solution)/shard_map/all_to_all | solution.py:338
  66.9 1.4 %collective-permute-start.15 = (f32[16,1792]{1,0:T(8,128)S(1)}, f32[16,1792]{1,0:T(8,128)S(1)}, u32[]{:S(2)}, u32[]{:S(2)}) collective-permute-start(f32[16,1792]{1,0:T(8,128)S(1)} %get-tuple-element.46), channel_id=1, source_target_pairs={{0,1},{1,0},{2,3},{3,2},{4,5},{5,4},{6,7},{7,6},{8,9},{9,8},{10,11... | collective-permute-start | bytes 344072 | tf_op jit(solution)/shard_map/ppermute | solution.py:332
  67.4 1.4 %collective-permute-start.20 = (f32[16,1792]{1,0:T(8,128)S(1)}, f32[16,1792]{1,0:T(8,128)S(1)}, u32[]{:S(2)}, u32[]{:S(2)}) collective-permute-start(f32[16,1792]{1,0:T(8,128)S(1)} %get-tuple-element.42), channel_id=1, source_target_pairs={{0,1},{1,0},{2,3},{3,2},{4,5},{5,4},{6,7},{7,6},{8,9},{9,8},{10,11... | collective-permute-start | bytes 344072 | tf_op jit(solution)/shard_map/ppermute | solution.py:332
  (7 other events, 39.9 us)

commit v6 on v5

--- a/solution.py
+++ b/solution.py
@@ -15,10 +15,8 @@
 DMA = pltpu.SemaphoreType.DMA
 MIB = 1024 * 1024
 
-
 def mm(a, b, ca=1, cb=0, precision=None):
     return lax.dot_general(a, b, (((ca,), (cb,)), ((), ())), preferred_element_type=F32, precision=precision)
-
 
 def call(kernel, outs, args, scalars=None, after=(), scratch=(), spaces=None, out_spaces=None, alias=None, limit=None):
     size = sum((x.size * x.dtype.itemsize for x in [*args, *outs]))
@@ -34,19 +32,16 @@
         kernel(*refs[:used], *refs[used + len(after):])
     return pl.pallas_call(body, out_shape=[jax.ShapeDtypeStruct(o.shape, o.dtype) for o in outs], in_specs=specs + [pl.BlockSpec(memory_space=pl.ANY)] * len(after), out_specs=[pl.BlockSpec(memory_space=space) for space in out_spaces], scratch_shapes=list(scratch), input_output_aliases=alias or {}, compiler_params=pltpu.CompilerParams(vmem_limit_bytes=limit or min(60 * MIB, int(8 * MIB + 1.5 * total))), cost_estimate=pl.CostEstimate(flops=0, bytes_accessed=size, transcendentals=0))(*args, *after)
 
-
 def split(x):
     high = x.astype(BF)
     return (high, (x - high.astype(F32)).astype(BF))
 
-
 def lanes(start, size):
     return pl.ds(pl.multiple_of(start, 128), size)
 
-
-def low_rank_kernel(hidden, a_in, a_out, low_out, stats_out, hidden_in, a_in_in, a_out_in, sems):
-    slots = stats_out.shape[1]
-    pieces = 4
+def low_slots_kernel(hidden, a_in, a_out, lows, hidden_in, a_in_in, a_out_in, sems):
+    slots = lows.shape[2] // 2
+    pieces = 2
     rows = hidden.shape[0] // pieces
     copies = [pltpu.make_async_copy(a_in, a_in_in, sems.at[pieces]), pltpu.make_async_copy(a_out, a_out_in, sems.at[pieces + 1])]
     for i in range(pieces):
@@ -66,20 +61,19 @@
             part = rest.astype(BF).astype(F32)
             stats = jnp.where(row == base + piece, part, stats)
             rest = rest - part
-    stats_out[...] = stats.astype(BF)
+    stats = stats.astype(BF)
+    low = []
     for i in range(pieces):
         copies[2 + i].wait()
-        part = slice(i * rows, (i + 1) * rows)
-        low_out[:, part] = mm(a_in_in[...], hidden_in[part, :], 1, 1).astype(BF)
-
-
-def pack_low_kernel(low, stats, out):
-    slots = out.shape[2] // 2
-    for device in range(out.shape[0]):
+        low.append(mm(a_in_in[...], hidden_in[i * rows:(i + 1) * rows, :], 1, 1).astype(BF))
+    low = jnp.concatenate(low, axis=1)
+    for device in range(lows.shape[0]):
         chip = device // 2
-        out[device, :, 0:slots] = low[:, chip * slots:(chip + 1) * slots]
-        out[device, :, slots:] = stats[...]
-
+        lows[device, :, 0:slots] = low[:, chip * slots:(chip + 1) * slots]
+        lows[device, :, slots:] = stats
+
+def copy_kernel(value, out):
+    out[...] = value[...]
 
 def join_kernel(*refs):
     pieces, out = (refs[:-1], refs[-1])
@@ -88,12 +82,10 @@
         out[start:start + piece.shape[0], :] = piece[...]
         start += piece.shape[0]
 
-
 def fold_of(slots, experts, capacity, source):
     column = lax.broadcasted_iota(jnp.int32, (slots, experts * capacity), 1)
     row = lax.broadcasted_iota(jnp.int32, (slots, experts * capacity), 0)
     return (row == source * capacity + lax.rem(column, capacity)).astype(BF)
-
 
 def own_expert(experts, capacity):
     shape = (experts * RANK, experts * capacity)
@@ -101,11 +93,9 @@
     column = lax.div(lax.broadcasted_iota(jnp.int32, shape, 1), capacity)
     return row == column
 
-
 def relative_experts(order_size, tokens, me):
     row = lax.broadcasted_iota(jnp.int32, (order_size, tokens), 0)
     return jnp.bitwise_xor(row, me).astype(F32)
-
 
 def weights_of(where, order, own_meta, far_meta, lows, z_out, w_out):
     me, core = (where[0], where[1])
@@ -137,7 +127,6 @@
             z_out[...] = ordered.T.astype(BF)
     return rows
 
-
 def product_of(rows, own_in, far_in, here, keep, send):
     count, tokens = (keep.shape[0], rows[0].shape[1])
     groups = rows[0].shape[0] // (4 * RANK)
@@ -146,7 +135,6 @@
         total = mm(first, own_in[:, here]) + mm(second, far_in[:, here])
         target[...] = total.astype(target.dtype)
 
-
 def token_copies(where, cot, packed, own_in, far_in, sems):
     half = own_in.shape[1]
     here = lanes(where[1] * half, half)
@@ -157,7 +145,6 @@
         copy.start()
     return copies
 
-
 def partial_kernel(order, where, cot, packed, own_meta, far_meta, lows, z_out, w_out, *outs):
     keeps, sends = (outs[:CHUNKS], outs[CHUNKS:2 * CHUNKS])
     own_in, far_in, sems = outs[2 * CHUNKS:]
@@ -170,7 +157,6 @@
         here = slice(base, base + keep.shape[1])
         base += keep.shape[1]
         product_of(rows, own_in, far_in, here, keep, send)
-
 
 def fold_step_kernel(received, keep, *refs):
     sends, kept = (refs[received:-1], refs[-1])
@@ -184,7 +170,6 @@
     for i, send in enumerate(sends):
         send[...] = total[:, i + 1].reshape(send.shape).astype(send.dtype)
 
-
 def last_fold_kernel(keep, *refs):
     received, (kept, sent) = (refs[:-2], refs[-2:])
     total = keep[...]
@@ -192,7 +177,6 @@
         total = total + more[...].astype(F32)
     kept[...] = total[0:RANK]
     sent[...] = total[RANK:]
-
 
 def factor_half(flip, side, cot, z, factors, delta, scratch):
     tokens_in, table, result, sems = scratch
@@ -223,13 +207,11 @@
         coords = coords + mm(block, tokens_in[piece], 1, 1)
     return (coords, writes)
 
-
 def near_kernel(where, cot, z, *refs):
     factors, (coords_out, delta), scratch = (refs[:-6], refs[-6:-4], refs[-4:])
     coords_out[...], copies = factor_half(0, where[2], cot, z, factors, delta, scratch)
     for copy in copies:
         copy.wait()
-
 
 def far_kernel(order, where, cot, z, w, near, _, *refs):
     factors, (coords_out, delta), scratch = (refs[:-6], refs[-6:-4], refs[-4:])
@@ -248,7 +230,6 @@
         coords_out[jnp.bitwise_xor(where[0], e)] = rows[e * RANK:(e + 1) * RANK]
     for copy in copies:
         copy.wait()
-
 
 def inverse_kernel(a_in, a_out, lows, inv_in, inv_out):
     experts, _, double = lows.shape
@@ -273,7 +254,6 @@
     inv_in[...] = works[0][1]
     inv_out[...] = works[1][1]
 
-
 def scaled_in_kernel(coords, hidden, inverse, out):
     pieces = []
     for base in range(0, coords.shape[0], 4):
@@ -283,7 +263,6 @@
         pieces.append(total)
     grad_low = jnp.concatenate(pieces, axis=1).astype(BF)
     out[...] = mm(inverse[...], mm(grad_low, hidden[...]), precision=HIGHEST)
-
 
 def scaled_out_kernel(where, inverse, *refs):
     pieces, (out, rows, sems) = (refs[:-3], refs[-3:])
@@ -300,22 +279,19 @@
     for copy in copies:
         copy.wait()
 
-
-def radix_groups(experts, most):
+def radix_groups(experts):
     groups, bit = ([], 4)
     while bit < experts:
-        radix = min(most, experts // bit)
+        radix = min(4, experts // bit)
         groups.append([bit * k for k in range(1, radix)])
         bit *= radix
     return groups
-
 
 def relative_order(bits):
     order = [0]
     for bit in bits:
         order = order + [e ^ bit for e in order]
     return order
-
 
 def on_device(hidden_slots, adapter_in, adapter_out, expert_ids, gate_weights, cotangent):
     experts, groups = (lax.axis_size('expert'), lax.axis_size('group'))
@@ -336,66 +312,58 @@
 
     def spread(x):
         return lax.all_to_all(x, 'expert', split_axis=0, concat_axis=0, tiled=True)
-    groups_z = radix_groups(experts, 4)
-    groups_of = [radix_groups(experts, 2 if 0 & 1 << p else 4) for p in range(2)]
+    groups_z = radix_groups(experts)
     far_bits = [1 << i for i in reversed(range(2, experts.bit_length() - 1))]
     full = relative_order([2, *far_bits, 1])
-    block = jnp.where(group % 2 == 0, a_out[:, :half], a_out[:, half:])
+    block = lax.dynamic_slice_in_dim(a_out, group % 2 * half, half, axis=1)
     received = swap(block, 2)
-    low, stats = call(low_rank_kernel, [struct((RANK, hidden.shape[0]), BF), struct((RANK, 2 * capacity), BF)], [hidden, a_in, a_out], scratch=[VMEM(hidden.shape, BF), VMEM(a_in.shape, BF), VMEM(a_out.shape, BF), DMA((6,))], spaces=[HBM] * 3, limit=63 * MIB)
+    low, = call(low_slots_kernel, [struct((experts, RANK, 4 * capacity), BF)], [hidden, a_in, a_out], scratch=[VMEM(hidden.shape, BF), VMEM(a_in.shape, BF), VMEM(a_out.shape, BF), DMA((2 + 2,))], spaces=[HBM] * 3, limit=63 * MIB)
     far_tokens = swap(cotangent, 1)
     own_meta = jnp.concatenate([expert_ids.T.astype(BF), gate_weights.T.astype(BF), jnp.zeros((12, tokens), BF)], axis=0)
     far_meta = swap(own_meta, 1)
     block, = call(join_kernel, [struct((2 * RANK, half), BF)], [block, received], after=[low])
-    lows, = call(pack_low_kernel, [struct((experts, RANK, 4 * capacity), BF)], [low, stats], after=[block])
+    lows, = call(copy_kernel, [low], [low], after=[block])
     lows = spread(lows)
     inv_in, inv_out = call(inverse_kernel, [struct((RANK, RANK), F32)] * 2, [a_in, a_out, lows])
     count = experts * RANK // 2
 
     def planes_of(block, gate):
+        pieces = block
         for bit in far_bits:
-            received = swap(block, bit)
             if bit == far_bits[-1]:
-                return ([block, received], last)
-            last = [block, received]
-            block, = call(join_kernel, [struct((2 * block.shape[0], half), BF)], last, after=gate)
-    gate_inv = []
-    early = []
-    near, last = planes_of(block, [lows] + gate_inv)
-    early = [near[0]]
+                return ([block, swap(block, bit)], last)
+            last = pieces + [swap(piece, bit) for piece in pieces]
+            block, = call(join_kernel, [struct((2 * sum((piece.shape[0] for piece in pieces)), half), BF)], last, after=gate)
+            pieces = [block]
+    near, last = planes_of([block], [lows])
     tiles = half // 128
-    wides = [128 * (tiles * 14 // 28), half - 128 * (tiles * 14 // 28)]
+    wides = [128 * (tiles // 2), half - 128 * (tiles // 2)]
     token_args = [cotangent, far_tokens, own_meta, far_meta, lows]
     token_scratch = [VMEM((tokens, half), BF), VMEM((tokens, half), BF), DMA((2,))]
     shapes = [struct((tokens, experts * RANK), BF), struct((experts * capacity, tokens), BF)]
-    far_space = pl.ANY
-    z, weights, *parts = call(lambda *refs: partial_kernel(full, *refs), shapes + [struct((count, wide), F32) for wide in wides] + [struct((count, wide), BF) for wide in wides], token_args, where, after=early, scratch=token_scratch, spaces=[HBM, far_space, VMEM, VMEM, VMEM])
+    z, weights, *parts = call(lambda *refs: partial_kernel(full, *refs), shapes + [struct((count, wide), F32) for wide in wides] + [struct((count, wide), BF) for wide in wides], token_args, where, after=[near[0]], scratch=token_scratch, spaces=[HBM, pl.ANY, VMEM, VMEM, VMEM])
     kept, sent = (parts[:CHUNKS], parts[CHUNKS:])
 
     def fold_y(piece, gate):
-        group = groups_of[piece][0]
+        group = groups_z[0]
         wide = wides[piece]
         rows = count // (1 + len(group))
         return list(call(lambda keep, *refs: fold_step_kernel(1, keep, *refs), [struct((rows, wide), BF)] * len(group) + [struct((rows, wide), F32)], [kept[piece], swap(sent[piece], 2)], after=gate))
     far = [swap_side(near[0])]
-    fold_a = []
-    gate = [sent[0], inv_in]
-    gate = gate + [far[-1]]
-    near[1:] = call(join_kernel, [struct(near[1].shape, BF)], [near[1]], after=gate)
+    near[1:] = call(join_kernel, [struct(near[1].shape, BF)], [near[1]], after=[sent[0], inv_in, far[0]])
     factors = list(near)
     far.append(swap_side(near[1]))
     factors += [swap(block, 1) for block in near]
     far += [swap(block, 1) for block in far]
     cuts = 2
     scratch = [VMEM((cuts, tokens, half // cuts), BF), VMEM((cuts, experts * RANK, half // cuts), BF), VMEM((cuts, tokens, half // cuts), BF), DMA((cuts, 2 * len(far) + 2))]
-    near_coords, delta = call(near_kernel, [struct((experts * RANK, tokens), F32), struct((tokens, width), BF)], [cotangent, z, *factors], where, after=[], scratch=scratch, spaces=[HBM, VMEM] + [HBM] * len(factors), out_spaces=[VMEM, HBM])
+    near_coords, delta = call(near_kernel, [struct((experts * RANK, tokens), F32), struct((tokens, width), BF)], [cotangent, z, *factors], where, scratch=scratch, spaces=[HBM, VMEM] + [HBM] * len(factors), out_spaces=[VMEM, HBM])
     own_rows, far_rows, ends = ([], [], [])
-    gates_b = {0: [], 1: [near_coords], 2: [near_coords, far[len(far) // 2 - 1]], 3: [near_coords, far[-1]], 4: [inv_in], 5: [far[len(far) // 2 - 1]], 6: [near_coords, inv_in]}
-    folds = [fold_a, fold_y(1, gates_b[2])]
+    folds = [None, fold_y(1, [near_coords, far[1]])]
     for piece in range(CHUNKS):
         rows, wide = (count, wides[piece])
         keep = kept[piece]
-        for n, group in enumerate(groups_of[piece]):
+        for n, group in enumerate(groups_z):
             radix = 1 + len(group)
             rows //= radix
             if n == 0 and folds[piece]:
@@ -414,8 +382,7 @@
                 keep = keep + more.astype(F32)
             own_rows.append(keep[:RANK])
             far_rows.append(swap(keep[RANK:], 1))
-    gate_far = [[], [folds[1][-1]], [own_rows[0]], [folds[1][-1], own_rows[0]]][0]
-    coords, delta = call(lambda *refs: far_kernel(full, *refs), [struct((experts, RANK, 4 * capacity), BF), struct((tokens, width), BF)], [cotangent, z, weights, near_coords, delta, *far], where, after=gate_far, scratch=scratch, spaces=[HBM, VMEM, VMEM, VMEM, HBM] + [HBM] * len(far), out_spaces=[VMEM, HBM], alias={5: 1})
+    coords, delta = call(lambda *refs: far_kernel(full, *refs), [struct((experts, RANK, 4 * capacity), BF), struct((tokens, width), BF)], [cotangent, z, weights, near_coords, delta, *far], where, scratch=scratch, spaces=[HBM, VMEM, VMEM, VMEM, HBM] + [HBM] * len(far), out_spaces=[VMEM, HBM], alias={5: 1})
     keep, received = ends[1]
     keep, send = call(last_fold_kernel, [struct((RANK, wides[1]), F32)] * 2, [keep, *received], after=[coords])
     own_rows.append(keep)
@@ -426,7 +393,6 @@
     scaled_in, = call(scaled_in_kernel, [struct((RANK, hidden.shape[1]), F32)], [coords, hidden, inv_out])
     return (delta, scaled_in[None], scaled_out[None])
 
-
 def solution(mesh):
     every = ('group', 'expert')
     return jax.shard_map(on_device, mesh=mesh, in_specs=(P(every, None, None), P('expert', None, None), P('expert', None, None), P(every, None), P(every, None), P(every, None)), out_specs=(P(every, None), P(every, None, None), P(every, None, None)), check_vma=False)

time: 75.4 us -> 75.4 us (level)
  local copies, waits for them, and re-layouts: 1.73 us -> 2.9 us
  other arithmetic: 1.33 us -> 0.36 us
    select_n x1 -> x0, other arithmetic: 0.97 us -> none  [on_device(): block = jnp.where(group % 2 == 0, a_out[:, :half], a_out[:, half:])]
    dynamic_slice x0 -> x1, local copies, waits for them, and re-layouts: none -> 0.91 us  [on_device(): block = lax.dynamic_slice_in_dim(a_out, group % 2 * half, half, axis=1)]
where the time goes in v6:
time: 75.4 us; the launch traced here: 75 us
  starting transfers between devices  30.9 us (41%)
  waiting for transfers between devices  21.9 us (29%)
  Pallas kernels  18 us (24%)
  local copies, waits for them, and re-layouts  2.9 us (4%)
  between operations  0.86 us (1%)
    ppermute x19, starting transfers between devices, swap(): return lax.ppermute(x, 'expert', [(i, i ^ bit) for i in range(experts)])  20 us
    pallas_call x13, Pallas kernels, call(): pl.pallas_call(body, out_shape=[jax.ShapeDtypeStruct(o.shape, o.dtype) fo...  18 us
    ppermute x19, waiting for transfers between devices, swap(): return lax.ppermute(x, 'expert', [(i, i ^ bit) for i in range(experts)])  11.4 us
    all_to_all x2, waiting for transfers between devices, spread(): return lax.all_to_all(x, 'expert', split_axis=0, concat_axis=0, tiled=True)  9.57 us
    all_to_all x2, starting transfers between devices, spread(): return lax.all_to_all(x, 'expert', split_axis=0, concat_axis=0, tiled=True)  7.85 us
    ppermute x2, starting transfers between devices, swap_side(): return lax.ppermute(x, 'group', [(i, i ^ 1) for i in range(groups)])  3.05 us
    unnamed x16, local copies, waits for them, and re-layouts  1.87 us
  transfers between devices with their start and end apart: 23, of which 11 were waited for; matrix products, arithmetic and copies ran while one was open for 2% of the time, Pallas kernels for 22%

profile of v6, /device:TPU:0, one launch (start us, length us, event | category | flops | bytes accessed | tf_op | source)
XLA Modules:
  0.0 75.0 jit_solution(2883055677096612852)
XLA Ops:
  2.1 2.6 %collective-permute-start.2 = (bf16[16,3584]{1,0:T(8,128)(2,1)S(1)}, bf16[16,3584]{1,0:T(8,128)(2,1)S(1)}, u32[]{:S(2)}, u32[]{:S(2)}) collective-permute-start(bf16[16,3584]{1,0:T(8,128)(2,1)S(1)} %dynamic-slice_bitcast_fusion.refs_0_), channel_id=1, source_target_pairs={{0,2},{1,3},{2,0},{3,1},{4,6},{5,7},{6,4},{7,5},{8,10},{9,11},{10,... | collective-permute-start | bytes 344072 | tf_op jit(solution)/shard_map/ppermute | solution.py:308
  4.6 3.4 %shard_map.85.refs_2_.refs_0_ = bf16[16,16,128]{2,1,0:T(8,128)(2,1)} custom-call(bf16[512,2048]{1,0:T(8,128)(2,1)} %bitcast.29, bf16[16,2048]{1,0:T(8,128)(2,1)} %bitcast.33, bf16[16,7168]{1,0:T(8,128)(2,1)} %bitcast.31), custom_call_target="tpu_custom_call" | custom-call | bytes 2457600 | tf_op jit(solution)/shard_map/pallas_call | solution.py:33
  9.4 2.7 %collective-permute-start.3 = (bf16[32,3584]{1,0:T(8,128)(2,1)S(1)}, bf16[32,3584]{1,0:T(8,128)(2,1)S(1)}, u32[]{:S(2)}, u32[]{:S(2)}) collective-permute-start(bf16[32,3584]{1,0:T(8,128)(2,1)S(1)} %shard_map.86.refs_1_.refs_0_), channel_id=1, source_target_pairs={{0,8},{1,9},{2,10},{3,11},{4,12},{5,13},{6,14},{7,15},{8,0},{9,1},... | collective-permute-start | bytes 688136 | tf_op jit(solution)/shard_map/ppermute | solution.py:308
  13.7 3.9 %all-to-all-start = ((bf16[16,16,128]{2,1,0:T(8,128)(2,1)}), bf16[16,16,128]{2,1,0:T(8,128)(2,1)S(1)}, u32[]{:S(2)}, u32[]{:S(2)}) async-start(bf16[16,16,128]{2,1,0:T(8,128)(2,1)} %shard_map.87), calls=%async_computation | async-start | bytes 131072 | tf_op jit(solution)/shard_map/all_to_all | solution.py:314
  18.1 6.5 %all-to-all-done.refs_2_.refs_5_ = bf16[16,16,128]{2,1,0:T(8,128)(2,1)S(1)} async-done(((bf16[16,16,128]{2,1,0:T(8,128)(2,1)}), bf16[16,16,128]{2,1,0:T(8,128)(2,1)S(1)}, u32[]{:S(2)}, u32[]{:S(2)}) %all-to-all-start) | async-done | bytes 65568 | tf_op jit(solution)/shard_map/all_to_all | solution.py:314
  25.4 1.5 %collective-permute-start.5 = (bf16[64,3584]{1,0:T(8,128)(2,1)S(1)}, bf16[64,3584]{1,0:T(8,128)(2,1)S(1)}, u32[]{:S(2)}, u32[]{:S(2)}) collective-permute-start(bf16[64,3584]{1,0:T(8,128)(2,1)S(1)} %shard_map.88.refs_6_.refs_3_), channel_id=1, source_target_pairs={{0,16},{16,0},{1,17},{17,1},{2,18},{18,2},{3,19},{19,3},{4,20},{20... | collective-permute-start | bytes 1376264 | tf_op jit(solution)/shard_map/ppermute | solution.py:311
  27.0 3.2 %shard_map.89 = (bf16[128,256]{1,0:T(8,128)(2,1)S(1)}, bf16[512,128]{1,0:T(8,128)(2,1)S(1)}, f32[128,1792]{1,0:T(8,128)S(1)}, f32[128,1792]{1,0:T(8,128)S(1)}, b...) custom-call(s32[3]{0:T(128)S(1)} %pad_add_fusion.refs_0_, bf16[128,7168]{1,0:T(8,128)(2,1)S(1)} %copy-done, ...), custom_call_target="tpu_custom_call" | custom-call | bytes 6692864 | tf_op jit(solution)/shard_map/pallas_call | solution.py:33
  31.1 1.6 %shard_map.90 = (f32[16,16]{1,0:T(8,128)S(1)}, f32[16,16]{1,0:T(8,128)S(1)}) custom-call(bf16[16,2048]{1,0:T(8,128)(2,1)S(1)} %bitcast.34, bf16[16,7168]{1,0:T(8,128)(2,1)S(1)} %bitcast.32, bf16[16,16,128]{2,1,0:T(8,128)(2,1)S(1)} %all-to-all-done.refs_2_.refs_5_), custom_call_target="tpu_custom_call" | custom-call | bytes 362496 | tf_op jit(solution)/shard_map/pallas_call | solution.py:33
  32.7 4.5 %collective-permute-done.4.refs_0_ = bf16[64,3584]{1,0:T(8,128)(2,1)S(1)} collective-permute-done((bf16[64,3584]{1,0:T(8,128)(2,1)S(1)}, bf16[64,3584]{1,0:T(8,128)(2,1)S(1)}, u32[]{:S(2)}, u32[]{:S(2)}) %collective-permute-start.4) | collective-permute-done | bytes 458784 | tf_op jit(solution)/shard_map/ppermute | solution.py:308
  37.7 1.6 %collective-permute-start.8 = (bf16[64,3584]{1,0:T(8,128)(2,1)S(1)}, bf16[64,3584]{1,0:T(8,128)(2,1)S(1)}, u32[]{:S(2)}, u32[]{:S(2)}) collective-permute-start(bf16[64,3584]{1,0:T(8,128)(2,1)S(1)} %shard_map.91.refs_4_), channel_id=1, source_target_pairs={{0,16},{16,0},{1,17},{17,1},{2,18},{18,2},{3,19},{19,3},{4,20},{20... | collective-permute-start | bytes 1376264 | tf_op jit(solution)/shard_map/ppermute | solution.py:311
  40.1 2.2 %collective-permute-done.11 = bf16[128,1792]{1,0:T(8,128)(2,1)S(1)} collective-permute-done((bf16[128,1792]{1,0:T(8,128)(2,1)S(1)}, bf16[128,1792]{1,0:T(8,128)(2,1)S(1)}, u32[]{:S(2)}, u32[]{:S(2)}) %collective-permute-start.11) | collective-permute-done | bytes 458784 | tf_op jit(solution)/shard_map/ppermute | solution.py:308
  42.5 1.4 %collective-permute-start.12 = (bf16[32,1792]{1,0:T(8,128)(2,1)S(1)}, bf16[32,1792]{1,0:T(8,128)(2,1)S(1)}, u32[]{:S(2)}, u32[]{:S(2)}) collective-permute-start(bf16[32,1792]{1,0:T(8,128)(2,1)S(1)} %get-tuple-element.39), channel_id=1, source_target_pairs={{0,4},{1,5},{2,6},{3,7},{4,0},{5,1},{6,2},{7,3},{8,12},{9,13},{10,... | collective-permute-start | bytes 344072 | tf_op jit(solution)/shard_map/ppermute | solution.py:308
  43.9 2.5 %collective-permute-start.13 = (bf16[32,1792]{1,0:T(8,128)(2,1)S(1)}, bf16[32,1792]{1,0:T(8,128)(2,1)S(1)}, u32[]{:S(2)}, u32[]{:S(2)}) collective-permute-start(bf16[32,1792]{1,0:T(8,128)(2,1)S(1)} %get-tuple-element.41), channel_id=1, source_target_pairs={{0,8},{1,9},{2,10},{3,11},{4,12},{5,13},{6,14},{7,15},{8,0},{9,1},... | collective-permute-start | bytes 344072 | tf_op jit(solution)/shard_map/ppermute | solution.py:308
  47.5 2.5 %shard_map.92 = (f32[256,128]{1,0:T(8,128)S(1)}, bf16[128,7168]{1,0:T(8,128)(2,1)}) custom-call(s32[3]{0:T(128)S(1)} %pad_add_fusion.refs_0_, bf16[128,7168]{1,0:T(8,128)(2,1)S(1)} %copy-done, bf16[128,256]{1,0:T(8,128)(2,1)S(1)} %get-tuple-element.21.refs_2_, bf16[64,3584]{1,0:T(8,128)(2,1)S(1)} %shard_map.88.refs_6_.refs_3_, ...), custom_call_target="tpu_custom_call" | custom-call | bytes 5701632 | tf_op jit(solution)/shard_map/pallas_call | solution.py:33
  50.7 1.4 %collective-permute-done.16.refs_1_ = bf16[128,1792]{1,0:T(8,128)(2,1)S(1)} collective-permute-done((bf16[128,1792]{1,0:T(8,128)(2,1)S(1)}, bf16[128,1792]{1,0:T(8,128)(2,1)S(1)}, u32[]{:S(2)}, u32[]{:S(2)}) %collective-permute-start.16) | collective-permute-done | bytes 458784 | tf_op jit(solution)/shard_map/ppermute | solution.py:308
  52.1 1.4 %collective-permute-start.17 = (bf16[32,1792]{1,0:T(8,128)(2,1)S(1)}, bf16[32,1792]{1,0:T(8,128)(2,1)S(1)}, u32[]{:S(2)}, u32[]{:S(2)}) collective-permute-start(bf16[32,1792]{1,0:T(8,128)(2,1)S(1)} %get-tuple-element.34), channel_id=1, source_target_pairs={{0,4},{1,5},{2,6},{3,7},{4,0},{5,1},{6,2},{7,3},{8,12},{9,13},{10,... | collective-permute-start | bytes 344072 | tf_op jit(solution)/shard_map/ppermute | solution.py:308
  53.6 2.5 %collective-permute-start.18 = (bf16[32,1792]{1,0:T(8,128)(2,1)S(1)}, bf16[32,1792]{1,0:T(8,128)(2,1)S(1)}, u32[]{:S(2)}, u32[]{:S(2)}) collective-permute-start(bf16[32,1792]{1,0:T(8,128)(2,1)S(1)} %get-tuple-element.35), channel_id=1, source_target_pairs={{0,8},{1,9},{2,10},{3,11},{4,12},{5,13},{6,14},{7,15},{8,0},{9,1},... | collective-permute-start | bytes 344072 | tf_op jit(solution)/shard_map/ppermute | solution.py:308
  56.1 1.6 %collective-permute-start.19 = (bf16[32,1792]{1,0:T(8,128)(2,1)S(1)}, bf16[32,1792]{1,0:T(8,128)(2,1)S(1)}, u32[]{:S(2)}, u32[]{:S(2)}) collective-permute-start(bf16[32,1792]{1,0:T(8,128)(2,1)S(1)} %get-tuple-element.36), channel_id=1, source_target_pairs={{0,12},{1,13},{2,14},{3,15},{4,8},{5,9},{6,10},{7,11},{8,4},{9,5},... | collective-permute-start | bytes 344072 | tf_op jit(solution)/shard_map/ppermute | solution.py:308
  57.7 1.7 %collective-permute-done.10.refs_9_ = bf16[64,3584]{1,0:T(8,128)(2,1)S(1)} collective-permute-done((bf16[64,3584]{1,0:T(8,128)(2,1)S(1)}, bf16[64,3584]{1,0:T(8,128)(2,1)S(1)}, u32[]{:S(2)}, u32[]{:S(2)}) %collective-permute-start.10) | collective-permute-done | bytes 458784 | tf_op jit(solution)/shard_map/ppermute | solution.py:308
  59.5 3.4 %shard_map.93 = (bf16[16,16,128]{2,1,0:T(8,128)(2,1)}, bf16[128,7168]{1,0:T(8,128)(2,1)}) custom-call(s32[3]{0:T(128)S(1)} %pad_add_fusion.refs_0_, bf16[128,7168]{1,0:T(8,128)(2,1)S(1)} %copy-done, bf16[128,256]{1,0:T(8,128)(2,1)S(1)} %get-tuple-element.21.refs_2_, bf16[512,128]{1,0:T(8,128)(2,1)S(1)} %get-tuple-element.22.refs_3_, ...), custom_call_target="tpu_custom_call", output_to_operand_aliasing={{1}: (5, {})} | custom-call | bytes 7733248 | tf_op jit(solution)/shard_map/pallas_call | solution.py:33
  62.8 4.0 %all-to-all-start.1 = ((bf16[16,16,128]{2,1,0:T(8,128)(2,1)}), bf16[16,16,128]{2,1,0:T(8,128)(2,1)S(1)}, u32[]{:S(2)}, u32[]{:S(2)}) async-start(bf16[16,16,128]{2,1,0:T(8,128)(2,1)} %get-tuple-element.28.refs_4_), calls=%async_computation.1 | async-start | bytes 131072 | tf_op jit(solution)/shard_map/all_to_all | solution.py:314
  68.8 1.9 %shard_map.97 = f32[16,7168]{1,0:T(8,128)} custom-call(s32[3]{0:T(128)S(1)} %pad_add_fusion.refs_0_, f32[16,16]{1,0:T(8,128)S(1)} %get-tuple-element.24.refs_2_.refs_1_, f32[16,1792]{1,0:T(8,128)S(1)} %get-tuple-element.43.refs_2_, f32[16,1792]{1,0:T(8,128)S(1)} %collective-permute-done.15.refs_3_, f32[16,1792]{1,0:T(8,128)S(1)} %get-tuple-element.37.refs_4_, ...), custom_call_target="tpu_custom_call" | custom-call | bytes 918528 | tf_op jit(solution)/shard_map/pallas_call | solution.py:33
  70.6 3.1 %all-to-all-done.1.refs_0_ = bf16[16,16,128]{2,1,0:T(8,128)(2,1)S(1)} async-done(((bf16[16,16,128]{2,1,0:T(8,128)(2,1)}), bf16[16,16,128]{2,1,0:T(8,128)(2,1)S(1)}, u32[]{:S(2)}, u32[]{:S(2)}) %all-to-all-start.1) | async-done | bytes 65568 | tf_op jit(solution)/shard_map/all_to_all | solution.py:314
  73.7 1.2 %shard_map.94 = f32[16,2048]{1,0:T(8,128)} custom-call(bf16[16,16,128]{2,1,0:T(8,128)(2,1)S(1)} %all-to-all-done.1.refs_0_, bf16[512,2048]{1,0:T(8,128)(2,1)S(1)} %bitcast.30, f32[16,16]{1,0:T(8,128)S(1)} %get-tuple-element.29.refs_2_), custom_call_target="tpu_custom_call" | custom-call | bytes 2294784 | tf_op jit(solution)/shard_map/pallas_call | solution.py:33
  (63 shorter events, 11.9 us)
Async XLA Ops:
  0.7 26.3 %collective-permute-start = (bf16[128,7168]{1,0:T(8,128)(2,1)}, bf16[128,7168]{1,0:T(8,128)(2,1)}, u32[]{:S(2)}, u32[]{:S(2)}) collective-permute-start(bf16[128,7168]{1,0:T(8,128)(2,1)} %refs_1_.5), channel_id=1, source_target_pairs={{0,1},{1,0},{2,3},{3,2},{4,5},{5,4},{6,7},{7,6},{8,9},{9,8},{10,11... | collective-permute-start | bytes 5505032 | tf_op jit(solution)/shard_map/ppermute | solution.py:308
  2.1 6.3 %collective-permute-start.2 = (bf16[16,3584]{1,0:T(8,128)(2,1)S(1)}, bf16[16,3584]{1,0:T(8,128)(2,1)S(1)}, u32[]{:S(2)}, u32[]{:S(2)}) collective-permute-start(bf16[16,3584]{1,0:T(8,128)(2,1)S(1)} %dynamic-slice_bitcast_fusion.refs_0_), channel_id=1, source_target_pairs={{0,2},{1,3},{2,0},{3,1},{4,6},{5,7},{6,4},{7,5},{8,10},{9,11},{10,... | collective-permute-start | bytes 344072 | tf_op jit(solution)/shard_map/ppermute | solution.py:308
  8.1 18.9 %copy-start = (bf16[128,7168]{1,0:T(8,128)(2,1)S(1)}, bf16[128,7168]{1,0:T(8,128)(2,1)}, u32[]{:S(2)}) copy-start(bf16[128,7168]{1,0:T(8,128)(2,1)} %refs_1_.5) | copy-start | bytes 5505028
  9.4 15.2 %collective-permute-start.3 = (bf16[32,3584]{1,0:T(8,128)(2,1)S(1)}, bf16[32,3584]{1,0:T(8,128)(2,1)S(1)}, u32[]{:S(2)}, u32[]{:S(2)}) collective-permute-start(bf16[32,3584]{1,0:T(8,128)(2,1)S(1)} %shard_map.86.refs_1_.refs_0_), channel_id=1, source_target_pairs={{0,8},{1,9},{2,10},{3,11},{4,12},{5,13},{6,14},{7,15},{8,0},{9,1},... | collective-permute-start | bytes 688136 | tf_op jit(solution)/shard_map/ppermute | solution.py:308
  13.7 10.9 %all-to-all-start = ((bf16[16,16,128]{2,1,0:T(8,128)(2,1)}), bf16[16,16,128]{2,1,0:T(8,128)(2,1)S(1)}, u32[]{:S(2)}, u32[]{:S(2)}) async-start(bf16[16,16,128]{2,1,0:T(8,128)(2,1)} %shard_map.87), calls=%async_computation | async-start | bytes 131072 | tf_op jit(solution)/shard_map/all_to_all | solution.py:314
  17.7 9.2 %collective-permute-start.1 = (bf16[16,128]{1,0:T(8,128)(2,1)S(1)}, bf16[16,128]{1,0:T(8,128)(2,1)S(1)}, u32[]{:S(2)}, u32[]{:S(2)}) collective-permute-start(bf16[16,128]{1,0:T(8,128)(2,1)S(1)} %maximum_maximum_fusion.refs_3_), channel_id=1, source_target_pairs={{0,1},{1,0},{2,3},{3,2},{4,5},{5,4},{6,7},{7,6},{8,9},{9,8},{10,11... | collective-permute-start | bytes 12296 | tf_op jit(solution)/shard_map/ppermute | solution.py:308
  24.7 12.6 %collective-permute-start.4 = (bf16[64,3584]{1,0:T(8,128)(2,1)S(1)}, bf16[64,3584]{1,0:T(8,128)(2,1)S(1)}, u32[]{:S(2)}, u32[]{:S(2)}) collective-permute-start(bf16[64,3584]{1,0:T(8,128)(2,1)S(1)} %shard_map.88.refs_6_.refs_3_), channel_id=1, source_target_pairs={{0,4},{1,5},{2,6},{3,7},{4,0},{5,1},{6,2},{7,3},{8,12},{9,13},{10,... | collective-permute-start | bytes 1376264 | tf_op jit(solution)/shard_map/ppermute | solution.py:308
  25.4 12.3 %collective-permute-start.5 = (bf16[64,3584]{1,0:T(8,128)(2,1)S(1)}, bf16[64,3584]{1,0:T(8,128)(2,1)S(1)}, u32[]{:S(2)}, u32[]{:S(2)}) collective-permute-start(bf16[64,3584]{1,0:T(8,128)(2,1)S(1)} %shard_map.88.refs_6_.refs_3_), channel_id=1, source_target_pairs={{0,16},{16,0},{1,17},{17,1},{2,18},{18,2},{3,19},{19,3},{4,20},{20... | collective-permute-start | bytes 1376264 | tf_op jit(solution)/shard_map/ppermute | solution.py:311
  30.2 12.1 %collective-permute-start.11 = (bf16[128,1792]{1,0:T(8,128)(2,1)S(1)}, bf16[128,1792]{1,0:T(8,128)(2,1)S(1)}, u32[]{:S(2)}, u32[]{:S(2)}) collective-permute-start(bf16[128,1792]{1,0:T(8,128)(2,1)S(1)} %get-tuple-element.23.refs_1_), channel_id=1, source_target_pairs={{0,2},{1,3},{2,0},{3,1},{4,6},{5,7},{6,4},{7,5},{8,10},{9,11},{10,... | collective-permute-start | bytes 1376264 | tf_op jit(solution)/shard_map/ppermute | solution.py:308
  32.7 11.3 %collective-permute-start.6 = (bf16[64,3584]{1,0:T(8,128)(2,1)S(1)}, bf16[64,3584]{1,0:T(8,128)(2,1)S(1)}, u32[]{:S(2)}, u32[]{:S(2)}) collective-permute-start(bf16[64,3584]{1,0:T(8,128)(2,1)S(1)} %shard_map.88.refs_6_.refs_3_), channel_id=1, source_target_pairs={{0,1},{1,0},{2,3},{3,2},{4,5},{5,4},{6,7},{7,6},{8,9},{9,8},{10,11... | collective-permute-start | bytes 1376264 | tf_op jit(solution)/shard_map/ppermute | solution.py:308
  37.7 8.8 %collective-permute-start.7 = (bf16[64,3584]{1,0:T(8,128)(2,1)S(1)}, bf16[64,3584]{1,0:T(8,128)(2,1)S(1)}, u32[]{:S(2)}, u32[]{:S(2)}) collective-permute-start(bf16[64,3584]{1,0:T(8,128)(2,1)S(1)} %shard_map.91.refs_4_), channel_id=1, source_target_pairs={{0,1},{1,0},{2,3},{3,2},{4,5},{5,4},{6,7},{7,6},{8,9},{9,8},{10,11... | collective-permute-start | bytes 1376264 | tf_op jit(solution)/shard_map/ppermute | solution.py:308
  37.7 12.9 %collective-permute-start.8 = (bf16[64,3584]{1,0:T(8,128)(2,1)S(1)}, bf16[64,3584]{1,0:T(8,128)(2,1)S(1)}, u32[]{:S(2)}, u32[]{:S(2)}) collective-permute-start(bf16[64,3584]{1,0:T(8,128)(2,1)S(1)} %shard_map.91.refs_4_), channel_id=1, source_target_pairs={{0,16},{16,0},{1,17},{17,1},{2,18},{18,2},{3,19},{19,3},{4,20},{20... | collective-permute-start | bytes 1376264 | tf_op jit(solution)/shard_map/ppermute | solution.py:311
  39.3 12.7 %collective-permute-start.16 = (bf16[128,1792]{1,0:T(8,128)(2,1)S(1)}, bf16[128,1792]{1,0:T(8,128)(2,1)S(1)}, u32[]{:S(2)}, u32[]{:S(2)}) collective-permute-start(bf16[128,1792]{1,0:T(8,128)(2,1)S(1)} %get-tuple-element.32), channel_id=1, source_target_pairs={{0,2},{1,3},{2,0},{3,1},{4,6},{5,7},{6,4},{7,5},{8,10},{9,11},{10,... | collective-permute-start | bytes 1376264 | tf_op jit(solution)/shard_map/ppermute | solution.py:308
  42.5 11.1 %collective-permute-start.12 = (bf16[32,1792]{1,0:T(8,128)(2,1)S(1)}, bf16[32,1792]{1,0:T(8,128)(2,1)S(1)}, u32[]{:S(2)}, u32[]{:S(2)}) collective-permute-start(bf16[32,1792]{1,0:T(8,128)(2,1)S(1)} %get-tuple-element.39), channel_id=1, source_target_pairs={{0,4},{1,5},{2,6},{3,7},{4,0},{5,1},{6,2},{7,3},{8,12},{9,13},{10,... | collective-permute-start | bytes 344072 | tf_op jit(solution)/shard_map/ppermute | solution.py:308
  43.9 12.1 %collective-permute-start.13 = (bf16[32,1792]{1,0:T(8,128)(2,1)S(1)}, bf16[32,1792]{1,0:T(8,128)(2,1)S(1)}, u32[]{:S(2)}, u32[]{:S(2)}) collective-permute-start(bf16[32,1792]{1,0:T(8,128)(2,1)S(1)} %get-tuple-element.41), channel_id=1, source_target_pairs={{0,8},{1,9},{2,10},{3,11},{4,12},{5,13},{6,14},{7,15},{8,0},{9,1},... | collective-permute-start | bytes 344072 | tf_op jit(solution)/shard_map/ppermute | solution.py:308
  46.4 11.2 %collective-permute-start.14 = (bf16[32,1792]{1,0:T(8,128)(2,1)S(1)}, bf16[32,1792]{1,0:T(8,128)(2,1)S(1)}, u32[]{:S(2)}, u32[]{:S(2)}) collective-permute-start(bf16[32,1792]{1,0:T(8,128)(2,1)S(1)} %get-tuple-element.40), channel_id=1, source_target_pairs={{0,12},{1,13},{2,14},{3,15},{4,8},{5,9},{6,10},{7,11},{8,4},{9,5},... | collective-permute-start | bytes 344072 | tf_op jit(solution)/shard_map/ppermute | solution.py:308
  50.7 7.0 %collective-permute-start.9 = (bf16[64,3584]{1,0:T(8,128)(2,1)S(1)}, bf16[64,3584]{1,0:T(8,128)(2,1)S(1)}, u32[]{:S(2)}, u32[]{:S(2)}) collective-permute-start(bf16[64,3584]{1,0:T(8,128)(2,1)S(1)} %collective-permute-done.5.refs_3_.refs_6_), channel_id=1, source_target_pairs={{0,1},{1,0},{2,3},{3,2},{4,5},{5,4},{6,7},{7,6},{8,9},{9,8},{10,11... | collective-permute-start | bytes 1376264 | tf_op jit(solution)/shard_map/ppermute | solution.py:308
  52.1 15.2 %collective-permute-start.17 = (bf16[32,1792]{1,0:T(8,128)(2,1)S(1)}, bf16[32,1792]{1,0:T(8,128)(2,1)S(1)}, u32[]{:S(2)}, u32[]{:S(2)}) collective-permute-start(bf16[32,1792]{1,0:T(8,128)(2,1)S(1)} %get-tuple-element.34), channel_id=1, source_target_pairs={{0,4},{1,5},{2,6},{3,7},{4,0},{5,1},{6,2},{7,3},{8,12},{9,13},{10,... | collective-permute-start | bytes 344072 | tf_op jit(solution)/shard_map/ppermute | solution.py:308
  53.6 13.8 %collective-permute-start.18 = (bf16[32,1792]{1,0:T(8,128)(2,1)S(1)}, bf16[32,1792]{1,0:T(8,128)(2,1)S(1)}, u32[]{:S(2)}, u32[]{:S(2)}) collective-permute-start(bf16[32,1792]{1,0:T(8,128)(2,1)S(1)} %get-tuple-element.35), channel_id=1, source_target_pairs={{0,8},{1,9},{2,10},{3,11},{4,12},{5,13},{6,14},{7,15},{8,0},{9,1},... | collective-permute-start | bytes 344072 | tf_op jit(solution)/shard_map/ppermute | solution.py:308
  56.1 11.3 %collective-permute-start.19 = (bf16[32,1792]{1,0:T(8,128)(2,1)S(1)}, bf16[32,1792]{1,0:T(8,128)(2,1)S(1)}, u32[]{:S(2)}, u32[]{:S(2)}) collective-permute-start(bf16[32,1792]{1,0:T(8,128)(2,1)S(1)} %get-tuple-element.36), channel_id=1, source_target_pairs={{0,12},{1,13},{2,14},{3,15},{4,8},{5,9},{6,10},{7,11},{8,4},{9,5},... | collective-permute-start | bytes 344072 | tf_op jit(solution)/shard_map/ppermute | solution.py:308
  57.6 1.8 %collective-permute-start.10 = (bf16[64,3584]{1,0:T(8,128)(2,1)S(1)}, bf16[64,3584]{1,0:T(8,128)(2,1)S(1)}, u32[]{:S(2)}, u32[]{:S(2)}) collective-permute-start(bf16[64,3584]{1,0:T(8,128)(2,1)S(1)} %collective-permute-done.8.refs_7_.refs_3_), channel_id=1, source_target_pairs={{0,1},{1,0},{2,3},{3,2},{4,5},{5,4},{6,7},{7,6},{8,9},{9,8},{10,11... | collective-permute-start | bytes 1376264 | tf_op jit(solution)/shard_map/ppermute | solution.py:308
  62.8 10.9 %all-to-all-start.1 = ((bf16[16,16,128]{2,1,0:T(8,128)(2,1)}), bf16[16,16,128]{2,1,0:T(8,128)(2,1)S(1)}, u32[]{:S(2)}, u32[]{:S(2)}) async-start(bf16[16,16,128]{2,1,0:T(8,128)(2,1)} %get-tuple-element.28.refs_4_), calls=%async_computation.1 | async-start | bytes 131072 | tf_op jit(solution)/shard_map/all_to_all | solution.py:314
  66.9 1.4 %collective-permute-start.15 = (f32[16,1792]{1,0:T(8,128)S(1)}, f32[16,1792]{1,0:T(8,128)S(1)}, u32[]{:S(2)}, u32[]{:S(2)}) collective-permute-start(f32[16,1792]{1,0:T(8,128)S(1)} %get-tuple-element.42), channel_id=1, source_target_pairs={{0,1},{1,0},{2,3},{3,2},{4,5},{5,4},{6,7},{7,6},{8,9},{9,8},{10,11... | collective-permute-start | bytes 344072 | tf_op jit(solution)/shard_map/ppermute | solution.py:308
  67.4 1.4 %collective-permute-start.20 = (f32[16,1792]{1,0:T(8,128)S(1)}, f32[16,1792]{1,0:T(8,128)S(1)}, u32[]{:S(2)}, u32[]{:S(2)}) collective-permute-start(f32[16,1792]{1,0:T(8,128)S(1)} %get-tuple-element.38), channel_id=1, source_target_pairs={{0,1},{1,0},{2,3},{3,2},{4,5},{5,4},{6,7},{7,6},{8,9},{9,8},{10,11... | collective-permute-start | bytes 344072 | tf_op jit(solution)/shard_map/ppermute | solution.py:308
  (7 other events, 40.1 us)

commit v7 on v6

--- a/solution.py
+++ b/solution.py
@@ -127,36 +127,39 @@
             z_out[...] = ordered.T.astype(BF)
     return rows
 
-def product_of(rows, own_in, far_in, here, keep, send):
-    count, tokens = (keep.shape[0], rows[0].shape[1])
-    groups = rows[0].shape[0] // (4 * RANK)
-    for side, target in ((0, keep), (1, send)):
-        first, second = (r.reshape(groups, 2, 2 * RANK, tokens)[:, side].reshape(count, tokens) for r in rows)
-        total = mm(first, own_in[:, here]) + mm(second, far_in[:, here])
-        target[...] = total.astype(target.dtype)
-
-def token_copies(where, cot, packed, own_in, far_in, sems):
-    half = own_in.shape[1]
+def product_of(rows, tokens_in, here, keep, send):
+    count = keep.shape[0]
+    total = mm(rows, tokens_in[:, here])
+    keep[...] = total[0:count]
+    send[...] = total[count:].astype(send.dtype)
+
+def token_copies(where, cot, packed, tokens_in, sems):
+    half, tokens = tokens_in.shape[1], cot.shape[0]
     here = lanes(where[1] * half, half)
-    copies = [pltpu.make_async_copy(cot.at[:, here], own_in, sems.at[0])]
-    source = packed if packed.shape[1] == half else packed.at[:, here]
-    copies.append(pltpu.make_async_copy(source, far_in, sems.at[1]))
+    copies = [
+        pltpu.make_async_copy(cot.at[:, here], tokens_in.at[0:tokens, :], sems.at[0]),
+        pltpu.make_async_copy(packed.at[:, here], tokens_in.at[tokens : 2 * tokens, :], sems.at[1]),
+    ]
     for copy in copies:
         copy.start()
     return copies
 
 def partial_kernel(order, where, cot, packed, own_meta, far_meta, lows, z_out, w_out, *outs):
-    keeps, sends = (outs[:CHUNKS], outs[CHUNKS:2 * CHUNKS])
-    own_in, far_in, sems = outs[2 * CHUNKS:]
-    copies = token_copies(where, cot, packed, own_in, far_in, sems)
+    keeps, sends = outs[:CHUNKS], outs[CHUNKS : 2 * CHUNKS]
+    tokens_in, sems = outs[2 * CHUNKS :]
+    copies = token_copies(where, cot, packed, tokens_in, sems)
     rows = weights_of(where, order, own_meta, far_meta, lows, z_out, w_out)
+    rows = jnp.concatenate(rows, axis=1)
+    count, depth = keeps[0].shape[0], rows.shape[1]
+    rows = rows.reshape(count // (2 * RANK), 2, 2 * RANK, depth)
+    rows = jnp.concatenate([rows[:, side].reshape(count, depth) for side in range(2)], axis=0)
     for copy in copies:
         copy.wait()
     base = 0
     for keep, send in zip(keeps, sends):
         here = slice(base, base + keep.shape[1])
         base += keep.shape[1]
-        product_of(rows, own_in, far_in, here, keep, send)
+        product_of(rows, tokens_in, here, keep, send)
 
 def fold_step_kernel(received, keep, *refs):
     sends, kept = (refs[received:-1], refs[-1])
@@ -339,7 +342,7 @@
     tiles = half // 128
     wides = [128 * (tiles // 2), half - 128 * (tiles // 2)]
     token_args = [cotangent, far_tokens, own_meta, far_meta, lows]
-    token_scratch = [VMEM((tokens, half), BF), VMEM((tokens, half), BF), DMA((2,))]
+    token_scratch = [VMEM((2 * tokens, half), BF), DMA((2,))]
     shapes = [struct((tokens, experts * RANK), BF), struct((experts * capacity, tokens), BF)]
     z, weights, *parts = call(lambda *refs: partial_kernel(full, *refs), shapes + [struct((count, wide), F32) for wide in wides] + [struct((count, wide), BF) for wide in wides], token_args, where, after=[near[0]], scratch=token_scratch, spaces=[HBM, pl.ANY, VMEM, VMEM, VMEM])
     kept, sent = (parts[:CHUNKS], parts[CHUNKS:])

time: 75.4 us -> 75.2 us (level)
  no operation moved by 1% of the time
where the time goes in v7:
time: 75.2 us; the launch traced here: 74.8 us
  starting transfers between devices  30.9 us (41%)
  waiting for transfers between devices  22.2 us (30%)
  Pallas kernels  17.6 us (23%)
  local copies, waits for them, and re-layouts  2.9 us (4%)
  between operations  0.86 us (1%)
    ppermute x19, starting transfers between devices, swap(): return lax.ppermute(x, 'expert', [(i, i ^ bit) for i in range(experts)])  19.7 us
    pallas_call x13, Pallas kernels, call(): pl.pallas_call(body, out_shape=[jax.ShapeDtypeStruct(o.shape, o.dtype) fo...  17.6 us
    ppermute x19, waiting for transfers between devices, swap(): return lax.ppermute(x, 'expert', [(i, i ^ bit) for i in range(experts)])  11.1 us
    all_to_all x2, waiting for transfers between devices, spread(): return lax.all_to_all(x, 'expert', split_axis=0, concat_axis=0, tiled=True)  9.57 us
    all_to_all x2, starting transfers between devices, spread(): return lax.all_to_all(x, 'expert', split_axis=0, concat_axis=0, tiled=True)  8.14 us
    ppermute x2, starting transfers between devices, swap_side(): return lax.ppermute(x, 'group', [(i, i ^ 1) for i in range(groups)])  3.05 us
    unnamed x16, local copies, waits for them, and re-layouts  1.87 us
    ppermute x2, waiting for transfers between devices, swap_side(): return lax.ppermute(x, 'group', [(i, i ^ 1) for i in range(groups)])  1.52 us
  transfers between devices with their start and end apart: 23, of which 11 were waited for; matrix products, arithmetic and copies ran while one was open for 2% of the time, Pallas kernels for 22%

profile of v7, /device:TPU:0, one launch (start us, length us, event | category | flops | bytes accessed | tf_op | source)
XLA Modules:
  0.0 74.8 jit_solution(9850402989048950274)
XLA Ops:
  2.1 2.6 %collective-permute-start.2 = (bf16[16,3584]{1,0:T(8,128)(2,1)S(1)}, bf16[16,3584]{1,0:T(8,128)(2,1)S(1)}, u32[]{:S(2)}, u32[]{:S(2)}) collective-permute-start(bf16[16,3584]{1,0:T(8,128)(2,1)S(1)} %dynamic-slice_bitcast_fusion.refs_0_), channel_id=1, source_target_pairs={{0,2},{1,3},{2,0},{3,1},{4,6},{5,7},{6,4},{7,5},{8,10},{9,11},{10,... | collective-permute-start | bytes 344072 | tf_op jit(solution)/shard_map/ppermute | solution.py:311
  4.6 3.4 %shard_map.85.refs_2_.refs_0_ = bf16[16,16,128]{2,1,0:T(8,128)(2,1)} custom-call(bf16[512,2048]{1,0:T(8,128)(2,1)} %bitcast.29, bf16[16,2048]{1,0:T(8,128)(2,1)} %bitcast.33, bf16[16,7168]{1,0:T(8,128)(2,1)} %bitcast.31), custom_call_target="tpu_custom_call" | custom-call | bytes 2457600 | tf_op jit(solution)/shard_map/pallas_call | solution.py:33
  9.4 2.7 %collective-permute-start.3 = (bf16[32,3584]{1,0:T(8,128)(2,1)S(1)}, bf16[32,3584]{1,0:T(8,128)(2,1)S(1)}, u32[]{:S(2)}, u32[]{:S(2)}) collective-permute-start(bf16[32,3584]{1,0:T(8,128)(2,1)S(1)} %shard_map.86.refs_1_.refs_0_), channel_id=1, source_target_pairs={{0,8},{1,9},{2,10},{3,11},{4,12},{5,13},{6,14},{7,15},{8,0},{9,1},... | collective-permute-start | bytes 688136 | tf_op jit(solution)/shard_map/ppermute | solution.py:311
  13.7 3.9 %all-to-all-start = ((bf16[16,16,128]{2,1,0:T(8,128)(2,1)}), bf16[16,16,128]{2,1,0:T(8,128)(2,1)S(1)}, u32[]{:S(2)}, u32[]{:S(2)}) async-start(bf16[16,16,128]{2,1,0:T(8,128)(2,1)} %shard_map.87), calls=%async_computation | async-start | bytes 131072 | tf_op jit(solution)/shard_map/all_to_all | solution.py:317
  18.1 6.5 %all-to-all-done.refs_2_.refs_5_ = bf16[16,16,128]{2,1,0:T(8,128)(2,1)S(1)} async-done(((bf16[16,16,128]{2,1,0:T(8,128)(2,1)}), bf16[16,16,128]{2,1,0:T(8,128)(2,1)S(1)}, u32[]{:S(2)}, u32[]{:S(2)}) %all-to-all-start) | async-done | bytes 65568 | tf_op jit(solution)/shard_map/all_to_all | solution.py:317
  25.4 1.5 %collective-permute-start.5 = (bf16[64,3584]{1,0:T(8,128)(2,1)S(1)}, bf16[64,3584]{1,0:T(8,128)(2,1)S(1)}, u32[]{:S(2)}, u32[]{:S(2)}) collective-permute-start(bf16[64,3584]{1,0:T(8,128)(2,1)S(1)} %shard_map.88.refs_6_.refs_3_), channel_id=1, source_target_pairs={{0,16},{16,0},{1,17},{17,1},{2,18},{18,2},{3,19},{19,3},{4,20},{20... | collective-permute-start | bytes 1376264 | tf_op jit(solution)/shard_map/ppermute | solution.py:314
  27.0 2.7 %shard_map.89 = (bf16[128,256]{1,0:T(8,128)(2,1)S(1)}, bf16[512,128]{1,0:T(8,128)(2,1)S(1)}, f32[128,1792]{1,0:T(8,128)S(1)}, f32[128,1792]{1,0:T(8,128)S(1)}, b...) custom-call(s32[3]{0:T(128)S(1)} %pad_add_fusion.refs_0_, bf16[128,7168]{1,0:T(8,128)(2,1)S(1)} %copy-done, ...), custom_call_target="tpu_custom_call" | custom-call | bytes 6692864 | tf_op jit(solution)/shard_map/pallas_call | solution.py:33
  30.7 1.6 %shard_map.90 = (f32[16,16]{1,0:T(8,128)S(1)}, f32[16,16]{1,0:T(8,128)S(1)}) custom-call(bf16[16,2048]{1,0:T(8,128)(2,1)S(1)} %bitcast.34, bf16[16,7168]{1,0:T(8,128)(2,1)S(1)} %bitcast.32, bf16[16,16,128]{2,1,0:T(8,128)(2,1)S(1)} %all-to-all-done.refs_2_.refs_5_), custom_call_target="tpu_custom_call" | custom-call | bytes 362496 | tf_op jit(solution)/shard_map/pallas_call | solution.py:33
  32.3 5.0 %collective-permute-done.4.refs_0_ = bf16[64,3584]{1,0:T(8,128)(2,1)S(1)} collective-permute-done((bf16[64,3584]{1,0:T(8,128)(2,1)S(1)}, bf16[64,3584]{1,0:T(8,128)(2,1)S(1)}, u32[]{:S(2)}, u32[]{:S(2)}) %collective-permute-start.4) | collective-permute-done | bytes 458784 | tf_op jit(solution)/shard_map/ppermute | solution.py:311
  37.7 1.6 %collective-permute-start.8 = (bf16[64,3584]{1,0:T(8,128)(2,1)S(1)}, bf16[64,3584]{1,0:T(8,128)(2,1)S(1)}, u32[]{:S(2)}, u32[]{:S(2)}) collective-permute-start(bf16[64,3584]{1,0:T(8,128)(2,1)S(1)} %shard_map.91.refs_4_), channel_id=1, source_target_pairs={{0,16},{16,0},{1,17},{17,1},{2,18},{18,2},{3,19},{19,3},{4,20},{20... | collective-permute-start | bytes 1376264 | tf_op jit(solution)/shard_map/ppermute | solution.py:314
  40.1 1.7 %collective-permute-done.11 = bf16[128,1792]{1,0:T(8,128)(2,1)S(1)} collective-permute-done((bf16[128,1792]{1,0:T(8,128)(2,1)S(1)}, bf16[128,1792]{1,0:T(8,128)(2,1)S(1)}, u32[]{:S(2)}, u32[]{:S(2)}) %collective-permute-start.11) | collective-permute-done | bytes 458784 | tf_op jit(solution)/shard_map/ppermute | solution.py:311
  42.0 1.4 %collective-permute-start.12 = (bf16[32,1792]{1,0:T(8,128)(2,1)S(1)}, bf16[32,1792]{1,0:T(8,128)(2,1)S(1)}, u32[]{:S(2)}, u32[]{:S(2)}) collective-permute-start(bf16[32,1792]{1,0:T(8,128)(2,1)S(1)} %get-tuple-element.39), channel_id=1, source_target_pairs={{0,4},{1,5},{2,6},{3,7},{4,0},{5,1},{6,2},{7,3},{8,12},{9,13},{10,... | collective-permute-start | bytes 344072 | tf_op jit(solution)/shard_map/ppermute | solution.py:311
  43.4 2.5 %collective-permute-start.13 = (bf16[32,1792]{1,0:T(8,128)(2,1)S(1)}, bf16[32,1792]{1,0:T(8,128)(2,1)S(1)}, u32[]{:S(2)}, u32[]{:S(2)}) collective-permute-start(bf16[32,1792]{1,0:T(8,128)(2,1)S(1)} %get-tuple-element.41), channel_id=1, source_target_pairs={{0,8},{1,9},{2,10},{3,11},{4,12},{5,13},{6,14},{7,15},{8,0},{9,1},... | collective-permute-start | bytes 344072 | tf_op jit(solution)/shard_map/ppermute | solution.py:311
  47.0 2.5 %shard_map.92 = (f32[256,128]{1,0:T(8,128)S(1)}, bf16[128,7168]{1,0:T(8,128)(2,1)}) custom-call(s32[3]{0:T(128)S(1)} %pad_add_fusion.refs_0_, bf16[128,7168]{1,0:T(8,128)(2,1)S(1)} %copy-done, bf16[128,256]{1,0:T(8,128)(2,1)S(1)} %get-tuple-element.21.refs_2_, bf16[64,3584]{1,0:T(8,128)(2,1)S(1)} %shard_map.88.refs_6_.refs_3_, ...), custom_call_target="tpu_custom_call" | custom-call | bytes 5701632 | tf_op jit(solution)/shard_map/pallas_call | solution.py:33
  50.7 1.2 %collective-permute-done.16.refs_1_ = bf16[128,1792]{1,0:T(8,128)(2,1)S(1)} collective-permute-done((bf16[128,1792]{1,0:T(8,128)(2,1)S(1)}, bf16[128,1792]{1,0:T(8,128)(2,1)S(1)}, u32[]{:S(2)}, u32[]{:S(2)}) %collective-permute-start.16) | collective-permute-done | bytes 458784 | tf_op jit(solution)/shard_map/ppermute | solution.py:311
  52.0 1.4 %collective-permute-start.17 = (bf16[32,1792]{1,0:T(8,128)(2,1)S(1)}, bf16[32,1792]{1,0:T(8,128)(2,1)S(1)}, u32[]{:S(2)}, u32[]{:S(2)}) collective-permute-start(bf16[32,1792]{1,0:T(8,128)(2,1)S(1)} %get-tuple-element.34), channel_id=1, source_target_pairs={{0,4},{1,5},{2,6},{3,7},{4,0},{5,1},{6,2},{7,3},{8,12},{9,13},{10,... | collective-permute-start | bytes 344072 | tf_op jit(solution)/shard_map/ppermute | solution.py:311
  53.4 2.5 %collective-permute-start.18 = (bf16[32,1792]{1,0:T(8,128)(2,1)S(1)}, bf16[32,1792]{1,0:T(8,128)(2,1)S(1)}, u32[]{:S(2)}, u32[]{:S(2)}) collective-permute-start(bf16[32,1792]{1,0:T(8,128)(2,1)S(1)} %get-tuple-element.35), channel_id=1, source_target_pairs={{0,8},{1,9},{2,10},{3,11},{4,12},{5,13},{6,14},{7,15},{8,0},{9,1},... | collective-permute-start | bytes 344072 | tf_op jit(solution)/shard_map/ppermute | solution.py:311
  55.9 1.3 %collective-permute-start.19 = (bf16[32,1792]{1,0:T(8,128)(2,1)S(1)}, bf16[32,1792]{1,0:T(8,128)(2,1)S(1)}, u32[]{:S(2)}, u32[]{:S(2)}) collective-permute-start(bf16[32,1792]{1,0:T(8,128)(2,1)S(1)} %get-tuple-element.36), channel_id=1, source_target_pairs={{0,12},{1,13},{2,14},{3,15},{4,8},{5,9},{6,10},{7,11},{8,4},{9,5},... | collective-permute-start | bytes 344072 | tf_op jit(solution)/shard_map/ppermute | solution.py:311
  57.3 1.7 %collective-permute-done.10.refs_9_ = bf16[64,3584]{1,0:T(8,128)(2,1)S(1)} collective-permute-done((bf16[64,3584]{1,0:T(8,128)(2,1)S(1)}, bf16[64,3584]{1,0:T(8,128)(2,1)S(1)}, u32[]{:S(2)}, u32[]{:S(2)}) %collective-permute-start.10) | collective-permute-done | bytes 458784 | tf_op jit(solution)/shard_map/ppermute | solution.py:311
  59.0 3.4 %shard_map.93 = (bf16[16,16,128]{2,1,0:T(8,128)(2,1)}, bf16[128,7168]{1,0:T(8,128)(2,1)}) custom-call(s32[3]{0:T(128)S(1)} %pad_add_fusion.refs_0_, bf16[128,7168]{1,0:T(8,128)(2,1)S(1)} %copy-done, bf16[128,256]{1,0:T(8,128)(2,1)S(1)} %get-tuple-element.21.refs_2_, bf16[512,128]{1,0:T(8,128)(2,1)S(1)} %get-tuple-element.22.refs_3_, ...), custom_call_target="tpu_custom_call", output_to_operand_aliasing={{1}: (5, {})} | custom-call | bytes 7733248 | tf_op jit(solution)/shard_map/pallas_call | solution.py:33
  62.4 4.3 %all-to-all-start.1 = ((bf16[16,16,128]{2,1,0:T(8,128)(2,1)}), bf16[16,16,128]{2,1,0:T(8,128)(2,1)S(1)}, u32[]{:S(2)}, u32[]{:S(2)}) async-start(bf16[16,16,128]{2,1,0:T(8,128)(2,1)} %get-tuple-element.28.refs_4_), calls=%async_computation.1 | async-start | bytes 131072 | tf_op jit(solution)/shard_map/all_to_all | solution.py:317
  68.6 1.9 %shard_map.97 = f32[16,7168]{1,0:T(8,128)} custom-call(s32[3]{0:T(128)S(1)} %pad_add_fusion.refs_0_, f32[16,16]{1,0:T(8,128)S(1)} %get-tuple-element.24.refs_2_.refs_1_, f32[16,1792]{1,0:T(8,128)S(1)} %get-tuple-element.43.refs_2_, f32[16,1792]{1,0:T(8,128)S(1)} %collective-permute-done.15.refs_3_, f32[16,1792]{1,0:T(8,128)S(1)} %get-tuple-element.37.refs_4_, ...), custom_call_target="tpu_custom_call" | custom-call | bytes 918528 | tf_op jit(solution)/shard_map/pallas_call | solution.py:33
  70.5 3.1 %all-to-all-done.1.refs_0_ = bf16[16,16,128]{2,1,0:T(8,128)(2,1)S(1)} async-done(((bf16[16,16,128]{2,1,0:T(8,128)(2,1)}), bf16[16,16,128]{2,1,0:T(8,128)(2,1)S(1)}, u32[]{:S(2)}, u32[]{:S(2)}) %all-to-all-start.1) | async-done | bytes 65568 | tf_op jit(solution)/shard_map/all_to_all | solution.py:317
  73.6 1.2 %shard_map.94 = f32[16,2048]{1,0:T(8,128)} custom-call(bf16[16,16,128]{2,1,0:T(8,128)(2,1)S(1)} %all-to-all-done.1.refs_0_, bf16[512,2048]{1,0:T(8,128)(2,1)S(1)} %bitcast.30, f32[16,16]{1,0:T(8,128)S(1)} %get-tuple-element.29.refs_2_), custom_call_target="tpu_custom_call" | custom-call | bytes 2294784 | tf_op jit(solution)/shard_map/pallas_call | solution.py:33
  (63 shorter events, 12.4 us)
Async XLA Ops:
  0.7 26.3 %collective-permute-start = (bf16[128,7168]{1,0:T(8,128)(2,1)}, bf16[128,7168]{1,0:T(8,128)(2,1)}, u32[]{:S(2)}, u32[]{:S(2)}) collective-permute-start(bf16[128,7168]{1,0:T(8,128)(2,1)} %refs_1_.5), channel_id=1, source_target_pairs={{0,1},{1,0},{2,3},{3,2},{4,5},{5,4},{6,7},{7,6},{8,9},{9,8},{10,11... | collective-permute-start | bytes 5505032 | tf_op jit(solution)/shard_map/ppermute | solution.py:311
  2.1 6.3 %collective-permute-start.2 = (bf16[16,3584]{1,0:T(8,128)(2,1)S(1)}, bf16[16,3584]{1,0:T(8,128)(2,1)S(1)}, u32[]{:S(2)}, u32[]{:S(2)}) collective-permute-start(bf16[16,3584]{1,0:T(8,128)(2,1)S(1)} %dynamic-slice_bitcast_fusion.refs_0_), channel_id=1, source_target_pairs={{0,2},{1,3},{2,0},{3,1},{4,6},{5,7},{6,4},{7,5},{8,10},{9,11},{10,... | collective-permute-start | bytes 344072 | tf_op jit(solution)/shard_map/ppermute | solution.py:311
  8.1 18.9 %copy-start = (bf16[128,7168]{1,0:T(8,128)(2,1)S(1)}, bf16[128,7168]{1,0:T(8,128)(2,1)}, u32[]{:S(2)}) copy-start(bf16[128,7168]{1,0:T(8,128)(2,1)} %refs_1_.5) | copy-start | bytes 5505028
  9.4 15.2 %collective-permute-start.3 = (bf16[32,3584]{1,0:T(8,128)(2,1)S(1)}, bf16[32,3584]{1,0:T(8,128)(2,1)S(1)}, u32[]{:S(2)}, u32[]{:S(2)}) collective-permute-start(bf16[32,3584]{1,0:T(8,128)(2,1)S(1)} %shard_map.86.refs_1_.refs_0_), channel_id=1, source_target_pairs={{0,8},{1,9},{2,10},{3,11},{4,12},{5,13},{6,14},{7,15},{8,0},{9,1},... | collective-permute-start | bytes 688136 | tf_op jit(solution)/shard_map/ppermute | solution.py:311
  13.7 10.9 %all-to-all-start = ((bf16[16,16,128]{2,1,0:T(8,128)(2,1)}), bf16[16,16,128]{2,1,0:T(8,128)(2,1)S(1)}, u32[]{:S(2)}, u32[]{:S(2)}) async-start(bf16[16,16,128]{2,1,0:T(8,128)(2,1)} %shard_map.87), calls=%async_computation | async-start | bytes 131072 | tf_op jit(solution)/shard_map/all_to_all | solution.py:317
  17.7 9.2 %collective-permute-start.1 = (bf16[16,128]{1,0:T(8,128)(2,1)S(1)}, bf16[16,128]{1,0:T(8,128)(2,1)S(1)}, u32[]{:S(2)}, u32[]{:S(2)}) collective-permute-start(bf16[16,128]{1,0:T(8,128)(2,1)S(1)} %maximum_maximum_fusion.refs_3_), channel_id=1, source_target_pairs={{0,1},{1,0},{2,3},{3,2},{4,5},{5,4},{6,7},{7,6},{8,9},{9,8},{10,11... | collective-permute-start | bytes 12296 | tf_op jit(solution)/shard_map/ppermute | solution.py:311
  24.7 12.6 %collective-permute-start.4 = (bf16[64,3584]{1,0:T(8,128)(2,1)S(1)}, bf16[64,3584]{1,0:T(8,128)(2,1)S(1)}, u32[]{:S(2)}, u32[]{:S(2)}) collective-permute-start(bf16[64,3584]{1,0:T(8,128)(2,1)S(1)} %shard_map.88.refs_6_.refs_3_), channel_id=1, source_target_pairs={{0,4},{1,5},{2,6},{3,7},{4,0},{5,1},{6,2},{7,3},{8,12},{9,13},{10,... | collective-permute-start | bytes 1376264 | tf_op jit(solution)/shard_map/ppermute | solution.py:311
  25.4 12.3 %collective-permute-start.5 = (bf16[64,3584]{1,0:T(8,128)(2,1)S(1)}, bf16[64,3584]{1,0:T(8,128)(2,1)S(1)}, u32[]{:S(2)}, u32[]{:S(2)}) collective-permute-start(bf16[64,3584]{1,0:T(8,128)(2,1)S(1)} %shard_map.88.refs_6_.refs_3_), channel_id=1, source_target_pairs={{0,16},{16,0},{1,17},{17,1},{2,18},{18,2},{3,19},{19,3},{4,20},{20... | collective-permute-start | bytes 1376264 | tf_op jit(solution)/shard_map/ppermute | solution.py:314
  29.7 12.0 %collective-permute-start.11 = (bf16[128,1792]{1,0:T(8,128)(2,1)S(1)}, bf16[128,1792]{1,0:T(8,128)(2,1)S(1)}, u32[]{:S(2)}, u32[]{:S(2)}) collective-permute-start(bf16[128,1792]{1,0:T(8,128)(2,1)S(1)} %get-tuple-element.23.refs_1_), channel_id=1, source_target_pairs={{0,2},{1,3},{2,0},{3,1},{4,6},{5,7},{6,4},{7,5},{8,10},{9,11},{10,... | collective-permute-start | bytes 1376264 | tf_op jit(solution)/shard_map/ppermute | solution.py:311
  32.2 11.2 %collective-permute-start.6 = (bf16[64,3584]{1,0:T(8,128)(2,1)S(1)}, bf16[64,3584]{1,0:T(8,128)(2,1)S(1)}, u32[]{:S(2)}, u32[]{:S(2)}) collective-permute-start(bf16[64,3584]{1,0:T(8,128)(2,1)S(1)} %shard_map.88.refs_6_.refs_3_), channel_id=1, source_target_pairs={{0,1},{1,0},{2,3},{3,2},{4,5},{5,4},{6,7},{7,6},{8,9},{9,8},{10,11... | collective-permute-start | bytes 1376264 | tf_op jit(solution)/shard_map/ppermute | solution.py:311
  37.7 8.2 %collective-permute-start.7 = (bf16[64,3584]{1,0:T(8,128)(2,1)S(1)}, bf16[64,3584]{1,0:T(8,128)(2,1)S(1)}, u32[]{:S(2)}, u32[]{:S(2)}) collective-permute-start(bf16[64,3584]{1,0:T(8,128)(2,1)S(1)} %shard_map.91.refs_4_), channel_id=1, source_target_pairs={{0,1},{1,0},{2,3},{3,2},{4,5},{5,4},{6,7},{7,6},{8,9},{9,8},{10,11... | collective-permute-start | bytes 1376264 | tf_op jit(solution)/shard_map/ppermute | solution.py:311
  37.7 12.9 %collective-permute-start.8 = (bf16[64,3584]{1,0:T(8,128)(2,1)S(1)}, bf16[64,3584]{1,0:T(8,128)(2,1)S(1)}, u32[]{:S(2)}, u32[]{:S(2)}) collective-permute-start(bf16[64,3584]{1,0:T(8,128)(2,1)S(1)} %shard_map.91.refs_4_), channel_id=1, source_target_pairs={{0,16},{16,0},{1,17},{17,1},{2,18},{18,2},{3,19},{19,3},{4,20},{20... | collective-permute-start | bytes 1376264 | tf_op jit(solution)/shard_map/ppermute | solution.py:314
  39.3 12.6 %collective-permute-start.16 = (bf16[128,1792]{1,0:T(8,128)(2,1)S(1)}, bf16[128,1792]{1,0:T(8,128)(2,1)S(1)}, u32[]{:S(2)}, u32[]{:S(2)}) collective-permute-start(bf16[128,1792]{1,0:T(8,128)(2,1)S(1)} %get-tuple-element.32), channel_id=1, source_target_pairs={{0,2},{1,3},{2,0},{3,1},{4,6},{5,7},{6,4},{7,5},{8,10},{9,11},{10,... | collective-permute-start | bytes 1376264 | tf_op jit(solution)/shard_map/ppermute | solution.py:311
  42.0 11.5 %collective-permute-start.12 = (bf16[32,1792]{1,0:T(8,128)(2,1)S(1)}, bf16[32,1792]{1,0:T(8,128)(2,1)S(1)}, u32[]{:S(2)}, u32[]{:S(2)}) collective-permute-start(bf16[32,1792]{1,0:T(8,128)(2,1)S(1)} %get-tuple-element.39), channel_id=1, source_target_pairs={{0,4},{1,5},{2,6},{3,7},{4,0},{5,1},{6,2},{7,3},{8,12},{9,13},{10,... | collective-permute-start | bytes 344072 | tf_op jit(solution)/shard_map/ppermute | solution.py:311
  43.4 12.5 %collective-permute-start.13 = (bf16[32,1792]{1,0:T(8,128)(2,1)S(1)}, bf16[32,1792]{1,0:T(8,128)(2,1)S(1)}, u32[]{:S(2)}, u32[]{:S(2)}) collective-permute-start(bf16[32,1792]{1,0:T(8,128)(2,1)S(1)} %get-tuple-element.41), channel_id=1, source_target_pairs={{0,8},{1,9},{2,10},{3,11},{4,12},{5,13},{6,14},{7,15},{8,0},{9,1},... | collective-permute-start | bytes 344072 | tf_op jit(solution)/shard_map/ppermute | solution.py:311
  45.9 11.3 %collective-permute-start.14 = (bf16[32,1792]{1,0:T(8,128)(2,1)S(1)}, bf16[32,1792]{1,0:T(8,128)(2,1)S(1)}, u32[]{:S(2)}, u32[]{:S(2)}) collective-permute-start(bf16[32,1792]{1,0:T(8,128)(2,1)S(1)} %get-tuple-element.40), channel_id=1, source_target_pairs={{0,12},{1,13},{2,14},{3,15},{4,8},{5,9},{6,10},{7,11},{8,4},{9,5},... | collective-permute-start | bytes 344072 | tf_op jit(solution)/shard_map/ppermute | solution.py:311
  50.7 6.6 %collective-permute-start.9 = (bf16[64,3584]{1,0:T(8,128)(2,1)S(1)}, bf16[64,3584]{1,0:T(8,128)(2,1)S(1)}, u32[]{:S(2)}, u32[]{:S(2)}) collective-permute-start(bf16[64,3584]{1,0:T(8,128)(2,1)S(1)} %collective-permute-done.5.refs_3_.refs_6_), channel_id=1, source_target_pairs={{0,1},{1,0},{2,3},{3,2},{4,5},{5,4},{6,7},{7,6},{8,9},{9,8},{10,11... | collective-permute-start | bytes 1376264 | tf_op jit(solution)/shard_map/ppermute | solution.py:311
  52.0 15.2 %collective-permute-start.17 = (bf16[32,1792]{1,0:T(8,128)(2,1)S(1)}, bf16[32,1792]{1,0:T(8,128)(2,1)S(1)}, u32[]{:S(2)}, u32[]{:S(2)}) collective-permute-start(bf16[32,1792]{1,0:T(8,128)(2,1)S(1)} %get-tuple-element.34), channel_id=1, source_target_pairs={{0,4},{1,5},{2,6},{3,7},{4,0},{5,1},{6,2},{7,3},{8,12},{9,13},{10,... | collective-permute-start | bytes 344072 | tf_op jit(solution)/shard_map/ppermute | solution.py:311
  53.4 13.8 %collective-permute-start.18 = (bf16[32,1792]{1,0:T(8,128)(2,1)S(1)}, bf16[32,1792]{1,0:T(8,128)(2,1)S(1)}, u32[]{:S(2)}, u32[]{:S(2)}) collective-permute-start(bf16[32,1792]{1,0:T(8,128)(2,1)S(1)} %get-tuple-element.35), channel_id=1, source_target_pairs={{0,8},{1,9},{2,10},{3,11},{4,12},{5,13},{6,14},{7,15},{8,0},{9,1},... | collective-permute-start | bytes 344072 | tf_op jit(solution)/shard_map/ppermute | solution.py:311
  55.9 11.3 %collective-permute-start.19 = (bf16[32,1792]{1,0:T(8,128)(2,1)S(1)}, bf16[32,1792]{1,0:T(8,128)(2,1)S(1)}, u32[]{:S(2)}, u32[]{:S(2)}) collective-permute-start(bf16[32,1792]{1,0:T(8,128)(2,1)S(1)} %get-tuple-element.36), channel_id=1, source_target_pairs={{0,12},{1,13},{2,14},{3,15},{4,8},{5,9},{6,10},{7,11},{8,4},{9,5},... | collective-permute-start | bytes 344072 | tf_op jit(solution)/shard_map/ppermute | solution.py:311
  57.2 1.8 %collective-permute-start.10 = (bf16[64,3584]{1,0:T(8,128)(2,1)S(1)}, bf16[64,3584]{1,0:T(8,128)(2,1)S(1)}, u32[]{:S(2)}, u32[]{:S(2)}) collective-permute-start(bf16[64,3584]{1,0:T(8,128)(2,1)S(1)} %collective-permute-done.8.refs_7_.refs_3_), channel_id=1, source_target_pairs={{0,1},{1,0},{2,3},{3,2},{4,5},{5,4},{6,7},{7,6},{8,9},{9,8},{10,11... | collective-permute-start | bytes 1376264 | tf_op jit(solution)/shard_map/ppermute | solution.py:311
  62.4 11.2 %all-to-all-start.1 = ((bf16[16,16,128]{2,1,0:T(8,128)(2,1)}), bf16[16,16,128]{2,1,0:T(8,128)(2,1)S(1)}, u32[]{:S(2)}, u32[]{:S(2)}) async-start(bf16[16,16,128]{2,1,0:T(8,128)(2,1)} %get-tuple-element.28.refs_4_), calls=%async_computation.1 | async-start | bytes 131072 | tf_op jit(solution)/shard_map/all_to_all | solution.py:317
  66.7 1.4 %collective-permute-start.15 = (f32[16,1792]{1,0:T(8,128)S(1)}, f32[16,1792]{1,0:T(8,128)S(1)}, u32[]{:S(2)}, u32[]{:S(2)}) collective-permute-start(f32[16,1792]{1,0:T(8,128)S(1)} %get-tuple-element.42), channel_id=1, source_target_pairs={{0,1},{1,0},{2,3},{3,2},{4,5},{5,4},{6,7},{7,6},{8,9},{9,8},{10,11... | collective-permute-start | bytes 344072 | tf_op jit(solution)/shard_map/ppermute | solution.py:311
  67.2 1.4 %collective-permute-start.20 = (f32[16,1792]{1,0:T(8,128)S(1)}, f32[16,1792]{1,0:T(8,128)S(1)}, u32[]{:S(2)}, u32[]{:S(2)}) collective-permute-start(f32[16,1792]{1,0:T(8,128)S(1)} %get-tuple-element.38), channel_id=1, source_target_pairs={{0,1},{1,0},{2,3},{3,2},{4,5},{5,4},{6,7},{7,6},{8,9},{9,8},{10,11... | collective-permute-start | bytes 344072 | tf_op jit(solution)/shard_map/ppermute | solution.py:311
  (7 other events, 39.5 us)

commit v8 on v7

--- a/solution.py
+++ b/solution.py
@@ -265,7 +265,9 @@
             total = total + coords[base + q].astype(F32)
         pieces.append(total)
     grad_low = jnp.concatenate(pieces, axis=1).astype(BF)
-    out[...] = mm(inverse[...], mm(grad_low, hidden[...]), precision=HIGHEST)
+    high, low = split(mm(inverse[...], grad_low.astype(F32), precision=HIGHEST))
+    both = mm(jnp.concatenate([high, low], axis=0), hidden[...])
+    out[...] = both[0:RANK] + both[RANK:]
 
 def scaled_out_kernel(where, inverse, *refs):
     pieces, (out, rows, sems) = (refs[:-3], refs[-3:])

time: 75.2 us -> 75.2 us (level)
  no operation moved by 1% of the time
where the time goes in v8:
time: 75.2 us; the launch traced here: 74.8 us
  starting transfers between devices  30.9 us (41%)
  waiting for transfers between devices  22.2 us (30%)
  Pallas kernels  17.6 us (23%)
  local copies, waits for them, and re-layouts  2.9 us (4%)
  between operations  0.86 us (1%)
    ppermute x19, starting transfers between devices, swap(): return lax.ppermute(x, 'expert', [(i, i ^ bit) for i in range(experts)])  19.7 us
    pallas_call x13, Pallas kernels, call(): pl.pallas_call(body, out_shape=[jax.ShapeDtypeStruct(o.shape, o.dtype) fo...  17.6 us
    ppermute x19, waiting for transfers between devices, swap(): return lax.ppermute(x, 'expert', [(i, i ^ bit) for i in range(experts)])  11.1 us
    all_to_all x2, waiting for transfers between devices, spread(): return lax.all_to_all(x, 'expert', split_axis=0, concat_axis=0, tiled=True)  9.57 us
    all_to_all x2, starting transfers between devices, spread(): return lax.all_to_all(x, 'expert', split_axis=0, concat_axis=0, tiled=True)  8.14 us
    ppermute x2, starting transfers between devices, swap_side(): return lax.ppermute(x, 'group', [(i, i ^ 1) for i in range(groups)])  3.05 us
    unnamed x16, local copies, waits for them, and re-layouts  1.87 us
    ppermute x2, waiting for transfers between devices, swap_side(): return lax.ppermute(x, 'group', [(i, i ^ 1) for i in range(groups)])  1.52 us
  transfers between devices with their start and end apart: 23, of which 11 were waited for; matrix products, arithmetic and copies ran while one was open for 2% of the time, Pallas kernels for 22%

profile of v8, /device:TPU:0, one launch (start us, length us, event | category | flops | bytes accessed | tf_op | source)
XLA Modules:
  0.0 74.8 jit_solution(8902792659484478479)
XLA Ops:
  2.1 2.6 %collective-permute-start.2 = (bf16[16,3584]{1,0:T(8,128)(2,1)S(1)}, bf16[16,3584]{1,0:T(8,128)(2,1)S(1)}, u32[]{:S(2)}, u32[]{:S(2)}) collective-permute-start(bf16[16,3584]{1,0:T(8,128)(2,1)S(1)} %dynamic-slice_bitcast_fusion.refs_0_), channel_id=1, source_target_pairs={{0,2},{1,3},{2,0},{3,1},{4,6},{5,7},{6,4},{7,5},{8,10},{9,11},{10,... | collective-permute-start | bytes 344072 | tf_op jit(solution)/shard_map/ppermute | solution.py:313
  4.6 3.4 %shard_map.85.refs_2_.refs_0_ = bf16[16,16,128]{2,1,0:T(8,128)(2,1)} custom-call(bf16[512,2048]{1,0:T(8,128)(2,1)} %bitcast.29, bf16[16,2048]{1,0:T(8,128)(2,1)} %bitcast.33, bf16[16,7168]{1,0:T(8,128)(2,1)} %bitcast.31), custom_call_target="tpu_custom_call" | custom-call | bytes 2457600 | tf_op jit(solution)/shard_map/pallas_call | solution.py:33
  9.4 2.7 %collective-permute-start.3 = (bf16[32,3584]{1,0:T(8,128)(2,1)S(1)}, bf16[32,3584]{1,0:T(8,128)(2,1)S(1)}, u32[]{:S(2)}, u32[]{:S(2)}) collective-permute-start(bf16[32,3584]{1,0:T(8,128)(2,1)S(1)} %shard_map.86.refs_1_.refs_0_), channel_id=1, source_target_pairs={{0,8},{1,9},{2,10},{3,11},{4,12},{5,13},{6,14},{7,15},{8,0},{9,1},... | collective-permute-start | bytes 688136 | tf_op jit(solution)/shard_map/ppermute | solution.py:313
  13.7 3.9 %all-to-all-start = ((bf16[16,16,128]{2,1,0:T(8,128)(2,1)}), bf16[16,16,128]{2,1,0:T(8,128)(2,1)S(1)}, u32[]{:S(2)}, u32[]{:S(2)}) async-start(bf16[16,16,128]{2,1,0:T(8,128)(2,1)} %shard_map.87), calls=%async_computation | async-start | bytes 131072 | tf_op jit(solution)/shard_map/all_to_all | solution.py:319
  18.1 6.5 %all-to-all-done.refs_2_.refs_5_ = bf16[16,16,128]{2,1,0:T(8,128)(2,1)S(1)} async-done(((bf16[16,16,128]{2,1,0:T(8,128)(2,1)}), bf16[16,16,128]{2,1,0:T(8,128)(2,1)S(1)}, u32[]{:S(2)}, u32[]{:S(2)}) %all-to-all-start) | async-done | bytes 65568 | tf_op jit(solution)/shard_map/all_to_all | solution.py:319
  25.4 1.5 %collective-permute-start.5 = (bf16[64,3584]{1,0:T(8,128)(2,1)S(1)}, bf16[64,3584]{1,0:T(8,128)(2,1)S(1)}, u32[]{:S(2)}, u32[]{:S(2)}) collective-permute-start(bf16[64,3584]{1,0:T(8,128)(2,1)S(1)} %shard_map.88.refs_6_.refs_3_), channel_id=1, source_target_pairs={{0,16},{16,0},{1,17},{17,1},{2,18},{18,2},{3,19},{19,3},{4,20},{20... | collective-permute-start | bytes 1376264 | tf_op jit(solution)/shard_map/ppermute | solution.py:316
  27.0 2.7 %shard_map.89 = (bf16[128,256]{1,0:T(8,128)(2,1)S(1)}, bf16[512,128]{1,0:T(8,128)(2,1)S(1)}, f32[128,1792]{1,0:T(8,128)S(1)}, f32[128,1792]{1,0:T(8,128)S(1)}, b...) custom-call(s32[3]{0:T(128)S(1)} %pad_add_fusion.refs_0_, bf16[128,7168]{1,0:T(8,128)(2,1)S(1)} %copy-done, ...), custom_call_target="tpu_custom_call" | custom-call | bytes 6692864 | tf_op jit(solution)/shard_map/pallas_call | solution.py:33
  30.7 1.6 %shard_map.90 = (f32[16,16]{1,0:T(8,128)S(1)}, f32[16,16]{1,0:T(8,128)S(1)}) custom-call(bf16[16,2048]{1,0:T(8,128)(2,1)S(1)} %bitcast.34, bf16[16,7168]{1,0:T(8,128)(2,1)S(1)} %bitcast.32, bf16[16,16,128]{2,1,0:T(8,128)(2,1)S(1)} %all-to-all-done.refs_2_.refs_5_), custom_call_target="tpu_custom_call" | custom-call | bytes 362496 | tf_op jit(solution)/shard_map/pallas_call | solution.py:33
  32.3 5.0 %collective-permute-done.4.refs_0_ = bf16[64,3584]{1,0:T(8,128)(2,1)S(1)} collective-permute-done((bf16[64,3584]{1,0:T(8,128)(2,1)S(1)}, bf16[64,3584]{1,0:T(8,128)(2,1)S(1)}, u32[]{:S(2)}, u32[]{:S(2)}) %collective-permute-start.4) | collective-permute-done | bytes 458784 | tf_op jit(solution)/shard_map/ppermute | solution.py:313
  37.7 1.6 %collective-permute-start.8 = (bf16[64,3584]{1,0:T(8,128)(2,1)S(1)}, bf16[64,3584]{1,0:T(8,128)(2,1)S(1)}, u32[]{:S(2)}, u32[]{:S(2)}) collective-permute-start(bf16[64,3584]{1,0:T(8,128)(2,1)S(1)} %shard_map.91.refs_4_), channel_id=1, source_target_pairs={{0,16},{16,0},{1,17},{17,1},{2,18},{18,2},{3,19},{19,3},{4,20},{20... | collective-permute-start | bytes 1376264 | tf_op jit(solution)/shard_map/ppermute | solution.py:316
  40.1 1.7 %collective-permute-done.11 = bf16[128,1792]{1,0:T(8,128)(2,1)S(1)} collective-permute-done((bf16[128,1792]{1,0:T(8,128)(2,1)S(1)}, bf16[128,1792]{1,0:T(8,128)(2,1)S(1)}, u32[]{:S(2)}, u32[]{:S(2)}) %collective-permute-start.11) | collective-permute-done | bytes 458784 | tf_op jit(solution)/shard_map/ppermute | solution.py:313
  42.0 1.4 %collective-permute-start.12 = (bf16[32,1792]{1,0:T(8,128)(2,1)S(1)}, bf16[32,1792]{1,0:T(8,128)(2,1)S(1)}, u32[]{:S(2)}, u32[]{:S(2)}) collective-permute-start(bf16[32,1792]{1,0:T(8,128)(2,1)S(1)} %get-tuple-element.39), channel_id=1, source_target_pairs={{0,4},{1,5},{2,6},{3,7},{4,0},{5,1},{6,2},{7,3},{8,12},{9,13},{10,... | collective-permute-start | bytes 344072 | tf_op jit(solution)/shard_map/ppermute | solution.py:313
  43.4 2.5 %collective-permute-start.13 = (bf16[32,1792]{1,0:T(8,128)(2,1)S(1)}, bf16[32,1792]{1,0:T(8,128)(2,1)S(1)}, u32[]{:S(2)}, u32[]{:S(2)}) collective-permute-start(bf16[32,1792]{1,0:T(8,128)(2,1)S(1)} %get-tuple-element.41), channel_id=1, source_target_pairs={{0,8},{1,9},{2,10},{3,11},{4,12},{5,13},{6,14},{7,15},{8,0},{9,1},... | collective-permute-start | bytes 344072 | tf_op jit(solution)/shard_map/ppermute | solution.py:313
  47.0 2.5 %shard_map.92 = (f32[256,128]{1,0:T(8,128)S(1)}, bf16[128,7168]{1,0:T(8,128)(2,1)}) custom-call(s32[3]{0:T(128)S(1)} %pad_add_fusion.refs_0_, bf16[128,7168]{1,0:T(8,128)(2,1)S(1)} %copy-done, bf16[128,256]{1,0:T(8,128)(2,1)S(1)} %get-tuple-element.21.refs_2_, bf16[64,3584]{1,0:T(8,128)(2,1)S(1)} %shard_map.88.refs_6_.refs_3_, ...), custom_call_target="tpu_custom_call" | custom-call | bytes 5701632 | tf_op jit(solution)/shard_map/pallas_call | solution.py:33
  50.7 1.2 %collective-permute-done.16.refs_1_ = bf16[128,1792]{1,0:T(8,128)(2,1)S(1)} collective-permute-done((bf16[128,1792]{1,0:T(8,128)(2,1)S(1)}, bf16[128,1792]{1,0:T(8,128)(2,1)S(1)}, u32[]{:S(2)}, u32[]{:S(2)}) %collective-permute-start.16) | collective-permute-done | bytes 458784 | tf_op jit(solution)/shard_map/ppermute | solution.py:313
  52.0 1.4 %collective-permute-start.17 = (bf16[32,1792]{1,0:T(8,128)(2,1)S(1)}, bf16[32,1792]{1,0:T(8,128)(2,1)S(1)}, u32[]{:S(2)}, u32[]{:S(2)}) collective-permute-start(bf16[32,1792]{1,0:T(8,128)(2,1)S(1)} %get-tuple-element.34), channel_id=1, source_target_pairs={{0,4},{1,5},{2,6},{3,7},{4,0},{5,1},{6,2},{7,3},{8,12},{9,13},{10,... | collective-permute-start | bytes 344072 | tf_op jit(solution)/shard_map/ppermute | solution.py:313
  53.4 2.5 %collective-permute-start.18 = (bf16[32,1792]{1,0:T(8,128)(2,1)S(1)}, bf16[32,1792]{1,0:T(8,128)(2,1)S(1)}, u32[]{:S(2)}, u32[]{:S(2)}) collective-permute-start(bf16[32,1792]{1,0:T(8,128)(2,1)S(1)} %get-tuple-element.35), channel_id=1, source_target_pairs={{0,8},{1,9},{2,10},{3,11},{4,12},{5,13},{6,14},{7,15},{8,0},{9,1},... | collective-permute-start | bytes 344072 | tf_op jit(solution)/shard_map/ppermute | solution.py:313
  55.9 1.3 %collective-permute-start.19 = (bf16[32,1792]{1,0:T(8,128)(2,1)S(1)}, bf16[32,1792]{1,0:T(8,128)(2,1)S(1)}, u32[]{:S(2)}, u32[]{:S(2)}) collective-permute-start(bf16[32,1792]{1,0:T(8,128)(2,1)S(1)} %get-tuple-element.36), channel_id=1, source_target_pairs={{0,12},{1,13},{2,14},{3,15},{4,8},{5,9},{6,10},{7,11},{8,4},{9,5},... | collective-permute-start | bytes 344072 | tf_op jit(solution)/shard_map/ppermute | solution.py:313
  57.3 1.7 %collective-permute-done.10.refs_9_ = bf16[64,3584]{1,0:T(8,128)(2,1)S(1)} collective-permute-done((bf16[64,3584]{1,0:T(8,128)(2,1)S(1)}, bf16[64,3584]{1,0:T(8,128)(2,1)S(1)}, u32[]{:S(2)}, u32[]{:S(2)}) %collective-permute-start.10) | collective-permute-done | bytes 458784 | tf_op jit(solution)/shard_map/ppermute | solution.py:313
  59.0 3.4 %shard_map.93 = (bf16[16,16,128]{2,1,0:T(8,128)(2,1)}, bf16[128,7168]{1,0:T(8,128)(2,1)}) custom-call(s32[3]{0:T(128)S(1)} %pad_add_fusion.refs_0_, bf16[128,7168]{1,0:T(8,128)(2,1)S(1)} %copy-done, bf16[128,256]{1,0:T(8,128)(2,1)S(1)} %get-tuple-element.21.refs_2_, bf16[512,128]{1,0:T(8,128)(2,1)S(1)} %get-tuple-element.22.refs_3_, ...), custom_call_target="tpu_custom_call", output_to_operand_aliasing={{1}: (5, {})} | custom-call | bytes 7733248 | tf_op jit(solution)/shard_map/pallas_call | solution.py:33
  62.4 4.3 %all-to-all-start.1 = ((bf16[16,16,128]{2,1,0:T(8,128)(2,1)}), bf16[16,16,128]{2,1,0:T(8,128)(2,1)S(1)}, u32[]{:S(2)}, u32[]{:S(2)}) async-start(bf16[16,16,128]{2,1,0:T(8,128)(2,1)} %get-tuple-element.28.refs_4_), calls=%async_computation.1 | async-start | bytes 131072 | tf_op jit(solution)/shard_map/all_to_all | solution.py:319
  68.6 1.9 %shard_map.97 = f32[16,7168]{1,0:T(8,128)} custom-call(s32[3]{0:T(128)S(1)} %pad_add_fusion.refs_0_, f32[16,16]{1,0:T(8,128)S(1)} %get-tuple-element.24.refs_2_.refs_1_, f32[16,1792]{1,0:T(8,128)S(1)} %get-tuple-element.43.refs_2_, f32[16,1792]{1,0:T(8,128)S(1)} %collective-permute-done.15.refs_3_, f32[16,1792]{1,0:T(8,128)S(1)} %get-tuple-element.37.refs_4_, ...), custom_call_target="tpu_custom_call" | custom-call | bytes 918528 | tf_op jit(solution)/shard_map/pallas_call | solution.py:33
  70.5 3.1 %all-to-all-done.1.refs_0_ = bf16[16,16,128]{2,1,0:T(8,128)(2,1)S(1)} async-done(((bf16[16,16,128]{2,1,0:T(8,128)(2,1)}), bf16[16,16,128]{2,1,0:T(8,128)(2,1)S(1)}, u32[]{:S(2)}, u32[]{:S(2)}) %all-to-all-start.1) | async-done | bytes 65568 | tf_op jit(solution)/shard_map/all_to_all | solution.py:319
  73.6 1.2 %shard_map.94 = f32[16,2048]{1,0:T(8,128)} custom-call(bf16[16,16,128]{2,1,0:T(8,128)(2,1)S(1)} %all-to-all-done.1.refs_0_, bf16[512,2048]{1,0:T(8,128)(2,1)S(1)} %bitcast.30, f32[16,16]{1,0:T(8,128)S(1)} %get-tuple-element.29.refs_2_), custom_call_target="tpu_custom_call" | custom-call | bytes 2294784 | tf_op jit(solution)/shard_map/pallas_call | solution.py:33
  (63 shorter events, 12.4 us)
Async XLA Ops:
  0.7 26.3 %collective-permute-start = (bf16[128,7168]{1,0:T(8,128)(2,1)}, bf16[128,7168]{1,0:T(8,128)(2,1)}, u32[]{:S(2)}, u32[]{:S(2)}) collective-permute-start(bf16[128,7168]{1,0:T(8,128)(2,1)} %refs_1_.5), channel_id=1, source_target_pairs={{0,1},{1,0},{2,3},{3,2},{4,5},{5,4},{6,7},{7,6},{8,9},{9,8},{10,11... | collective-permute-start | bytes 5505032 | tf_op jit(solution)/shard_map/ppermute | solution.py:313
  2.1 6.3 %collective-permute-start.2 = (bf16[16,3584]{1,0:T(8,128)(2,1)S(1)}, bf16[16,3584]{1,0:T(8,128)(2,1)S(1)}, u32[]{:S(2)}, u32[]{:S(2)}) collective-permute-start(bf16[16,3584]{1,0:T(8,128)(2,1)S(1)} %dynamic-slice_bitcast_fusion.refs_0_), channel_id=1, source_target_pairs={{0,2},{1,3},{2,0},{3,1},{4,6},{5,7},{6,4},{7,5},{8,10},{9,11},{10,... | collective-permute-start | bytes 344072 | tf_op jit(solution)/shard_map/ppermute | solution.py:313
  8.1 18.9 %copy-start = (bf16[128,7168]{1,0:T(8,128)(2,1)S(1)}, bf16[128,7168]{1,0:T(8,128)(2,1)}, u32[]{:S(2)}) copy-start(bf16[128,7168]{1,0:T(8,128)(2,1)} %refs_1_.5) | copy-start | bytes 5505028
  9.4 15.2 %collective-permute-start.3 = (bf16[32,3584]{1,0:T(8,128)(2,1)S(1)}, bf16[32,3584]{1,0:T(8,128)(2,1)S(1)}, u32[]{:S(2)}, u32[]{:S(2)}) collective-permute-start(bf16[32,3584]{1,0:T(8,128)(2,1)S(1)} %shard_map.86.refs_1_.refs_0_), channel_id=1, source_target_pairs={{0,8},{1,9},{2,10},{3,11},{4,12},{5,13},{6,14},{7,15},{8,0},{9,1},... | collective-permute-start | bytes 688136 | tf_op jit(solution)/shard_map/ppermute | solution.py:313
  13.7 10.9 %all-to-all-start = ((bf16[16,16,128]{2,1,0:T(8,128)(2,1)}), bf16[16,16,128]{2,1,0:T(8,128)(2,1)S(1)}, u32[]{:S(2)}, u32[]{:S(2)}) async-start(bf16[16,16,128]{2,1,0:T(8,128)(2,1)} %shard_map.87), calls=%async_computation | async-start | bytes 131072 | tf_op jit(solution)/shard_map/all_to_all | solution.py:319
  17.7 9.2 %collective-permute-start.1 = (bf16[16,128]{1,0:T(8,128)(2,1)S(1)}, bf16[16,128]{1,0:T(8,128)(2,1)S(1)}, u32[]{:S(2)}, u32[]{:S(2)}) collective-permute-start(bf16[16,128]{1,0:T(8,128)(2,1)S(1)} %maximum_maximum_fusion.refs_3_), channel_id=1, source_target_pairs={{0,1},{1,0},{2,3},{3,2},{4,5},{5,4},{6,7},{7,6},{8,9},{9,8},{10,11... | collective-permute-start | bytes 12296 | tf_op jit(solution)/shard_map/ppermute | solution.py:313
  24.7 12.6 %collective-permute-start.4 = (bf16[64,3584]{1,0:T(8,128)(2,1)S(1)}, bf16[64,3584]{1,0:T(8,128)(2,1)S(1)}, u32[]{:S(2)}, u32[]{:S(2)}) collective-permute-start(bf16[64,3584]{1,0:T(8,128)(2,1)S(1)} %shard_map.88.refs_6_.refs_3_), channel_id=1, source_target_pairs={{0,4},{1,5},{2,6},{3,7},{4,0},{5,1},{6,2},{7,3},{8,12},{9,13},{10,... | collective-permute-start | bytes 1376264 | tf_op jit(solution)/shard_map/ppermute | solution.py:313
  25.4 12.3 %collective-permute-start.5 = (bf16[64,3584]{1,0:T(8,128)(2,1)S(1)}, bf16[64,3584]{1,0:T(8,128)(2,1)S(1)}, u32[]{:S(2)}, u32[]{:S(2)}) collective-permute-start(bf16[64,3584]{1,0:T(8,128)(2,1)S(1)} %shard_map.88.refs_6_.refs_3_), channel_id=1, source_target_pairs={{0,16},{16,0},{1,17},{17,1},{2,18},{18,2},{3,19},{19,3},{4,20},{20... | collective-permute-start | bytes 1376264 | tf_op jit(solution)/shard_map/ppermute | solution.py:316
  29.7 12.0 %collective-permute-start.11 = (bf16[128,1792]{1,0:T(8,128)(2,1)S(1)}, bf16[128,1792]{1,0:T(8,128)(2,1)S(1)}, u32[]{:S(2)}, u32[]{:S(2)}) collective-permute-start(bf16[128,1792]{1,0:T(8,128)(2,1)S(1)} %get-tuple-element.23.refs_1_), channel_id=1, source_target_pairs={{0,2},{1,3},{2,0},{3,1},{4,6},{5,7},{6,4},{7,5},{8,10},{9,11},{10,... | collective-permute-start | bytes 1376264 | tf_op jit(solution)/shard_map/ppermute | solution.py:313
  32.2 11.2 %collective-permute-start.6 = (bf16[64,3584]{1,0:T(8,128)(2,1)S(1)}, bf16[64,3584]{1,0:T(8,128)(2,1)S(1)}, u32[]{:S(2)}, u32[]{:S(2)}) collective-permute-start(bf16[64,3584]{1,0:T(8,128)(2,1)S(1)} %shard_map.88.refs_6_.refs_3_), channel_id=1, source_target_pairs={{0,1},{1,0},{2,3},{3,2},{4,5},{5,4},{6,7},{7,6},{8,9},{9,8},{10,11... | collective-permute-start | bytes 1376264 | tf_op jit(solution)/shard_map/ppermute | solution.py:313
  37.7 8.2 %collective-permute-start.7 = (bf16[64,3584]{1,0:T(8,128)(2,1)S(1)}, bf16[64,3584]{1,0:T(8,128)(2,1)S(1)}, u32[]{:S(2)}, u32[]{:S(2)}) collective-permute-start(bf16[64,3584]{1,0:T(8,128)(2,1)S(1)} %shard_map.91.refs_4_), channel_id=1, source_target_pairs={{0,1},{1,0},{2,3},{3,2},{4,5},{5,4},{6,7},{7,6},{8,9},{9,8},{10,11... | collective-permute-start | bytes 1376264 | tf_op jit(solution)/shard_map/ppermute | solution.py:313
  37.7 12.9 %collective-permute-start.8 = (bf16[64,3584]{1,0:T(8,128)(2,1)S(1)}, bf16[64,3584]{1,0:T(8,128)(2,1)S(1)}, u32[]{:S(2)}, u32[]{:S(2)}) collective-permute-start(bf16[64,3584]{1,0:T(8,128)(2,1)S(1)} %shard_map.91.refs_4_), channel_id=1, source_target_pairs={{0,16},{16,0},{1,17},{17,1},{2,18},{18,2},{3,19},{19,3},{4,20},{20... | collective-permute-start | bytes 1376264 | tf_op jit(solution)/shard_map/ppermute | solution.py:316
  39.3 12.6 %collective-permute-start.16 = (bf16[128,1792]{1,0:T(8,128)(2,1)S(1)}, bf16[128,1792]{1,0:T(8,128)(2,1)S(1)}, u32[]{:S(2)}, u32[]{:S(2)}) collective-permute-start(bf16[128,1792]{1,0:T(8,128)(2,1)S(1)} %get-tuple-element.32), channel_id=1, source_target_pairs={{0,2},{1,3},{2,0},{3,1},{4,6},{5,7},{6,4},{7,5},{8,10},{9,11},{10,... | collective-permute-start | bytes 1376264 | tf_op jit(solution)/shard_map/ppermute | solution.py:313
  42.0 11.5 %collective-permute-start.12 = (bf16[32,1792]{1,0:T(8,128)(2,1)S(1)}, bf16[32,1792]{1,0:T(8,128)(2,1)S(1)}, u32[]{:S(2)}, u32[]{:S(2)}) collective-permute-start(bf16[32,1792]{1,0:T(8,128)(2,1)S(1)} %get-tuple-element.39), channel_id=1, source_target_pairs={{0,4},{1,5},{2,6},{3,7},{4,0},{5,1},{6,2},{7,3},{8,12},{9,13},{10,... | collective-permute-start | bytes 344072 | tf_op jit(solution)/shard_map/ppermute | solution.py:313
  43.4 12.5 %collective-permute-start.13 = (bf16[32,1792]{1,0:T(8,128)(2,1)S(1)}, bf16[32,1792]{1,0:T(8,128)(2,1)S(1)}, u32[]{:S(2)}, u32[]{:S(2)}) collective-permute-start(bf16[32,1792]{1,0:T(8,128)(2,1)S(1)} %get-tuple-element.41), channel_id=1, source_target_pairs={{0,8},{1,9},{2,10},{3,11},{4,12},{5,13},{6,14},{7,15},{8,0},{9,1},... | collective-permute-start | bytes 344072 | tf_op jit(solution)/shard_map/ppermute | solution.py:313
  45.9 11.3 %collective-permute-start.14 = (bf16[32,1792]{1,0:T(8,128)(2,1)S(1)}, bf16[32,1792]{1,0:T(8,128)(2,1)S(1)}, u32[]{:S(2)}, u32[]{:S(2)}) collective-permute-start(bf16[32,1792]{1,0:T(8,128)(2,1)S(1)} %get-tuple-element.40), channel_id=1, source_target_pairs={{0,12},{1,13},{2,14},{3,15},{4,8},{5,9},{6,10},{7,11},{8,4},{9,5},... | collective-permute-start | bytes 344072 | tf_op jit(solution)/shard_map/ppermute | solution.py:313
  50.7 6.6 %collective-permute-start.9 = (bf16[64,3584]{1,0:T(8,128)(2,1)S(1)}, bf16[64,3584]{1,0:T(8,128)(2,1)S(1)}, u32[]{:S(2)}, u32[]{:S(2)}) collective-permute-start(bf16[64,3584]{1,0:T(8,128)(2,1)S(1)} %collective-permute-done.5.refs_3_.refs_6_), channel_id=1, source_target_pairs={{0,1},{1,0},{2,3},{3,2},{4,5},{5,4},{6,7},{7,6},{8,9},{9,8},{10,11... | collective-permute-start | bytes 1376264 | tf_op jit(solution)/shard_map/ppermute | solution.py:313
  52.0 15.2 %collective-permute-start.17 = (bf16[32,1792]{1,0:T(8,128)(2,1)S(1)}, bf16[32,1792]{1,0:T(8,128)(2,1)S(1)}, u32[]{:S(2)}, u32[]{:S(2)}) collective-permute-start(bf16[32,1792]{1,0:T(8,128)(2,1)S(1)} %get-tuple-element.34), channel_id=1, source_target_pairs={{0,4},{1,5},{2,6},{3,7},{4,0},{5,1},{6,2},{7,3},{8,12},{9,13},{10,... | collective-permute-start | bytes 344072 | tf_op jit(solution)/shard_map/ppermute | solution.py:313
  53.4 13.8 %collective-permute-start.18 = (bf16[32,1792]{1,0:T(8,128)(2,1)S(1)}, bf16[32,1792]{1,0:T(8,128)(2,1)S(1)}, u32[]{:S(2)}, u32[]{:S(2)}) collective-permute-start(bf16[32,1792]{1,0:T(8,128)(2,1)S(1)} %get-tuple-element.35), channel_id=1, source_target_pairs={{0,8},{1,9},{2,10},{3,11},{4,12},{5,13},{6,14},{7,15},{8,0},{9,1},... | collective-permute-start | bytes 344072 | tf_op jit(solution)/shard_map/ppermute | solution.py:313
  55.9 11.3 %collective-permute-start.19 = (bf16[32,1792]{1,0:T(8,128)(2,1)S(1)}, bf16[32,1792]{1,0:T(8,128)(2,1)S(1)}, u32[]{:S(2)}, u32[]{:S(2)}) collective-permute-start(bf16[32,1792]{1,0:T(8,128)(2,1)S(1)} %get-tuple-element.36), channel_id=1, source_target_pairs={{0,12},{1,13},{2,14},{3,15},{4,8},{5,9},{6,10},{7,11},{8,4},{9,5},... | collective-permute-start | bytes 344072 | tf_op jit(solution)/shard_map/ppermute | solution.py:313
  57.2 1.8 %collective-permute-start.10 = (bf16[64,3584]{1,0:T(8,128)(2,1)S(1)}, bf16[64,3584]{1,0:T(8,128)(2,1)S(1)}, u32[]{:S(2)}, u32[]{:S(2)}) collective-permute-start(bf16[64,3584]{1,0:T(8,128)(2,1)S(1)} %collective-permute-done.8.refs_7_.refs_3_), channel_id=1, source_target_pairs={{0,1},{1,0},{2,3},{3,2},{4,5},{5,4},{6,7},{7,6},{8,9},{9,8},{10,11... | collective-permute-start | bytes 1376264 | tf_op jit(solution)/shard_map/ppermute | solution.py:313
  62.4 11.2 %all-to-all-start.1 = ((bf16[16,16,128]{2,1,0:T(8,128)(2,1)}), bf16[16,16,128]{2,1,0:T(8,128)(2,1)S(1)}, u32[]{:S(2)}, u32[]{:S(2)}) async-start(bf16[16,16,128]{2,1,0:T(8,128)(2,1)} %get-tuple-element.28.refs_4_), calls=%async_computation.1 | async-start | bytes 131072 | tf_op jit(solution)/shard_map/all_to_all | solution.py:319
  66.7 1.4 %collective-permute-start.15 = (f32[16,1792]{1,0:T(8,128)S(1)}, f32[16,1792]{1,0:T(8,128)S(1)}, u32[]{:S(2)}, u32[]{:S(2)}) collective-permute-start(f32[16,1792]{1,0:T(8,128)S(1)} %get-tuple-element.42), channel_id=1, source_target_pairs={{0,1},{1,0},{2,3},{3,2},{4,5},{5,4},{6,7},{7,6},{8,9},{9,8},{10,11... | collective-permute-start | bytes 344072 | tf_op jit(solution)/shard_map/ppermute | solution.py:313
  67.2 1.4 %collective-permute-start.20 = (f32[16,1792]{1,0:T(8,128)S(1)}, f32[16,1792]{1,0:T(8,128)S(1)}, u32[]{:S(2)}, u32[]{:S(2)}) collective-permute-start(f32[16,1792]{1,0:T(8,128)S(1)} %get-tuple-element.38), channel_id=1, source_target_pairs={{0,1},{1,0},{2,3},{3,2},{4,5},{5,4},{6,7},{7,6},{8,9},{9,8},{10,11... | collective-permute-start | bytes 344072 | tf_op jit(solution)/shard_map/ppermute | solution.py:313
  (7 other events, 39.5 us)
